TPU v7x, 256 devices: a whole 4x4x8 slice. The times are simulated.
256 devices in a mesh: inst: 32 (over x, z_lo, core), tp: 8 (over z_hi, y).
Axes of the slice: x: 4, y: 4, z: 8 (z_hi: 2, z_lo: 4; z = z_hi * 4 + z_lo), core: 2. Of those that a mesh axis runs over, the one named last changes fastest.
Arguments:
- queries: bfloat16 [2048, 2, 8192], P('inst', None, 'tp'), may hold values from -6 to 6
- new_kv: bfloat16 [2048, 2, 2048], P('inst', None, 'tp'), may hold values from -6 to 6
- kv_cache: bfloat16 [16384, 16, 2048], P('inst', None, 'tp'), may hold values from -6 to 6
- block_table: int32 [2048, 8], P('inst'), may hold values from 0 to 511, as said below
- lengths: int32 [2048], P('inst'), may hold values from 1 to 128, as said below
- mig_rows: int32 [768], P('inst'), may hold values from 0 to 63, as said below
- mig_target: int32 [768], P('inst'), may hold values from 0 to 31, as said below
- dirty_hidden: bfloat16 [768, 16, 8192], P('inst', None, 'tp'), may hold values from -60 to 60
- norm_gain: bfloat16 [8192], replicated, may hold values from 0.25 to 1.75
- kv_weight: bfloat16 [8192, 2048], P(None, 'tp'), may hold values from -0.0625 to 0.0625
Outputs:
- decoded: bfloat16 [2048, 2, 8192], P('inst', None, 'tp')
- mig_kv: bfloat16 [8192, 16, 2048], P('inst', None, 'tp')
Inputs may be any that keep to these rules, and one draw needn't show every extreme that they name: `lengths`: every instance has a request of exactly 128 tokens. `block_table`: the rows of one instance use distinct pages of its own pool. `mig_rows`: the 24 rows of one instance are distinct. `mig_target`: a target differs from its source; slots 2c and 2c + 1 of an instance share a target and the pairs of one instance go to distinct targets, so at most 2 requests of one instance go to one target, and their pages together are at most 8; some instance receives exactly 8 pages from every other instance.
All inputs are finite; a program needn't handle non-finite values.
Results may differ from a plain program's by a relative error of at most 0.0049.
Values may be sent and summed in bfloat16 or wider, within the bound.
No kernel may reach another device: no remote copies, remote signals or barrier semaphores. Data moves between devices by JAX's collectives and lax.ppermute only.
A program may use at most 128 MiB of HBM per device.

v0:
```python
import math

import jax
import jax.numpy as jnp
from jax import lax
from jax.sharding import PartitionSpec as P

HD = 128
PAGE = 16
MAXP = 8
MIG = 24
CAP = 2


def rotate_keys(key_part, positions):
    half_dim = key_part.shape[-1] // 2
    frequency = jnp.exp(
        jnp.arange(half_dim, dtype=jnp.float32) * (-2.0 * math.log(500000.0) / key_part.shape[-1])
    )
    angles = positions.astype(jnp.float32)[..., None, None] * frequency
    cosine = jnp.cos(angles)
    sine_part = jnp.sin(angles)
    first_half = key_part[..., :half_dim]
    second = key_part[..., half_dim:]
    return jnp.concatenate(
        [first_half * cosine - second * sine_part, second * cosine + first_half * sine_part],
        axis=-1,
    )


def refill(hidden, gain_vec, weight, first_pos, valid_count):
    item_count = hidden.shape[0]
    page_len = hidden.shape[1]
    head_count = weight.shape[1] // (2 * HD)
    states = hidden.astype(jnp.float32)
    mean_square = jnp.mean(states * states, axis=-1, keepdims=True)
    normed = (states * lax.rsqrt(mean_square + 1e-05) * gain_vec.astype(jnp.float32)).astype(
        jnp.bfloat16
    )
    projected = jnp.dot(
        normed.reshape(item_count * page_len, -1), weight, preferred_element_type=jnp.float32
    )
    projected = projected.reshape(item_count, page_len, head_count, 2, HD)
    offsets = jnp.arange(page_len, dtype=jnp.int32)
    positions = first_pos[:, None] + offsets[None, :]
    rotated = rotate_keys(projected[:, :, :, 0, :], positions)
    merged = jnp.stack([rotated, projected[:, :, :, 1, :]], axis=3).reshape(
        item_count, page_len, head_count * 2 * HD
    )
    keep_mask = offsets[None, :] < valid_count[:, None]
    return jnp.where(keep_mask[:, :, None], merged, 0.0).astype(jnp.bfloat16)


def attend(queries, new_kv, gathered, row_lengths):
    row_count = queries.shape[0]
    head_count = gathered.shape[-1] // (2 * HD)
    group_size = queries.shape[-1] // (HD * head_count)
    span_len = gathered.shape[1]
    stored_tokens = gathered.reshape(row_count, span_len, head_count, 2, HD)
    query_heads = queries.reshape(row_count, 2, head_count, group_size, HD)
    fresh_tokens = new_kv.reshape(row_count, 2, head_count, 2, HD)
    score_scale = 1.0 / math.sqrt(HD)
    cached_scores = (
        jnp.einsum(
            "rsghd,rtgd->rsght",
            query_heads,
            stored_tokens[:, :, :, 0],
            preferred_element_type=jnp.float32,
        )
        * score_scale
    )
    own_scores = (
        jnp.einsum(
            "rsghd,rugd->rsghu",
            query_heads,
            fresh_tokens[:, :, :, 0],
            preferred_element_type=jnp.float32,
        )
        * score_scale
    )
    live_tokens = jnp.arange(span_len, dtype=jnp.int32)[None, :] < row_lengths[:, None]
    cached_scores = jnp.where(live_tokens[:, None, None, None, :], cached_scores, -jnp.inf)
    step_index = jnp.arange(2, dtype=jnp.int32)
    visible = step_index[None, :] <= step_index[:, None]
    own_scores = jnp.where(visible[None, :, None, None, :], own_scores, -jnp.inf)
    scores = jnp.concatenate([cached_scores, own_scores], axis=-1)
    row_max = jnp.max(scores, axis=-1, keepdims=True)
    raised = jnp.exp(scores - row_max)
    weights = (raised / jnp.sum(raised, axis=-1, keepdims=True)).astype(jnp.bfloat16)
    mixture = jnp.einsum(
        "rsght,rtgd->rsghd",
        weights[..., :span_len],
        stored_tokens[:, :, :, 1],
        preferred_element_type=jnp.float32,
    )
    mixture = mixture + jnp.einsum(
        "rsghu,rugd->rsghd",
        weights[..., span_len:],
        fresh_tokens[:, :, :, 1],
        preferred_element_type=jnp.float32,
    )
    return mixture.reshape(row_count, 2, head_count * group_size * HD).astype(jnp.bfloat16)


def per_device(
    queries,
    new_kv,
    kv_cache,
    block_table,
    lengths,
    mig_rows,
    mig_target,
    dirty_hidden,
    norm_gain,
    kv_weight,
):
    row_count = queries.shape[0]
    lane_width = kv_cache.shape[-1]
    gathered = kv_cache[block_table].reshape(row_count, MAXP * PAGE, lane_width)
    decoded = attend(queries, new_kv, gathered, lengths)
    gathered_rows = lax.all_gather(dirty_hidden, "tp", axis=2, tiled=True)
    picked = mig_rows[:, None] == jnp.arange(row_count, dtype=jnp.int32)[None, :]
    mig_len = jnp.sum(jnp.where(picked, lengths[None, :], 0), axis=1)
    held_pages = jnp.sum(jnp.where(picked[:, :, None], block_table[None], 0), axis=1)
    mig_pages = (mig_len + PAGE - 1) // PAGE
    fresh_pages = refill(
        gathered_rows,
        norm_gain,
        kv_weight,
        (mig_pages - 1) * PAGE,
        mig_len - (mig_pages - 1) * PAGE,
    )
    page_slot = jnp.arange(MAXP, dtype=jnp.int32)[None, :]
    is_last = page_slot == (mig_pages - 1)[:, None]
    in_use = page_slot < mig_pages[:, None]
    outgoing_pages = jnp.where(
        is_last[:, :, None, None], fresh_pages[:, None], kv_cache[held_pages]
    )
    outgoing_pages = jnp.where(
        in_use[:, :, None, None], outgoing_pages, jnp.zeros((), jnp.bfloat16)
    )
    slot_order = jnp.arange(MIG, dtype=jnp.int32)
    earlier = slot_order[None, :] < slot_order[:, None]
    same_goal = mig_target[:, None] == mig_target[None, :]
    members = lax.axis_size("inst")
    rank_slot = jnp.sum((same_goal & earlier).astype(jnp.int32), axis=1)
    target_place = mig_target * CAP + rank_slot
    outgoing = (
        jnp.zeros((members * CAP, MAXP, PAGE, lane_width), jnp.bfloat16)
        .at[target_place]
        .set(outgoing_pages)
    )
    counts = jnp.zeros((members * CAP,), jnp.int32).at[target_place].set(mig_pages)
    arrived, arrived_counts = (
        lax.all_to_all(
            outgoing.reshape(members, CAP, MAXP, PAGE, lane_width),
            "inst",
            split_axis=0,
            concat_axis=0,
            tiled=True,
        ),
        lax.all_to_all(
            counts.reshape(members, CAP), "inst", split_axis=0, concat_axis=0, tiled=True
        ),
    )
    front_count = arrived_counts[:, 0:1]
    shifted = jnp.clip(page_slot - front_count, 0, MAXP - 1)
    later_part = jnp.take_along_axis(arrived[:, 1], shifted[:, :, None, None], axis=1)
    mig_kv = jnp.where((page_slot < front_count)[:, :, None, None], arrived[:, 0], later_part)
    return (decoded, mig_kv.reshape(members * MAXP, PAGE, lane_width))


def solution(mesh):
    return jax.shard_map(
        per_device,
        mesh=mesh,
        in_specs=(
            P("inst", None, "tp"),
            P("inst", None, "tp"),
            P("inst", None, "tp"),
            P("inst", None),
            P("inst"),
            P("inst"),
            P("inst"),
            P("inst", None, "tp"),
            P(),
            P(None, "tp"),
        ),
        out_specs=(P("inst", None, "tp"), P("inst", None, "tp")),
        check_vma=False,
    )
```

profile of v0, /device:TPU:1, one launch (start us, length us, event | category | flops | bytes accessed | tf_op | source)
XLA Modules:
  0.0 292.0 jit_solution(11378138204289254486)
XLA Ops:
  7.2 0.7 all-gather.2.cloned.1.call-update
  7.9 0.9 convert_reduce_fusion
  8.8 0.9 select_reduce_fusion.1
  9.7 0.7 compare_select_fusion.4
  10.3 0.6 scatter_custom_fusion
  11.0 0.7 all_to_all.11
  11.7 10.0 %all-to-all-start = ((s32[32,1,2]{2,1,0:T(1,128)}), s32[32,1,2]{2,1,0:T(1,128)S(1)}, u32[]{:S(2)}, u32[]{:S(2)}) async-start(s32[32,1,2]{2,1,0:T(1,128)} %bitcast.21), calls=%async_computation | async-start | bytes 32768 | tf_op jit(solution)/shard_map/all_to_all | solution.py:162
  21.8 6.4 %copy.71 = bf16[256,8192]{1,0:T(8,128)(2,1)} copy(bf16[256,8192]{0,1:T(8,128)(2,1)} %bitcast.120) | data formatting | bytes 8388608 | tf_op jit(solution)/shard_map/reshape.192
  28.3 0.5 select_reduce_fusion
  28.9 3.1 %gather_fusion.1 = bf16[192,16,256]{2,1,0:T(8,128)(2,1)S(1)} fusion(bf16[512,16,256]{2,1,0:T(8,128)(2,1)} %param.12, s32[1024]{0:T(1024)S(1)} %pad_clamp_fusion), kind=kCustom, calls=%fused_computation.1 | custom fusion | bytes 3146496 | tf_op jit(solution)/shard_map/gather | solution.py:137
  32.2 121.6 %all-gather.2.cloned.1.call-done = bf16[24,16,8192]{2,1,0:T(8,128)(2,1)} async-done(((bf16[24,16,1024]{2,1,0:T(8,128)(2,1)}), bf16[24,16,8192]{2,1,0:T(8,128)(2,1)}) %all-gather.2.cloned.1.call-update) | async-done | bytes 6291472 | tf_op jit(solution)/shard_map/all_gather | solution.py:121
  153.8 4.2 %fusion = f32[24,16]{1,0:T(8,128)S(1)} fusion(bf16[24,16,8192]{2,1,0:T(8,128)(2,1)} %all-gather.2.cloned.1.call-done), kind=kLoop, calls=%fused_computation.7 | loop fusion | flops 9436800 | bytes 6292992 | tf_op jit(solution)/shard_map/reduce_sum | solution.py:36
  158.0 0.4 copy-done
  158.4 5.7 %fusion.13 = f32[24,16,1,2,128]{4,1,3,0,2:T(8,128)S(1)} fusion(bf16[2,128,8192,1]{2,1,0,3:T(8,128)(2,1)} %bitcast.121, bf16[24,16,8192]{2,1,0:T(8,128)(2,1)S(1)} %copy-done, f32[8192]{0:T(1024)S(1)} %convert_element_type.56, f32[24,16]{1,0:T(8,128)S(1)} %add_rsqrt_fusion), kind=kOutput, calls=%fused_computation.26 | convolution fusion | flops 1623195648 | bytes 10913280 | tf_op jit(solution)/shard_map/dot_general | solution.py:40
  164.2 0.8 fusion.26
  165.6 0.6 select_select_fusion
  166.2 2.5 broadcast_in_dim.170
  168.6 5.3 %scatter_fusion = bf16[64,8,16,256]{3,2,1,0:T(8,128)(2,1)} fusion(bf16[64,8,16,256]{3,2,1,0:T(8,128)(2,1)} %broadcast_in_dim.170, s32[24]{0:T(128)S(1)} %compare_select_fusion.4, bf16[24,8,16,256]{3,2,1,0:T(8,128)(2,1)S(1)} %select_select_fusion), kind=kCustom, calls=%fused_computation.4 | custom fusion | bytes 4718688 | tf_op jit(solution)/shard_map/scatter | solution.py:151
  174.0 5.7 %all-to-all-start.1 = ((bf16[32,2,8,16,256]{4,3,2,1,0:T(8,128)(2,1)}), bf16[32,2,8,16,256]{4,3,2,1,0:T(8,128)(2,1)}, u32[]{:S(2)}, u32[]{:S(2)}) async-start(bf16[32,2,8,16,256]{4,3,2,1,0:T(8,128)(2,1)} %bitcast.118), calls=%async_computation.1 | async-start | bytes 8388608 | tf_op jit(solution)/shard_map/all_to_all | solution.py:155
  179.9 5.1 %gather_fusion = bf16[512,16,256]{2,1,0:T(8,128)(2,1)} fusion(bf16[512,16,256]{2,1,0:T(8,128)(2,1)} %param.12, s32[1024]{0:T(1024)S(1)} %pad_clamp_fusion.1), kind=kCustom, calls=%fused_computation | custom fusion | bytes 8390656 | tf_op jit(solution)/shard_map/gather | solution.py:119
  185.0 7.0 %reshape_reshape.3 = bf16[64,128,1,2,128]{4,3,1,0,2:T(2,128)(2,1)} reshape(bf16[512,16,256]{2,1,0:T(8,128)(2,1)} %gather_fusion) | data formatting | bytes 8388608 | tf_op jit(solution)/shard_map/reshape;reshape | solution.py:59
  192.4 0.4 fusion.38
  192.8 10.3 %fusion.35 = (bf16[64,128,1,1,128]{4,3,1,0,2:T(2,128)(2,1)S(1)}, bf16[64,128,1,1,128]{4,3,1,0,2:T(2,128)(2,1)S(1)}) fusion(bf16[64,128,1,2,128]{4,3,1,0,2:T(2,128)(2,1)} %reshape_reshape.3), kind=kLoop, calls=%fused_computation.88 | loop fusion | bytes 8388608 | tf_op jit(solution)/shard_map/slice | solution.py:67
  203.1 1.3 fusion.37
  204.5 0.4 fusion.21
  204.9 0.3 divide_convert_fusion
  205.3 0.7 fusion.7
  206.2 0.8 convert_element_type.53
  207.6 66.6 %all-to-all-done.1 = bf16[32,2,8,16,256]{4,3,2,1,0:T(8,128)(2,1)} async-done(((bf16[32,2,8,16,256]{4,3,2,1,0:T(8,128)(2,1)}), bf16[32,2,8,16,256]{4,3,2,1,0:T(8,128)(2,1)}, u32[]{:S(2)}, u32[]{:S(2)}) %all-to-all-start.1) | async-done | bytes 4194336 | tf_op jit(solution)/shard_map/all_to_all | solution.py:155
  274.2 4.7 %slice_bitcast_fusion = (bf16[32,8,16,256]{3,2,1,0:T(8,128)(2,1)}, bf16[32,1,8,16,256]{4,3,2,1,0:T(8,128)(2,1)}) fusion(bf16[32,2,8,16,256]{4,3,2,1,0:T(8,128)(2,1)} %all-to-all-done.1), kind=kLoop, calls=%fused_computation.12 | loop fusion | bytes 8388608 | tf_op jit(solution)/shard_map/squeeze | solution.py:168
  278.9 2.7 gather_fusion.2
  281.7 3.5 %bitcast_select_fusion = bf16[256,16,256]{2,1,0:T(8,128)(2,1)} fusion(bf16[32,1,8,16,256]{4,3,2,1,0:T(8,128)(2,1)} %get-tuple-element.5, bf16[256,16,256]{2,1,0:T(8,128)(2,1)S(1)} %gather_fusion.2, pred[256]{0:T(512)(128)(4,1)S(1)} %compare_and_fusion, pred[256]{0:T(512)(128)(4,1)S(1)} %lt.156), kind=kLoop, calls=%fused_computation.17 | loop fusion | flops 2097152 | bytes 6291968 | tf_op jit(solution)/shard_map/jit(_where)/select_n | solution.py:169
  (54 shorter events, 2.5 us)
Async XLA Ops:
  7.2 146.6 %all-gather.2.cloned.1.call-start = ((), (), s32[]{:S(2)}) async-start(), calls=%async_computation.2 | async-start | bytes 7077888 | tf_op jit(solution)/shard_map/all_gather | solution.py:121
  11.7 162.3 %all-to-all-start = ((s32[32,1,2]{2,1,0:T(1,128)}), s32[32,1,2]{2,1,0:T(1,128)S(1)}, u32[]{:S(2)}, u32[]{:S(2)}) async-start(s32[32,1,2]{2,1,0:T(1,128)} %bitcast.21), calls=%async_computation | async-start | bytes 32768 | tf_op jit(solution)/shard_map/all_to_all | solution.py:162
  21.7 6.5 %copy-start.3 = (bf16[8192]{0:T(1024)(128)(2,1)S(1)}, bf16[8192]{0:T(1024)(128)(2,1)}, u32[]{:S(2)}) copy-start(bf16[8192]{0:T(1024)(128)(2,1)} %param.18) | copy-start | bytes 49156
  21.8 6.4 %copy-start.5 = (s32[24]{0:T(128)S(1)}, s32[24]{0:T(128)}, u32[]{:S(2)}) copy-start(s32[24]{0:T(128)} %param.15) | copy-start | bytes 292
  21.8 6.5 %copy-start.4 = (s32[64,8]{0,1:T(8,128)S(1)}, s32[64,8]{0,1:T(8,128)}, u32[]{:S(2)}) copy-start(s32[64,8]{0,1:T(8,128)} %param.13) | copy-start | bytes 6148
  153.8 4.6 %copy-start = (bf16[24,16,8192]{2,1,0:T(8,128)(2,1)S(1)}, bf16[24,16,8192]{2,1,0:T(8,128)(2,1)}, u32[]{:S(2)}) copy-start(bf16[24,16,8192]{2,1,0:T(8,128)(2,1)} %all-gather.2.cloned.1.call-done) | copy-start | bytes 18874372
  174.0 100.2 %all-to-all-start.1 = ((bf16[32,2,8,16,256]{4,3,2,1,0:T(8,128)(2,1)}), bf16[32,2,8,16,256]{4,3,2,1,0:T(8,128)(2,1)}, u32[]{:S(2)}, u32[]{:S(2)}) async-start(bf16[32,2,8,16,256]{4,3,2,1,0:T(8,128)(2,1)} %bitcast.118), calls=%async_computation.1 | async-start | bytes 8388608 | tf_op jit(solution)/shard_map/all_to_all | solution.py:155
  185.0 7.0 %copy-start.1 = (bf16[64,2,1024]{2,1,0:T(2,128)(2,1)S(1)}, bf16[64,2,1024]{2,1,0:T(2,128)(2,1)}, u32[]{:S(2)}) copy-start(bf16[64,2,1024]{2,1,0:T(2,128)(2,1)} %param.10) | copy-start | bytes 786436
  185.0 7.2 %copy-start.2 = (bf16[64,2,256]{2,1,0:T(2,128)(2,1)S(1)}, bf16[64,2,256]{2,1,0:T(2,128)(2,1)}, u32[]{:S(2)}) copy-start(bf16[64,2,256]{2,1,0:T(2,128)(2,1)} %param.11) | copy-start | bytes 196612
  185.0 7.2 %copy-start.6 = (s32[64]{0:T(128)S(1)}, s32[64]{0:T(128)}, u32[]{:S(2)}) copy-start(s32[64]{0:T(128)} %param.14) | copy-start | bytes 772
Sparse Core Ops, SparseCore 0:
  10.6 143.1 all-gather.1
where the time goes:
time: 293 us; the launch traced here: 292 us
  waiting for transfers between devices  189 us (65%)
  local copies, waits for them, and re-layouts  50.9 us (17%)
  starting transfers between devices  15.7 us (5%)
  between operations  14.3 us (5%)
  other arithmetic  13.8 us (5%)
  matrix products  8.32 us (3%)
    all_gather x1, waiting for transfers between devices, per_device(): gathered_rows = lax.all_gather(dirty_hidden, 'tp', axis=2, tiled=True)  122 us
    all_to_all x1, waiting for transfers between devices, per_device(): lax.all_to_all(outgoing.reshape(members, CAP, MAXP, PAGE, lane_width), 'i...  66.6 us
    slice x1, local copies, waits for them, and re-layouts, attend(): stored_tokens[:, :, :, 0]  10.3 us
    all_to_all x1, starting transfers between devices, per_device(): lax.all_to_all(counts.reshape(members, CAP), 'inst', split_axis=0, concat...  10 us
    another operation x1, local copies, waits for them, and re-layouts, attend(): stored_tokens = gathered.reshape(row_count, span_len, head_count, 2, HD)  6.98 us
    another operation x2, local copies, waits for them, and re-layouts  6.58 us
  transfers between devices with their start and end apart: 3, of which 2 were waited for; matrix products, arithmetic and copies ran while one was open for 21% of the time, Pallas kernels for 0%

commit v1 on v0

v1 whole, which is shorter than its diff:
```python
import functools
import math

import jax
import jax.numpy as jnp
from jax import lax
from jax.experimental import pallas as pl
from jax.experimental.pallas import tpu as pltpu
from jax.sharding import PartitionSpec as P

HD = 128
PAGE = 16
MAXP = 8
MIG = 24
PAIRS = MIG // 2
STORED = MAXP - 2
NX, NZL, NCORE, NZH, NY = 4, 4, 2, 2, 4
TP = NZH * NY
AXES = ("inst", "tp")
VMEM_LIMIT = 40 * 1024 * 1024
F32 = jnp.float32
BF16 = jnp.bfloat16


def index_of(x, zl, core, zh, y):
    return (((x * NZL + zl) * NCORE) + core) * TP + zh * NY + y


def moves(dx=0, dcore=0, dzh=0, dy=0):
    pairs = []
    for x in range(NX):
        for zl in range(NZL):
            for core in range(NCORE):
                for zh in range(NZH):
                    for y in range(NY):
                        pairs.append(
                            (
                                index_of(x, zl, core, zh, y),
                                index_of(
                                    (x + dx) % NX,
                                    zl,
                                    (core + dcore) % NCORE,
                                    (zh + dzh) % NZH,
                                    (y + dy) % NY,
                                ),
                            )
                        )
    return pairs


def send(value, **by):
    return lax.ppermute(value, AXES, moves(**by))


def params(**more):
    return pltpu.CompilerParams(vmem_limit_bytes=VMEM_LIMIT, **more)


SMEM = pl.BlockSpec(memory_space=pltpu.SMEM)
VMEM = pl.BlockSpec(memory_space=pltpu.VMEM)
ANY = pl.BlockSpec(memory_space=pl.ANY)


def pack_kernel(rows_ref, target_ref, len_ref, table_ref, cache_ref, out_ref, sems):
    def copy_of(c, m):
        first = rows_ref[2 * c]
        second = rows_ref[2 * c + 1]
        front = (len_ref[first] + PAGE - 1) // PAGE - 1
        in_front = m < front
        row = jnp.where(in_front, first, second)
        slot = jnp.where(in_front, m, jnp.minimum(m - front, MAXP - 1))
        page = table_ref[row, slot]
        return pltpu.make_async_copy(
            cache_ref.at[page], out_ref.at[target_ref[2 * c] * STORED + m], sems.at[c * STORED + m]
        )

    for c in range(PAIRS):
        for m in range(STORED):
            copy_of(c, m).start()
    for c in range(PAIRS):
        for m in range(STORED):
            copy_of(c, m).wait()


def pack(rows, target, lengths, table, cache, members):
    lanes = cache.shape[-1]
    return pl.pallas_call(
        pack_kernel,
        out_shape=jax.ShapeDtypeStruct((members * STORED, PAGE, lanes), cache.dtype),
        in_specs=[SMEM, SMEM, SMEM, SMEM, ANY],
        out_specs=ANY,
        scratch_shapes=[pltpu.SemaphoreType.DMA((PAIRS * STORED,))],
        compiler_params=params(),
        cost_estimate=pl.CostEstimate(flops=0, bytes_accessed=8 * 1024 * 1024, transcendentals=0),
        name="pack",
    )(rows, target, lengths, table, cache)


def attend_kernel(table_ref, len_ref, q_ref, new_ref, cache_ref, out_ref):
    row_count, heads, _ = q_ref.shape
    span = MAXP * PAGE + PAGE
    scale = 1.0 / math.sqrt(HD)
    column = lax.broadcasted_iota(jnp.int32, (heads, span), 1)
    step = lax.broadcasted_iota(jnp.int32, (heads, span), 0) // (heads // 2)
    own = (column >= MAXP * PAGE) & (column - MAXP * PAGE <= step)

    def one(r):
        parts = [cache_ref[table_ref[r, b]] for b in range(MAXP)] + [new_ref[r]]
        tokens = jnp.concatenate(parts, axis=0)
        scores = lax.dot_general(
            q_ref[r], tokens[:, :HD], (((1,), (1,)), ((), ())), preferred_element_type=F32
        )
        seen = (column < len_ref[r]) | own
        scores = jnp.where(seen, scores * scale, -jnp.inf)
        raised = jnp.exp(scores - jnp.max(scores, axis=-1, keepdims=True))
        weights = (raised / jnp.sum(raised, axis=-1, keepdims=True)).astype(BF16)
        out_ref[r] = jnp.dot(weights, tokens[:, HD:], preferred_element_type=F32).astype(BF16)

    unroll = 4

    def body(i, carry):
        for u in range(unroll):
            one(i * unroll + u)
        return carry

    lax.fori_loop(0, row_count // unroll, body, 0)


def attend(queries, new_kv, cache, table, lengths):
    row_count = queries.shape[0]
    heads = queries.shape[-1] // HD
    q = queries.reshape(row_count, 2 * heads, HD)
    fresh = jnp.pad(new_kv, ((0, 0), (0, PAGE - 2), (0, 0)))
    out = pl.pallas_call(
        attend_kernel,
        out_shape=jax.ShapeDtypeStruct((row_count, 2 * heads, HD), BF16),
        in_specs=[SMEM, SMEM, VMEM, VMEM, VMEM],
        out_specs=VMEM,
        compiler_params=params(),
        cost_estimate=pl.CostEstimate(
            flops=64 * 16 * 144 * 128 * 4, bytes_accessed=32 * 1024 * 1024, transcendentals=0
        ),
        name="attend",
    )(table, lengths, q, fresh, cache)
    return out.reshape(row_count, 2, heads * HD)


def project_kernel(count, has_acc, place_ref, gain_ref, own_ref, mine_ref, other_ref, *refs):
    blocks = refs[:count]
    refs = refs[count:]
    if has_acc:
        acc_own_ref, acc_oth_ref = refs[:2]
        refs = refs[2:]
    out_own_ref, out_oth_ref, x_ref = refs
    core = place_ref[0]
    depth = blocks[0].shape[1]
    half = depth // 2
    for i, block in enumerate(blocks):
        feature = place_ref[1 + 3 * i]
        near = place_ref[2 + 3 * i]
        gain = gain_ref[pl.ds(feature, 1), :]
        x_ref[...] = (block[...].astype(F32) * gain).astype(BF16)
        part_own = jnp.dot(
            x_ref[...],
            own_ref[pl.ds(pl.multiple_of(feature * depth, depth), depth), :],
            preferred_element_type=F32,
        )
        rows = pl.ds(pl.multiple_of(near * half, half), half)
        part_oth = jnp.dot(
            x_ref[:, pl.ds(pl.multiple_of(core * half, half), half)],
            mine_ref[rows, :],
            preferred_element_type=F32,
        ) + jnp.dot(
            x_ref[:, pl.ds(pl.multiple_of((1 - core) * half, half), half)],
            other_ref[rows, :],
            preferred_element_type=F32,
        )
        if i == 0:
            if has_acc:
                part_own = part_own + acc_own_ref[...]
                part_oth = part_oth + acc_oth_ref[...]
            sum_own, sum_oth = part_own, part_oth
        else:
            sum_own, sum_oth = sum_own + part_own, sum_oth + part_oth
    out_own_ref[...] = sum_own
    out_oth_ref[...] = sum_oth.astype(out_oth_ref.dtype)


def project(place, gain, own, mine, other, blocks, acc, oth_dtype):
    tokens, depth = blocks[0].shape
    width = own.shape[1]
    shape = (tokens, width)
    args = list(blocks) + (list(acc) if acc else [])
    return pl.pallas_call(
        functools.partial(project_kernel, len(blocks), bool(acc)),
        out_shape=(jax.ShapeDtypeStruct(shape, F32), jax.ShapeDtypeStruct(shape, oth_dtype)),
        in_specs=[SMEM] + [VMEM] * (4 + len(args)),
        out_specs=(VMEM, VMEM),
        scratch_shapes=[pltpu.VMEM((tokens, depth), BF16)],
        compiler_params=params(),
        cost_estimate=pl.CostEstimate(
            flops=len(blocks) * tokens * depth * width * 4,
            bytes_accessed=8 * 1024 * 1024,
            transcendentals=0,
        ),
        name="project",
    )(place, gain, own, mine, other, *args)


def combine_kernel(target_ref, own_ref, got_ref, cos_ref, sin_ref, inv_ref, out_ref):
    total = own_ref[...] + got_ref[...].astype(F32)
    keys = total[:, :HD]
    turned = keys * cos_ref[...] + pltpu.roll(keys, HD // 2, 1) * sin_ref[...]
    page_rows = jnp.concatenate([turned, total[:, HD:] * inv_ref[...]], axis=1).astype(BF16)
    for k in range(MIG):
        out_ref[target_ref[k] * 2 + k % 2] = page_rows[k * PAGE : (k + 1) * PAGE]


def combine(target, own, got, cos_t, sin_t, inv_t, members):
    return pl.pallas_call(
        combine_kernel,
        out_shape=jax.ShapeDtypeStruct((members * 2, PAGE, own.shape[1]), BF16),
        in_specs=[SMEM] + [VMEM] * 5,
        out_specs=VMEM,
        compiler_params=params(),
        name="combine",
    )(target, own, got, cos_t, sin_t, inv_t)


def assemble_kernel(sources, counts_ref, stored_ref, dirty_ref, out_ref):
    base = pl.program_id(0) * sources

    def one(s, carry):
        first = counts_ref[base + s, 0]
        second = counts_ref[base + s, 1]
        for m in range(MAXP):
            behind = (m >= first).astype(jnp.int32)
            index = jnp.clip(m - behind, 0, STORED - 1)
            kept = stored_ref[s * STORED + index]
            made = dirty_ref[s * 2 + behind]
            is_made = (m == first - 1) | (m == first + second - 1)
            page = jnp.where(is_made, made, kept)
            out_ref[s * MAXP + m] = jnp.where(m < first + second, page, jnp.zeros_like(page))
        return carry

    lax.fori_loop(0, sources, one, 0)


def assemble(counts, stored, dirty, members):
    lanes = stored.shape[-1]
    steps = 4
    sources = members // steps
    return pl.pallas_call(
        functools.partial(assemble_kernel, sources),
        out_shape=jax.ShapeDtypeStruct((members * MAXP, PAGE, lanes), stored.dtype),
        grid=(steps,),
        in_specs=[
            SMEM,
            pl.BlockSpec((sources * STORED, PAGE, lanes), lambda i: (i, 0, 0)),
            pl.BlockSpec((sources * 2, PAGE, lanes), lambda i: (i, 0, 0)),
        ],
        out_specs=pl.BlockSpec((sources * MAXP, PAGE, lanes), lambda i: (i, 0, 0)),
        compiler_params=params(),
        name="assemble",
    )(counts, stored, dirty)


def exchange(pages, members, each):
    lanes = pages.shape[-1]
    moved = lax.all_to_all(
        pages.reshape(members, each * PAGE, lanes), "inst", split_axis=0, concat_axis=0, tiled=True
    )
    return moved.reshape(members * each, PAGE, lanes)


def per_device(
    queries,
    new_kv,
    kv_cache,
    block_table,
    lengths,
    mig_rows,
    mig_target,
    dirty_hidden,
    norm_gain,
    kv_weight,
):
    members = lax.axis_size("inst")
    inst = lax.axis_index("inst")
    tp = lax.axis_index("tp")
    x_at, core = inst // (NZL * NCORE), inst % NCORE
    zh, y_at = tp // NY, tp % NY
    tokens = MIG * PAGE
    depth = dirty_hidden.shape[-1]
    features = depth * TP
    half_features = depth * NY

    hidden = dirty_hidden.reshape(tokens, depth)
    from_below = send(hidden, dy=1)
    from_above = send(hidden, dy=-1)
    from_across = send(hidden, dy=2)

    slice_rows = half_features // (NX * NCORE)
    begin = (1 - zh) * half_features + (x_at * NCORE + core) * slice_rows
    outgoing_slice = lax.dynamic_slice_in_dim(kv_weight, begin, slice_rows, axis=0)
    slice_here = send(outgoing_slice, dzh=1)
    slices = jnp.concatenate(
        [slice_here] + [send(slice_here, dx=-d) for d in range(1, NX)], axis=0
    )
    other_slices = send(slices, dcore=1)

    row_count = queries.shape[0]
    picked = mig_rows[:, None] == jnp.arange(row_count, dtype=jnp.int32)[None, :]
    mig_len = jnp.sum(jnp.where(picked, lengths[None, :], 0), axis=1)
    mig_pages = (mig_len + PAGE - 1) // PAGE
    notes = lax.all_gather(jnp.stack([mig_target, mig_pages]), "inst", axis=0)
    aimed_here = notes[:, 0] == inst
    counts = jnp.sum(
        jnp.where(aimed_here, notes[:, 1], 0).reshape(members, PAIRS, 2), axis=1
    )

    stored = exchange(
        pack(mig_rows, mig_target, lengths, block_table, kv_cache, members), members, STORED
    )

    squares = jnp.sum(jnp.square(hidden.astype(F32)), axis=1)
    squares = lax.psum(squares, "tp")
    inv = lax.rsqrt(squares / features + 1e-05)
    offsets = jnp.arange(PAGE, dtype=jnp.int32)
    positions = ((mig_pages - 1) * PAGE)[:, None] + offsets[None, :]
    keep = (positions < mig_len[:, None]).reshape(tokens)
    inv = jnp.where(keep, inv, 0.0)[:, None]
    half_dim = HD // 2
    frequency = jnp.exp(
        jnp.arange(half_dim, dtype=F32) * (-2.0 * math.log(500000.0) / HD)
    )
    angles = positions.reshape(tokens).astype(F32)[:, None] * frequency[None, :]
    cosine = jnp.cos(angles) * inv
    sine = jnp.sin(angles) * inv
    cos_t = jnp.concatenate([cosine, cosine], axis=1)
    sin_t = jnp.concatenate([-sine, sine], axis=1)
    inv_t = jnp.broadcast_to(inv, (tokens, HD))

    decoded = attend(queries, new_kv, kv_cache, block_table, lengths)

    gain = norm_gain.astype(F32).reshape(TP, depth)

    def place_of(shifts):
        entries = [core]
        for dy in shifts:
            block = (y_at + dy) % NY
            entries += [zh * NY + block, (block - x_at) % NX, block]
        return jnp.stack(entries).astype(jnp.int32)

    acc = project(
        place_of((0, -1, 1)),
        gain,
        kv_weight,
        slices,
        other_slices,
        (hidden, from_below, from_above),
        None,
        F32,
    )
    own, outgoing = project(
        place_of((2,)), gain, kv_weight, slices, other_slices, (from_across,), acc, BF16
    )
    got = send(outgoing, dzh=1)
    dirty = exchange(
        combine(mig_target, own, got, cos_t, sin_t, inv_t, members), members, 2
    )
    return decoded, assemble(counts, stored, dirty, members)


def solution(mesh):
    return jax.shard_map(
        per_device,
        mesh=mesh,
        in_specs=(
            P("inst", None, "tp"),
            P("inst", None, "tp"),
            P("inst", None, "tp"),
            P("inst", None),
            P("inst"),
            P("inst"),
            P("inst"),
            P("inst", None, "tp"),
            P(),
            P(None, "tp"),
        ),
        out_specs=(P("inst", None, "tp"), P("inst", None, "tp")),
        check_vma=False,
    )
```

time: 293 us -> 217 us (0.74)
  waiting for transfers between devices: 189 us -> 31.5 us
  blocking collectives: 0 us -> 96.1 us
  local copies, waits for them, and re-layouts: 50.9 us -> 10.2 us
  Pallas kernels: 0 us -> 37 us
  starting transfers between devices: 15.7 us -> 38.6 us
  between operations: 14.3 us -> 1.09 us
  other arithmetic: 13.8 us -> 2.36 us
  matrix products: 8.32 us -> 0 us
    all_gather x1 -> x0, waiting for transfers between devices: 122 us -> none  [per_device(): gathered_rows = lax.all_gather(dirty_hidden, 'tp', axis=2, tiled=True)]
    all_gather x0 -> x1, blocking collectives: none -> 67.6 us  [per_device(): notes = lax.all_gather(jnp.stack([mig_target, mig_pages]), 'inst', axis=0)]
    all_to_all x2, waiting for transfers between devices: 66.6 us -> 11.4 us  [exchange(): lax.all_to_all(pages.reshape(members, each * PAGE, lanes), 'inst', split_...]
    pallas_call x0 -> x6, Pallas kernels: none -> 37 us  [the longest x1 23.6 us: attend(): pl.pallas_call(attend_kernel, out_shape=jax.ShapeDtypeStruct((row_count,...]
    psum x0 -> x1, blocking collectives: none -> 28.5 us  [per_device(): squares = lax.psum(squares, 'tp')]
    ppermute x0 -> x9, waiting for transfers between devices: none -> 20.1 us  [send(): return lax.ppermute(value, AXES, moves(**by))]
    ppermute x0 -> x9, starting transfers between devices: none -> 18.9 us  [send(): return lax.ppermute(value, AXES, moves(**by))]
    another operation x4 -> x1, local copies, waits for them, and re-layouts: 13.7 us -> 0.09 us  [place_of(): return jnp.stack(entries).astype(jnp.int32)]
  transfers between devices with their start and end apart: 3 -> 11, of which waited for: 2 -> 5; matrix products, arithmetic and copies ran while one was open for 21% -> 2% of each run, Pallas kernels for 0% -> 14%
where the time goes in v1:
time: 217 us
  blocking collectives  96.1 us (44%)
  starting transfers between devices  38.6 us (18%)
  Pallas kernels  37 us (17%)
  waiting for transfers between devices  31.5 us (15%)
  local copies, waits for them, and re-layouts  10.2 us (5%)
  other arithmetic  2.36 us (1%)
    all_gather x1, blocking collectives, per_device(): notes = lax.all_gather(jnp.stack([mig_target, mig_pages]), 'inst', axis=0)  67.6 us
    psum x1, blocking collectives, per_device(): squares = lax.psum(squares, 'tp')  28.5 us
    pallas_call x1, Pallas kernels, attend(): pl.pallas_call(attend_kernel, out_shape=jax.ShapeDtypeStruct((row_count,...  23.6 us
    ppermute x9, waiting for transfers between devices, send(): return lax.ppermute(value, AXES, moves(**by))  20.1 us
    all_to_all x2, starting transfers between devices, exchange(): lax.all_to_all(pages.reshape(members, each * PAGE, lanes), 'inst', split_...  19.8 us
    ppermute x9, starting transfers between devices, send(): return lax.ppermute(value, AXES, moves(**by))  18.9 us
    all_to_all x2, waiting for transfers between devices, exchange(): lax.all_to_all(pages.reshape(members, each * PAGE, lanes), 'inst', split_...  11.4 us
    unnamed x24, local copies, waits for them, and re-layouts  6.73 us
  transfers between devices with their start and end apart: 11, of which 5 were waited for; matrix products, arithmetic and copies ran while one was open for 2% of the time, Pallas kernels for 14%

profile of v1, /device:TPU:1, one launch (start us, length us, event | category | flops | bytes accessed | tf_op | source)
XLA Modules:
  0.0 216.9 jit_solution(4512673247500662254)
XLA Ops:
  0.7 1.0 constant_dynamic-slice_fusion
  1.7 7.8 %collective-permute-start = (bf16[512,256]{1,0:T(8,128)(2,1)S(1)}, bf16[512,256]{1,0:T(8,128)(2,1)S(1)}, u32[]{:S(2)}, u32[]{:S(2)}) collective-permute-start(bf16[512,256]{1,0:T(8,128)(2,1)S(1)} %constant_dynamic-slice_fusion), channel_id=1, source_target_pairs={{0,4},{1,5},{2,6},{3,7},{4,0},{5,1},{6,2},{7,3},{8,12},{9,13},{10,... | collective-permute-start | bytes 786440 | tf_op jit(solution)/shard_map/ppermute | solution.py:52
  9.5 1.3 collective-permute-start.6
  10.8 1.4 collective-permute-start.7
  12.3 0.9 select_reduce_fusion
  13.1 1.9 collective-permute-done
  15.1 4.0 %collective-permute-start.1 = (bf16[512,256]{1,0:T(8,128)(2,1)S(1)}, bf16[512,256]{1,0:T(8,128)(2,1)S(1)}, u32[]{:S(2)}, u32[]{:S(2)}) collective-permute-start(bf16[512,256]{1,0:T(8,128)(2,1)S(1)} %collective-permute-done), channel_id=1, source_target_pairs={{0,192},{1,193},{2,194},{3,195},{4,196},{5,197},{6,198},{7,199},{8... | collective-permute-start | bytes 786440 | tf_op jit(solution)/shard_map/ppermute | solution.py:52
  19.0 0.5 collective-permute-start.2
  19.7 0.7 reshape.151.gain_ref
  20.5 0.7 collective-permute-start.3
  21.2 3.4 %collective-permute-done.1 = bf16[512,256]{1,0:T(8,128)(2,1)S(1)} collective-permute-done((bf16[512,256]{1,0:T(8,128)(2,1)S(1)}, bf16[512,256]{1,0:T(8,128)(2,1)S(1)}, u32[]{:S(2)}, u32[]{:S(2)}) %collective-permute-start.1) | collective-permute-done | bytes 262176 | tf_op jit(solution)/shard_map/ppermute | solution.py:52
  24.6 2.4 %collective-permute-start.5 = (bf16[384,1024]{1,0:T(8,128)(2,1)}, bf16[384,1024]{1,0:T(8,128)(2,1)}, u32[]{:S(2)}, u32[]{:S(2)}) collective-permute-start(bf16[384,1024]{1,0:T(8,128)(2,1)} %bitcast.33), channel_id=1, source_target_pairs={{0,2},{1,3},{2,0},{3,1},{4,6},{5,7},{6,4},{7,5},{8,10},{9,11},{10,... | collective-permute-start | bytes 2359304 | tf_op jit(solution)/shard_map/ppermute | solution.py:52
  27.0 7.4 %collective-permute-done.3 = bf16[512,256]{1,0:T(8,128)(2,1)S(1)} collective-permute-done((bf16[512,256]{1,0:T(8,128)(2,1)S(1)}, bf16[512,256]{1,0:T(8,128)(2,1)S(1)}, u32[]{:S(2)}, u32[]{:S(2)}) %collective-permute-start.3) | collective-permute-done | bytes 262176 | tf_op jit(solution)/shard_map/ppermute | solution.py:52
  34.4 0.6 collective-permute-start.4
  35.2 0.2 multiply_reduce_fusion
  35.7 28.5 %psum.7 = f32[384]{0:T(512)S(1)} all-reduce(f32[384]{0:T(512)S(1)} %reduce_sum.32), channel_id=1, replica_groups=mesh['inst'=32,'tp'=8] {'tp'}, use_global_device_ids=true, to_apply=%region_3.4 | all-reduce | flops 384 | bytes 3072 | tf_op jit(solution)/shard_map/psum | solution.py:327
  64.3 2.2 %copy-done = bf16[8192,256]{1,0:T(8,128)(2,1)S(1)} copy-done((bf16[8192,256]{1,0:T(8,128)(2,1)S(1)}, bf16[8192,256]{1,0:T(8,128)(2,1)}, u32[]{:S(2)}) %copy-start) | copy-done | bytes 4194328
  66.5 3.3 %project.2 = (f32[384,256]{1,0:T(8,128)S(1)}, f32[384,256]{1,0:T(8,128)S(1)}) custom-call(s32[10]{0:T(128)S(1)} %stack.69.place_ref, f32[8,1024]{1,0:T(8,128)S(1)} %reshape.151.gain_ref, bf16[8192,256]{1,0:T(8,128)(2,1)S(1)} %copy-done, bf16[2048,256]{1,0:T(8,128)(2,1)S(1)} %constant_dynamic-update-slice_fusion.mine_ref, ...), custom_call_target="tpu_custom_call" | custom-call | flops 1207959552 | bytes 8388608 | tf_op jit(solution)/shard_map/project/pallas_call | solution.py:194
  69.9 2.0 project.3
  72.0 0.8 fusion.2
  73.0 7.4 %collective-permute-done.8.got_ref = bf16[384,256]{1,0:T(8,128)(2,1)S(1)} collective-permute-done((bf16[384,256]{1,0:T(8,128)(2,1)S(1)}, bf16[384,256]{1,0:T(8,128)(2,1)S(1)}, u32[]{:S(2)}, u32[]{:S(2)}) %collective-permute-start.8) | collective-permute-done | bytes 196640 | tf_op jit(solution)/shard_map/ppermute | solution.py:52
  80.5 1.5 combine.1
  82.0 16.0 %all-to-all-start.1 = ((bf16[32,32,256]{2,1,0:T(8,128)(2,1)}), bf16[32,32,256]{2,1,0:T(8,128)(2,1)S(1)}, u32[]{:S(2)}, u32[]{:S(2)}) async-start(bf16[32,32,256]{2,1,0:T(8,128)(2,1)} %bitcast.20), calls=%async_computation.1 | async-start | bytes 1048576 | tf_op jit(solution)/shard_map/all_to_all | solution.py:270
  98.1 2.2 %copy-done.1 = bf16[512,16,256]{2,1,0:T(8,128)(2,1)S(1)} copy-done((bf16[512,16,256]{2,1,0:T(8,128)(2,1)S(1)}, bf16[512,16,256]{2,1,0:T(8,128)(2,1)}, u32[]{:S(2)}) %copy-start.1) | copy-done | bytes 4194328
  100.3 3.1 %pack.1 = bf16[192,16,256]{2,1,0:T(8,128)(2,1)} custom-call(s32[24]{0:T(128)S(1)} %copy-done.6, s32[24]{0:T(128)S(1)} %copy-done.4, s32[64]{0:T(128)S(1)} %copy-done.5, s32[64,8]{1,0:T(8,128)S(1)} %copy.21.table_ref, bf16[512,16,256]{2,1,0:T(8,128)(2,1)S(1)} %copy-done.1), custom_call_target="tpu_custom_call" | custom-call | bytes 8388608 | tf_op jit(solution)/shard_map/pack/pallas_call | solution.py:87
  103.4 11.4 %all-to-all-done.1 = bf16[32,32,256]{2,1,0:T(8,128)(2,1)S(1)} async-done(((bf16[32,32,256]{2,1,0:T(8,128)(2,1)}), bf16[32,32,256]{2,1,0:T(8,128)(2,1)S(1)}, u32[]{:S(2)}, u32[]{:S(2)}) %all-to-all-start.1) | async-done | bytes 524320 | tf_op jit(solution)/shard_map/all_to_all | solution.py:270
  114.8 3.8 %all-to-all-start = ((bf16[32,96,256]{2,1,0:T(8,128)(2,1)}), bf16[32,96,256]{2,1,0:T(8,128)(2,1)S(1)}, u32[]{:S(2)}, u32[]{:S(2)}) async-start(bf16[32,96,256]{2,1,0:T(8,128)(2,1)} %bitcast.4), calls=%async_computation | async-start | bytes 3145728 | tf_op jit(solution)/shard_map/all_to_all | solution.py:270
  118.6 67.6 %all-gather.1 = s32[32,2,24]{2,1,0:T(2,128)S(1)} all-gather(s32[1,2,24]{2,1,0:T(2,128)S(1)} %add_bitcast_fusion), channel_id=2, replica_groups=mesh['inst'=32,'tp'=8] {'inst'}, dimensions={0}, use_global_device_ids=true | all-gather | bytes 6336 | tf_op jit(solution)/shard_map/all_gather | solution.py:316
  186.7 2.2 %copy-done.2 = bf16[512,16,256]{2,1,0:T(8,128)(2,1)S(1)} copy-done((bf16[512,16,256]{2,1,0:T(8,128)(2,1)S(1)}, bf16[512,16,256]{2,1,0:T(8,128)(2,1)}, u32[]{:S(2)}) %copy-start.2) | copy-done | bytes 4194328
  188.9 23.6 %attend.1 = bf16[64,16,128]{2,1,0:T(8,128)(2,1)S(1)} custom-call(s32[64,8]{1,0:T(8,128)S(1)} %copy.21.table_ref, s32[64]{0:T(128)S(1)} %copy-done.5, bf16[64,16,128]{2,1,0:T(8,128)(2,1)S(1)} %reshape.141.q_ref, bf16[64,16,256]{2,1,0:T(8,128)(2,1)S(1)} %pad.4.new_ref, bf16[512,16,256]{2,1,0:T(8,128)(2,1)S(1)} %copy-done.2), custom_call_target="tpu_custom_call" | custom-call | flops 75497472 | bytes 33554432 | tf_op jit(solution)/shard_map/attend/pallas_call | solution.py:134
  212.5 0.8 reshape.142
  213.4 3.5 %assemble.1 = bf16[256,16,256]{2,1,0:T(8,128)(2,1)} custom-call(s32[32,2]{1,0:T(8,128)S(1)} %copy.24.counts_ref, bf16[192,16,256]{2,1,0:T(8,128)(2,1)S(1)} %bitcast.30, bf16[64,16,256]{2,1,0:T(8,128)(2,1)S(1)} %bitcast.35), custom_call_target="tpu_custom_call" | custom-call | tf_op jit(solution)/shard_map/assemble/pallas_call | solution.py:253
  (49 shorter events, 1.7 us)
Async XLA Ops:
  0.6 34.5 %copy-start.3 = (bf16[24,16,1024]{2,1,0:T(8,128)(2,1)S(1)}, bf16[24,16,1024]{2,1,0:T(8,128)(2,1)}, u32[]{:S(2)}) copy-start(bf16[24,16,1024]{2,1,0:T(8,128)(2,1)} %param.17) | copy-start | bytes 2359300
  1.7 13.3 %collective-permute-start = (bf16[512,256]{1,0:T(8,128)(2,1)S(1)}, bf16[512,256]{1,0:T(8,128)(2,1)S(1)}, u32[]{:S(2)}, u32[]{:S(2)}) collective-permute-start(bf16[512,256]{1,0:T(8,128)(2,1)S(1)} %constant_dynamic-slice_fusion), channel_id=1, source_target_pairs={{0,4},{1,5},{2,6},{3,7},{4,0},{5,1},{6,2},{7,3},{8,12},{9,13},{10,... | collective-permute-start | bytes 786440 | tf_op jit(solution)/shard_map/ppermute | solution.py:52
  9.5 54.7 %collective-permute-start.6 = (bf16[384,1024]{1,0:T(8,128)(2,1)}, bf16[384,1024]{1,0:T(8,128)(2,1)}, u32[]{:S(2)}, u32[]{:S(2)}) collective-permute-start(bf16[384,1024]{1,0:T(8,128)(2,1)} %bitcast.31), channel_id=1, source_target_pairs={{0,1},{1,2},{2,3},{3,0},{4,5},{5,6},{6,7},{7,4},{8,9},{9,10},{10,1... | collective-permute-start | bytes 2359304 | tf_op jit(solution)/shard_map/ppermute | solution.py:52
  10.8 53.5 %collective-permute-start.7 = (bf16[384,1024]{1,0:T(8,128)(2,1)}, bf16[384,1024]{1,0:T(8,128)(2,1)}, u32[]{:S(2)}, u32[]{:S(2)}) collective-permute-start(bf16[384,1024]{1,0:T(8,128)(2,1)} %bitcast.32), channel_id=1, source_target_pairs={{0,3},{1,0},{2,1},{3,2},{4,7},{5,4},{6,5},{7,6},{8,11},{9,8},{10,9... | collective-permute-start | bytes 2359304 | tf_op jit(solution)/shard_map/ppermute | solution.py:52
  15.1 9.5 %collective-permute-start.1 = (bf16[512,256]{1,0:T(8,128)(2,1)S(1)}, bf16[512,256]{1,0:T(8,128)(2,1)S(1)}, u32[]{:S(2)}, u32[]{:S(2)}) collective-permute-start(bf16[512,256]{1,0:T(8,128)(2,1)S(1)} %collective-permute-done), channel_id=1, source_target_pairs={{0,192},{1,193},{2,194},{3,195},{4,196},{5,197},{6,198},{7,199},{8... | collective-permute-start | bytes 786440 | tf_op jit(solution)/shard_map/ppermute | solution.py:52
  19.0 8.0 %collective-permute-start.2 = (bf16[512,256]{1,0:T(8,128)(2,1)S(1)}, bf16[512,256]{1,0:T(8,128)(2,1)S(1)}, u32[]{:S(2)}, u32[]{:S(2)}) collective-permute-start(bf16[512,256]{1,0:T(8,128)(2,1)S(1)} %collective-permute-done), channel_id=1, source_target_pairs={{0,128},{1,129},{2,130},{3,131},{4,132},{5,133},{6,134},{7,135},{8... | collective-permute-start | bytes 786440 | tf_op jit(solution)/shard_map/ppermute | solution.py:52
  20.5 13.9 %collective-permute-start.3 = (bf16[512,256]{1,0:T(8,128)(2,1)S(1)}, bf16[512,256]{1,0:T(8,128)(2,1)S(1)}, u32[]{:S(2)}, u32[]{:S(2)}) collective-permute-start(bf16[512,256]{1,0:T(8,128)(2,1)S(1)} %collective-permute-done), channel_id=1, source_target_pairs={{0,64},{1,65},{2,66},{3,67},{4,68},{5,69},{6,70},{7,71},{8,72},{9,... | collective-permute-start | bytes 786440 | tf_op jit(solution)/shard_map/ppermute | solution.py:52
  24.6 45.3 %collective-permute-start.5 = (bf16[384,1024]{1,0:T(8,128)(2,1)}, bf16[384,1024]{1,0:T(8,128)(2,1)}, u32[]{:S(2)}, u32[]{:S(2)}) collective-permute-start(bf16[384,1024]{1,0:T(8,128)(2,1)} %bitcast.33), channel_id=1, source_target_pairs={{0,2},{1,3},{2,0},{3,1},{4,6},{5,7},{6,4},{7,5},{8,10},{9,11},{10,... | collective-permute-start | bytes 2359304 | tf_op jit(solution)/shard_map/ppermute | solution.py:52
  34.4 29.9 %collective-permute-start.4 = (bf16[2048,256]{1,0:T(8,128)(2,1)S(1)}, bf16[2048,256]{1,0:T(8,128)(2,1)S(1)}, u32[]{:S(2)}, u32[]{:S(2)}) collective-permute-start(bf16[2048,256]{1,0:T(8,128)(2,1)S(1)} %constant_dynamic-update-slice_fusion.mine_ref), channel_id=1, source_target_pairs={{0,8},{1,9},{2,10},{3,11},{4,12},{5,13},{6,14},{7,15},{8,0},{9,1},... | collective-permute-start | bytes 3145736 | tf_op jit(solution)/shard_map/ppermute | solution.py:52
  64.3 2.2 %copy-start = (bf16[8192,256]{1,0:T(8,128)(2,1)S(1)}, bf16[8192,256]{1,0:T(8,128)(2,1)}, u32[]{:S(2)}) copy-start(bf16[8192,256]{1,0:T(8,128)(2,1)} %own_ref.3) | copy-start | bytes 12582916
  69.9 10.6 %copy-start.4 = (s32[24]{0:T(128)S(1)}, s32[24]{0:T(128)}, u32[]{:S(2)}) copy-start(s32[24]{0:T(128)} %target_ref.3) | copy-start | bytes 292
  71.9 8.5 %collective-permute-start.8 = (bf16[384,256]{1,0:T(8,128)(2,1)S(1)}, bf16[384,256]{1,0:T(8,128)(2,1)S(1)}, u32[]{:S(2)}, u32[]{:S(2)}) collective-permute-start(bf16[384,256]{1,0:T(8,128)(2,1)S(1)} %get-tuple-element.9), channel_id=1, source_target_pairs={{0,4},{1,5},{2,6},{3,7},{4,0},{5,1},{6,2},{7,3},{8,12},{9,13},{10,... | collective-permute-start | bytes 589832 | tf_op jit(solution)/shard_map/ppermute | solution.py:52
  72.8 25.2 %copy-start.9 = (s32[64,8]{0,1:T(8,128)S(1)}, s32[64,8]{0,1:T(8,128)}, u32[]{:S(2)}) copy-start(s32[64,8]{0,1:T(8,128)} %param.13) | copy-start | bytes 6148
  72.8 25.3 %copy-start.5 = (s32[64]{0:T(128)S(1)}, s32[64]{0:T(128)}, u32[]{:S(2)}) copy-start(s32[64]{0:T(128)} %len_ref.3) | copy-start | bytes 772
  72.8 25.3 %copy-start.6 = (s32[24]{0:T(128)S(1)}, s32[24]{0:T(128)}, u32[]{:S(2)}) copy-start(s32[24]{0:T(128)} %rows_ref.1) | copy-start | bytes 292
  82.0 32.8 %all-to-all-start.1 = ((bf16[32,32,256]{2,1,0:T(8,128)(2,1)}), bf16[32,32,256]{2,1,0:T(8,128)(2,1)S(1)}, u32[]{:S(2)}, u32[]{:S(2)}) async-start(bf16[32,32,256]{2,1,0:T(8,128)(2,1)} %bitcast.20), calls=%async_computation.1 | async-start | bytes 1048576 | tf_op jit(solution)/shard_map/all_to_all | solution.py:270
  98.1 2.2 %copy-start.1 = (bf16[512,16,256]{2,1,0:T(8,128)(2,1)S(1)}, bf16[512,16,256]{2,1,0:T(8,128)(2,1)}, u32[]{:S(2)}) copy-start(bf16[512,16,256]{2,1,0:T(8,128)(2,1)} %cache_ref.3) | copy-start | bytes 12582916
  103.4 83.1 %copy-start.7 = (bf16[64,2,1024]{2,1,0:T(2,128)(2,1)S(1)}, bf16[64,2,1024]{2,1,0:T(2,128)(2,1)}, u32[]{:S(2)}) copy-start(bf16[64,2,1024]{2,1,0:T(2,128)(2,1)} %param.10) | copy-start | bytes 786436
  103.4 83.2 %copy-start.8 = (bf16[64,2,256]{2,1,0:T(2,128)(2,1)S(1)}, bf16[64,2,256]{2,1,0:T(2,128)(2,1)}, u32[]{:S(2)}) copy-start(bf16[64,2,256]{2,1,0:T(2,128)(2,1)} %param.11) | copy-start | bytes 196612
  114.8 98.6 %all-to-all-start = ((bf16[32,96,256]{2,1,0:T(8,128)(2,1)}), bf16[32,96,256]{2,1,0:T(8,128)(2,1)S(1)}, u32[]{:S(2)}, u32[]{:S(2)}) async-start(bf16[32,96,256]{2,1,0:T(8,128)(2,1)} %bitcast.4), calls=%async_computation | async-start | bytes 3145728 | tf_op jit(solution)/shard_map/all_to_all | solution.py:270
  186.7 2.2 %copy-start.2 = (bf16[512,16,256]{2,1,0:T(8,128)(2,1)S(1)}, bf16[512,16,256]{2,1,0:T(8,128)(2,1)}, u32[]{:S(2)}) copy-start(bf16[512,16,256]{2,1,0:T(8,128)(2,1)} %cache_ref.3) | copy-start | bytes 12582916

commit v2 on v1

v2 whole, which is shorter than its diff:
```python
import functools
import math

import jax
import jax.numpy as jnp
from jax import lax
from jax.experimental import pallas as pl
from jax.experimental.pallas import tpu as pltpu
from jax.sharding import PartitionSpec as P

HD = 128
PAGE = 16
MAXP = 8
MIG = 24
PAIRS = MIG // 2
STORED = MAXP - 2
NX, NZL, NCORE, NZH, NY = 4, 4, 2, 2, 4
TP = NZH * NY
AXES = ("inst", "tp")
F32 = jnp.float32
BF16 = jnp.bfloat16


def index_of(x, zl, core, zh, y):
    return (((x * NZL + zl) * NCORE) + core) * TP + zh * NY + y


def moves(dx=0, dcore=0, dzh=0, dy=0, zl_xor=0):
    pairs = []
    for x in range(NX):
        for zl in range(NZL):
            for core in range(NCORE):
                for zh in range(NZH):
                    for y in range(NY):
                        pairs.append(
                            (
                                index_of(x, zl, core, zh, y),
                                index_of(
                                    (x + dx) % NX,
                                    zl ^ zl_xor,
                                    (core + dcore) % NCORE,
                                    (zh + dzh) % NZH,
                                    (y + dy) % NY,
                                ),
                            )
                        )
    return pairs


def send(value, **by):
    return lax.ppermute(value, AXES, moves(**by))


def params(mebibytes):
    return pltpu.CompilerParams(vmem_limit_bytes=mebibytes * 1024 * 1024)


SMEM = pl.BlockSpec(memory_space=pltpu.SMEM)
VMEM = pl.BlockSpec(memory_space=pltpu.VMEM)
HBM = pl.BlockSpec(memory_space=pltpu.HBM)


def meta_of(table, lengths, rows, target, place):
    parts = [table.reshape(-1), lengths, rows, target, jnp.stack(place)]
    return jnp.concatenate([p.astype(jnp.int32) for p in parts])


def meta_at(row_count):
    lengths = row_count * MAXP
    rows = lengths + row_count
    target = rows + MIG
    return lengths, rows, target, target + MIG


def pack_kernel(row_count, meta_ref, cache_ref, out_ref, sems):
    len_at, rows_at, target_at, place_at = meta_at(row_count)
    x_at, core_at = meta_ref[place_at], meta_ref[place_at + 2]
    for c in range(PAIRS):
        first = meta_ref[rows_at + 2 * c]
        second = meta_ref[rows_at + 2 * c + 1]
        target = meta_ref[target_at + 2 * c]
        x, z, core = target // (NZL * NCORE), target // NCORE % NZL, target % NCORE
        far_x = (x - x_at + NX) % NX
        base = (core ^ core_at) * STORED
        front = (meta_ref[len_at + first] + PAGE - 1) // PAGE - 1
        for m in range(STORED):
            in_front = m < front
            row = jnp.where(in_front, first, second)
            slot = jnp.where(in_front, m, jnp.minimum(m - front, MAXP - 1))
            page = meta_ref[row * MAXP + slot]
            pltpu.make_async_copy(
                cache_ref.at[page], out_ref.at[z, far_x, base + m], sems.at[c * STORED + m]
            ).start()
    for i in range(PAIRS * STORED):
        pltpu.make_async_copy(cache_ref.at[0], out_ref.at[0, 0, 0], sems.at[i]).wait()


def pack(meta, row_count, cache):
    lanes = cache.shape[-1]
    return pl.pallas_call(
        functools.partial(pack_kernel, row_count),
        out_shape=jax.ShapeDtypeStruct(
            (NZL, NX, NCORE * STORED, PAGE, lanes), cache.dtype
        ),
        in_specs=[SMEM, VMEM],
        out_specs=HBM,
        scratch_shapes=[pltpu.SemaphoreType.DMA((PAIRS * STORED,))],
        compiler_params=params(10),
        cost_estimate=pl.CostEstimate(flops=0, bytes_accessed=4 * 1024 * 1024, transcendentals=0),
        name="pack",
    )(meta, cache)


def attend_kernel(start, row_total, meta_ref, q_ref, new_ref, cache_ref, out_ref):
    row_count, heads, _ = q_ref.shape
    len_at = meta_at(row_total)[0]
    group = 8
    span = MAXP * PAGE + PAGE
    scale = 1.0 / math.sqrt(HD)
    column = lax.broadcasted_iota(jnp.int32, (heads, span), 1)
    step = lax.broadcasted_iota(jnp.int32, (heads, span), 0) // (heads // 2)
    own = (column >= MAXP * PAGE) & (column - MAXP * PAGE <= step)

    def body(i, carry):
        base = i * group
        scores = []
        values = []
        for u in range(group):
            r = base + u
            at = (start + r) * MAXP
            parts = [cache_ref[meta_ref[at + b]] for b in range(MAXP)] + [new_ref[r]]
            tokens = jnp.concatenate(parts, axis=0)
            raw = lax.dot_general(
                q_ref[r], tokens[:, :HD], (((1,), (1,)), ((), ())), preferred_element_type=F32
            )
            seen = (column < meta_ref[len_at + start + r]) | own
            scores.append(jnp.where(seen, raw * scale, -jnp.inf))
            values.append(tokens[:, HD:])
        stacked = jnp.concatenate(scores, axis=0)
        raised = jnp.exp(stacked - jnp.max(stacked, axis=-1, keepdims=True))
        weights = (raised / jnp.sum(raised, axis=-1, keepdims=True)).astype(BF16)
        mixed = [
            jnp.dot(weights[u * heads : (u + 1) * heads], values[u], preferred_element_type=F32)
            for u in range(group)
        ]
        for u in range(group):
            out_ref[base + u] = mixed[u].astype(BF16)
        return carry

    lax.fori_loop(0, row_count // group, body, 0)


def attend(start, row_total, q, fresh, cache, meta):
    row_count, heads, _ = q.shape
    return pl.pallas_call(
        functools.partial(attend_kernel, start, row_total),
        out_shape=jax.ShapeDtypeStruct((row_count, heads, HD), BF16),
        in_specs=[SMEM, VMEM, VMEM, VMEM],
        out_specs=VMEM,
        compiler_params=params(14),
        cost_estimate=pl.CostEstimate(
            flops=row_count * 16 * 144 * 128 * 4,
            bytes_accessed=row_count * 512 * 1024,
            transcendentals=0,
        ),
        name="attend",
    )(meta, q, fresh, cache)


def project_kernel(row_total, meta_ref, gain_ref, own_ref, mine_ref, other_ref, *refs):
    blocks = refs[:5]
    out_own_ref, out_oth_ref, out_sq_ref, in_ref, w_ref, x_ref, sems = refs[5:]
    place_at = meta_at(row_total)[3]
    x_at, core = meta_ref[place_at], meta_ref[place_at + 2]
    zh, y_at = meta_ref[place_at + 3], meta_ref[place_at + 4]
    _, tokens, depth = in_ref.shape
    half = tokens // 2
    part = depth // NCORE
    width = own_ref.shape[1]
    shifts = (0, NY - 1, 1, 2)

    def loads(i):
        y = (y_at + shifts[i]) % NY
        feature = zh * NY + y
        near = (y - x_at + NX) % NX
        rows = [
            pl.ds(pl.multiple_of((core ^ far) * part, part), part) for far in range(NCORE)
        ]
        copies = [
            (
                own_ref.at[pl.ds(pl.multiple_of(feature * depth, depth), depth)],
                w_ref.at[i, :, 0:width],
            ),
            (mine_ref.at[near, 0:part], w_ref.at[i, rows[0], width : 2 * width]),
            (other_ref.at[near, 0:part], w_ref.at[i, rows[1], width : 2 * width]),
        ]
        if i < 3:
            copies.append((blocks[i], in_ref.at[i]))
        else:
            copies.append((blocks[3], in_ref.at[i, 0:half]))
            copies.append((blocks[4], in_ref.at[i, half:tokens]))
        return [
            pltpu.make_async_copy(source, target, sems.at[i, n])
            for n, (source, target) in enumerate(copies)
        ]

    for i in range(NY):
        for copy in loads(i):
            copy.start()
    sums = None
    for i, shift in enumerate(shifts):
        gain = gain_ref[pl.ds(zh * NY + (y_at + shift) % NY, 1), :]
        for copy in loads(i):
            copy.wait()
        states = in_ref[i].astype(F32)
        squares = jnp.broadcast_to(jnp.sum(states * states, axis=1, keepdims=True), (tokens, HD))
        x_ref[i] = (states * gain).astype(BF16)
        parts = (jnp.dot(x_ref[i], w_ref[i], preferred_element_type=F32), squares)
        sums = parts if sums is None else tuple(p + q for p, q in zip(sums, parts))
    products, squares = sums
    out_own_ref[...] = products[:, 0:width]
    out_oth_ref[0:tokens, :] = products[:, width : 2 * width].astype(BF16)
    out_sq_ref[...] = squares
    turned = jnp.transpose(squares)
    front = turned[0:PAGE, 0 : 2 * HD]
    back = jnp.concatenate([turned[0:PAGE, 2 * HD : 3 * HD]] * 2, axis=1)
    line = lax.broadcasted_iota(jnp.int32, (PAGE, 2 * HD), 0)
    value = jnp.where(line < 3, front, back)
    term = line % 3
    high = value.astype(BF16).astype(F32)
    rest = value - high
    middle = rest.astype(BF16).astype(F32)
    lowest = rest - middle
    split = jnp.where(term == 0, high, jnp.where(term == 1, middle, lowest))
    out_oth_ref[tokens : tokens + PAGE, :] = jnp.where(line < 6, split, 0.0).astype(BF16)


def project(row_total, meta, gain, own, mine, other, blocks):
    tokens, depth = blocks[0].shape
    width = own.shape[1]
    return pl.pallas_call(
        functools.partial(project_kernel, row_total),
        out_shape=(
            jax.ShapeDtypeStruct((tokens, width), F32),
            jax.ShapeDtypeStruct((tokens + PAGE, width), BF16),
            jax.ShapeDtypeStruct((tokens, HD), F32),
        ),
        in_specs=[SMEM, VMEM, HBM, HBM, HBM] + [HBM] * len(blocks),
        out_specs=(VMEM, VMEM, VMEM),
        scratch_shapes=[
            pltpu.VMEM((NY, tokens, depth), BF16),
            pltpu.VMEM((NY, depth, 2 * width), BF16),
            pltpu.VMEM((NY, tokens, depth), BF16),
            pltpu.SemaphoreType.DMA((NY, 5)),
        ],
        compiler_params=params(56),
        cost_estimate=pl.CostEstimate(
            flops=NY * tokens * depth * width * 4,
            bytes_accessed=12 * 1024 * 1024,
            transcendentals=0,
        ),
        name="project",
    )(meta, gain, own, mine, other, *blocks)


def combine_kernel(
    features, row_total, meta_ref, own_ref, sq_ref, got_ref, turn_ref, out_ref
):
    tokens = own_ref.shape[0]
    total = own_ref[...] + got_ref[0:tokens, :].astype(F32)
    terms = got_ref[tokens : tokens + PAGE, :].astype(F32)
    line = lax.broadcasted_iota(jnp.int32, terms.shape, 0)
    front = jnp.sum(jnp.where(line < 3, terms, 0.0), axis=0, keepdims=True)
    back = jnp.sum(jnp.where(line >= 3, terms, 0.0), axis=0, keepdims=True)[:, 0:HD]
    row = jnp.concatenate([front, back], axis=1)
    squares = sq_ref[...] + jnp.transpose(jnp.broadcast_to(row, (HD, tokens)))
    inv = lax.rsqrt(squares * (1.0 / features) + 1e-05)
    turn = turn_ref[...]
    other = pltpu.roll(turn, HD // 2, 1)
    in_front = lax.broadcasted_iota(jnp.int32, turn.shape, 1) < HD // 2
    cosine = jnp.where(in_front, turn, other)
    sine = jnp.where(in_front, -other, turn)
    keys = total[:, :HD] * inv
    turned = keys * cosine + pltpu.roll(keys, HD // 2, 1) * sine
    page_rows = jnp.concatenate([turned, total[:, HD:] * inv], axis=1)
    len_at, rows_at, target_at, _ = meta_at(row_total)
    token = lax.broadcasted_iota(jnp.int32, (PAGE, page_rows.shape[1]), 0)
    for k in range(MIG):
        length = meta_ref[len_at + meta_ref[rows_at + k]]
        kept = length - (length - 1) // PAGE * PAGE
        page = jnp.where(token < kept, page_rows[k * PAGE : (k + 1) * PAGE], 0.0)
        out_ref[meta_ref[target_at + k] * 2 + k % 2] = page.astype(BF16)


def combine(features, row_total, meta, own, squares, got, turn, members):
    return pl.pallas_call(
        functools.partial(combine_kernel, features, row_total),
        out_shape=jax.ShapeDtypeStruct((members * 2, PAGE, own.shape[1]), BF16),
        in_specs=[SMEM] + [VMEM] * 4,
        out_specs=VMEM,
        compiler_params=params(10),
        name="combine",
    )(meta, own, squares, got, turn)


def assemble_kernel(row_total, meta_ref, counts_ref, *refs):
    kept_refs, other_ref, dirty_ref, out_ref = refs[:NX], refs[NX], refs[NX + 1], refs[NX + 2]
    place_at = meta_at(row_total)[3]
    x_at, z_at, core_at = (meta_ref[place_at + i] for i in range(3))

    for d in range(NX):
        x = (x_at - d + NX) % NX
        near = (x - x_at + NX) % NX
        for far_core in range(NCORE):

            def one(z, carry, d=d, x=x, near=near, far_core=far_core):
                far_z = z ^ z_at
                source = (x * NZL + z) * NCORE + (core_at ^ far_core)
                entry = (far_core * NX + near) * NZL + far_z
                first = counts_ref[2 * entry]
                second = counts_ref[2 * entry + 1]
                for m in range(MAXP):
                    behind = (m >= first).astype(jnp.int32)
                    index = jnp.clip(m - behind, 0, STORED - 1)
                    if far_core == 0:
                        kept = kept_refs[d][z, index]
                    else:
                        kept = other_ref[d, z, index]
                    made = dirty_ref[source * 2 + behind]
                    is_made = (m == first - 1) | (m == first + second - 1)
                    page = jnp.where(is_made, made, kept)
                    out_ref[source * MAXP + m] = jnp.where(
                        m < first + second, page, jnp.zeros_like(page)
                    )
                return carry

            lax.fori_loop(0, NZL, one, 0, unroll=2)


def assemble(row_total, meta, counts, kept, other, dirty, members):
    lanes = dirty.shape[-1]
    return pl.pallas_call(
        functools.partial(assemble_kernel, row_total),
        out_shape=jax.ShapeDtypeStruct((members * MAXP, PAGE, lanes), dirty.dtype),
        in_specs=[SMEM, SMEM] + [VMEM] * (NX + 2),
        out_specs=VMEM,
        compiler_params=params(14),
        name="assemble",
    )(meta, counts, *kept, other, dirty)


def exchange(pages, members, each):
    lanes = pages.shape[-1]
    moved = lax.all_to_all(
        pages.reshape(members, each * PAGE, lanes), "inst", split_axis=0, concat_axis=0, tiled=True
    )
    return moved.reshape(members * each, PAGE, lanes)


def per_device(
    queries,
    new_kv,
    kv_cache,
    block_table,
    lengths,
    mig_rows,
    mig_target,
    dirty_hidden,
    norm_gain,
    kv_weight,
):
    members = lax.axis_size("inst")
    inst = lax.axis_index("inst")
    tp = lax.axis_index("tp")
    x_at, z_lo, core = inst // (NZL * NCORE), inst // NCORE % NZL, inst % NCORE
    zh, y_at = tp // NY, tp % NY
    tokens = MIG * PAGE
    depth = dirty_hidden.shape[-1]
    features = depth * TP
    half_features = depth * NY

    row_count = queries.shape[0]
    meta = meta_of(block_table, lengths, mig_rows, mig_target, (x_at, z_lo, core, zh, y_at))

    hidden = dirty_hidden.reshape(tokens, depth)
    from_below = send(hidden, dy=1)
    from_above = send(hidden, dy=-1)

    picked = mig_rows[:, None] == jnp.arange(row_count, dtype=jnp.int32)[None, :]
    mig_len = jnp.sum(jnp.where(picked, lengths[None, :], 0), axis=1)
    mig_pages = (mig_len + PAGE - 1) // PAGE

    slice_rows = half_features // (NX * NCORE)
    begin = (1 - zh) * half_features + (x_at * NCORE + core) * slice_rows
    width = kv_weight.shape[1]
    notes = jnp.pad(
        jnp.stack([mig_target, mig_pages]).astype(BF16), ((0, PAGE - 2), (0, width - MIG))
    )
    notes = jnp.concatenate([notes[:2], send(notes, zl_xor=1)[:2]], axis=0)
    outgoing_slice = jnp.concatenate(
        [
            lax.dynamic_slice_in_dim(kv_weight, begin, slice_rows, axis=0),
            jnp.pad(notes, ((0, PAGE - 4), (0, 0))),
        ],
        axis=0,
    )
    slice_here = send(outgoing_slice, dzh=1, zl_xor=2)
    noted = jnp.concatenate(
        [slice_here[:slice_rows], notes, slice_here[slice_rows : slice_rows + PAGE - 4]], axis=0
    )
    packed = pack(meta, row_count, kv_cache)
    noted, from_below, from_above, packed = lax.optimization_barrier(
        (noted, from_below, from_above, packed)
    )
    across_top = send(from_below[: tokens // 2], dy=1)
    across_bottom = send(from_above[tokens // 2 :], dy=-1)
    slices = jnp.stack([noted] + [send(noted, dx=-d) for d in range(1, NX)])

    lines = [
        [(x * NZL + z) * NCORE + c for z in range(NZL)] for x in range(NX) for c in range(NCORE)
    ]
    by_z = lax.all_to_all(
        packed, "inst", split_axis=0, concat_axis=0, axis_index_groups=lines, tiled=True
    )

    offsets = jnp.arange(PAGE, dtype=jnp.int32)
    positions = ((mig_pages - 1) * PAGE)[:, None] + offsets[None, :]
    half_dim = HD // 2
    frequency = jnp.exp(
        jnp.arange(half_dim, dtype=F32) * (-2.0 * math.log(500000.0) / HD)
    )
    angles = positions.reshape(tokens).astype(F32)[:, None] * frequency[None, :]
    turn = jnp.concatenate([jnp.cos(angles), jnp.sin(angles)], axis=1)

    gain = norm_gain.astype(F32).reshape(TP, depth)

    slices, across_top, across_bottom = lax.optimization_barrier(
        (slices, across_top, across_bottom)
    )
    other_slices = send(slices, dcore=1)
    own, outgoing, squares = project(
        row_count,
        meta,
        gain,
        kv_weight,
        slices,
        other_slices,
        (hidden, from_below, from_above, across_top, across_bottom),
    )
    outgoing, by_z = lax.optimization_barrier((outgoing, by_z))
    got = send(outgoing, dzh=1)

    by_x = [by_z[:, d] for d in range(NX)]
    by_x = [by_x[0]] + [send(by_x[d], dx=d) for d in range(1, NX)]
    lines = slice(slice_rows, slice_rows + 2 * NZL)
    heard = jnp.stack([slices[:, lines, :MIG], other_slices[:, lines, :MIG]])
    heard = heard.reshape(NCORE, NX, NZL, 2, MIG)
    aimed_here = heard[..., 0, :] == inst.astype(BF16)
    counts = jnp.sum(
        jnp.where(aimed_here, heard[..., 1, :], jnp.zeros((), BF16))
        .astype(F32)
        .reshape(NCORE, NX, NZL, PAIRS, 2),
        axis=3,
    ).astype(jnp.int32)
    got, counts, turn = lax.optimization_barrier((got, counts, turn))
    made = combine(features, row_count, meta, own, squares, got, turn, members)
    dirty = exchange(made, members, 2)

    heads = queries.shape[-1] // HD
    q = queries.reshape(row_count, 2 * heads, HD)
    fresh = jnp.pad(new_kv, ((0, 0), (0, PAGE - 2), (0, 0)))
    q, fresh, _ = lax.optimization_barrier((q, fresh, made))
    decoded = attend(0, row_count, q, fresh, kv_cache, meta)
    decoded = decoded.reshape(row_count, 2, heads * HD)
    other_kept = send(jnp.stack([part[:, STORED:] for part in by_x]), dcore=1)
    dirty, decoded = lax.optimization_barrier((dirty, decoded))
    mig_kv = assemble(
        row_count, meta, counts.reshape(-1), by_x, other_kept, dirty, members
    )
    return decoded, mig_kv


def solution(mesh):
    return jax.shard_map(
        per_device,
        mesh=mesh,
        in_specs=(
            P("inst", None, "tp"),
            P("inst", None, "tp"),
            P("inst", None, "tp"),
            P("inst", None),
            P("inst"),
            P("inst"),
            P("inst"),
            P("inst", None, "tp"),
            P(),
            P(None, "tp"),
        ),
        out_specs=(P("inst", None, "tp"), P("inst", None, "tp")),
        check_vma=False,
    )
```

time: 217 us -> 114 us (0.53)
  blocking collectives: 96.1 us -> 0 us
  Pallas kernels: 37 us -> 18.2 us
  waiting for transfers between devices: 31.5 us -> 35 us
  local copies, waits for them, and re-layouts: 10.2 us -> 13.4 us
  other arithmetic: 2.36 us -> 4.88 us
  starting transfers between devices: 38.6 us -> 41.1 us
    all_gather x1 -> x0, blocking collectives: 67.6 us -> none  [per_device(): notes = lax.all_gather(jnp.stack([mig_target, mig_pages]), 'inst', axis=0)]
    psum x1 -> x0, blocking collectives: 28.5 us -> none  [per_device(): squares = lax.psum(squares, 'tp')]
    pallas_call x6 -> x5, Pallas kernels: 37 us -> 18.2 us  [the longest x1 5.75 us: project(): pl.pallas_call(functools.partial(project_kernel, row_total), out_shape=(j...]
    all_to_all x2 -> x1, starting transfers between devices: 19.8 us -> 7.65 us  [exchange(): lax.all_to_all(pages.reshape(members, each * PAGE, lanes), 'inst', split_...]
    ppermute x9 -> x15, starting transfers between devices: 18.9 us -> 29.8 us  [send(): return lax.ppermute(value, AXES, moves(**by))]
    all_to_all x0 -> x1, waiting for transfers between devices: none -> 8.07 us  [per_device(): lax.all_to_all(packed, 'inst', split_axis=0, concat_axis=0, axis_index_gr...]
    all_to_all x2 -> x1, waiting for transfers between devices: 11.4 us -> 5.94 us  [exchange(): lax.all_to_all(pages.reshape(members, each * PAGE, lanes), 'inst', split_...]
    all_to_all x0 -> x1, starting transfers between devices: none -> 3.58 us  [per_device(): lax.all_to_all(packed, 'inst', split_axis=0, concat_axis=0, axis_index_gr...]
  transfers between devices with their start and end apart: 11 -> 17, of which waited for: 5 -> 7; matrix products, arithmetic and copies ran while one was open for 2% -> 11% of each run, Pallas kernels for 14% -> 13%
where the time goes in v2:
time: 114 us; the launch traced here: 113 us
  starting transfers between devices  41.1 us (36%)
  waiting for transfers between devices  35 us (31%)
  Pallas kernels  18.2 us (16%)
  local copies, waits for them, and re-layouts  13.4 us (12%)
  other arithmetic  4.88 us (4%)
    ppermute x15, starting transfers between devices, send(): return lax.ppermute(value, AXES, moves(**by))  29.8 us
    ppermute x15, waiting for transfers between devices, send(): return lax.ppermute(value, AXES, moves(**by))  21 us
    all_to_all x1, waiting for transfers between devices, per_device(): lax.all_to_all(packed, 'inst', split_axis=0, concat_axis=0, axis_index_gr...  8.07 us
    all_to_all x1, starting transfers between devices, exchange(): lax.all_to_all(pages.reshape(members, each * PAGE, lanes), 'inst', split_...  7.65 us
    all_to_all x1, waiting for transfers between devices, exchange(): lax.all_to_all(pages.reshape(members, each * PAGE, lanes), 'inst', split_...  5.94 us
    pallas_call x1, Pallas kernels, project(): pl.pallas_call(functools.partial(project_kernel, row_total), out_shape=(j...  5.75 us
    unnamed x24, local copies, waits for them, and re-layouts  5.19 us
    pallas_call x1, Pallas kernels, attend(): pl.pallas_call(functools.partial(attend_kernel, start, row_total), out_sh...  5.12 us
  transfers between devices with their start and end apart: 17, of which 7 were waited for; matrix products, arithmetic and copies ran while one was open for 11% of the time, Pallas kernels for 13%

profile of v2, /device:TPU:1, one launch (start us, length us, event | category | flops | bytes accessed | tf_op | source)
XLA Modules:
  0.0 113.5 jit_solution(8994023767846950261)
XLA Ops:
  0.6 2.2 %collective-permute-start.2 = (bf16[384,1024]{1,0:T(8,128)(2,1)}, bf16[384,1024]{1,0:T(8,128)(2,1)S(1)}, u32[]{:S(2)}, u32[]{:S(2)}) collective-permute-start(bf16[384,1024]{1,0:T(8,128)(2,1)} %bitcast.45), channel_id=1, source_target_pairs={{0,1},{1,2},{2,3},{3,0},{4,5},{5,6},{6,7},{7,4},{8,9},{9,10},{10,1... | collective-permute-start | bytes 2359304 | tf_op jit(solution)/shard_map/ppermute | solution.py:51
  2.8 1.5 %collective-permute-start.3 = (bf16[384,1024]{1,0:T(8,128)(2,1)}, bf16[384,1024]{1,0:T(8,128)(2,1)S(1)}, u32[]{:S(2)}, u32[]{:S(2)}) collective-permute-start(bf16[384,1024]{1,0:T(8,128)(2,1)} %bitcast.46), channel_id=1, source_target_pairs={{0,3},{1,0},{2,1},{3,2},{4,7},{5,4},{6,5},{7,6},{8,11},{9,8},{10,9... | collective-permute-start | bytes 2359304 | tf_op jit(solution)/shard_map/ppermute | solution.py:51
  4.4 0.9 select_reduce_fusion
  5.9 1.7 %collective-permute-start = (bf16[16,256]{1,0:T(8,128)(2,1)S(1)}, bf16[16,256]{1,0:T(8,128)(2,1)S(1)}, u32[]{:S(2)}, u32[]{:S(2)}) collective-permute-start(bf16[16,256]{1,0:T(8,128)(2,1)S(1)} %fusion.7), channel_id=1, source_target_pairs={{0,16},{1,17},{2,18},{3,19},{4,20},{5,21},{6,22},{7,23},{8,24},{9,... | collective-permute-start | bytes 24584 | tf_op jit(solution)/shard_map/ppermute | solution.py:51
  7.6 1.0 constant_dynamic-slice_fusion
  9.0 5.9 %collective-permute-start.1 = (bf16[528,256]{1,0:T(8,128)(2,1)S(1)}, bf16[528,256]{1,0:T(8,128)(2,1)S(1)}, u32[]{:S(2)}, u32[]{:S(2)}) collective-permute-start(bf16[528,256]{1,0:T(8,128)(2,1)S(1)} %pad_maximum_fusion.2), channel_id=1, source_target_pairs={{0,36},{1,37},{2,38},{3,39},{4,32},{5,33},{6,34},{7,35},{8,44},{9,... | collective-permute-start | bytes 811016 | tf_op jit(solution)/shard_map/ppermute | solution.py:51
  16.6 2.2 %copy-done = bf16[512,16,256]{2,1,0:T(8,128)(2,1)S(1)} copy-done((bf16[512,16,256]{2,1,0:T(8,128)(2,1)S(1)}, bf16[512,16,256]{2,1,0:T(8,128)(2,1)}, u32[]{:S(2)}) %copy-start) | copy-done | bytes 4194328
  18.8 2.4 %pack.1 = bf16[4,4,12,16,256]{4,3,2,1,0:T(8,128)(2,1)} custom-call(s32[629]{0:T(1024)S(1)} %concatenate.17.meta_ref, bf16[512,16,256]{2,1,0:T(8,128)(2,1)S(1)} %copy-done), custom_call_target="tpu_custom_call" | custom-call | bytes 4194304 | tf_op jit(solution)/shard_map/pack/pallas_call | solution.py:100
  21.2 5.2 %collective-permute-done.1 = bf16[528,256]{1,0:T(8,128)(2,1)S(1)} collective-permute-done((bf16[528,256]{1,0:T(8,128)(2,1)S(1)}, bf16[528,256]{1,0:T(8,128)(2,1)S(1)}, u32[]{:S(2)}, u32[]{:S(2)}) %collective-permute-start.1) | collective-permute-done | bytes 270368 | tf_op jit(solution)/shard_map/ppermute | solution.py:51
  26.5 3.6 %all-to-all-start = ((bf16[4,4,12,16,256]{4,3,2,1,0:T(8,128)(2,1)}), bf16[4,4,12,16,256]{4,3,2,1,0:T(8,128)(2,1)S(1)}, u32[]{:S(2)}, u32[]{:S(2)}) async-start(bf16[4,4,12,16,256]{4,3,2,1,0:T(8,128)(2,1)} %pack.1), calls=%async_computation | async-start | bytes 3145728 | tf_op jit(solution)/shard_map/all_to_all | solution.py:422
  30.1 2.8 %collective-permute-start.5 = (bf16[528,256]{1,0:T(8,128)(2,1)S(1)}, bf16[528,256]{1,0:T(8,128)(2,1)}, u32[]{:S(2)}, u32[]{:S(2)}) collective-permute-start(bf16[528,256]{1,0:T(8,128)(2,1)S(1)} %pad_maximum_fusion.3), channel_id=1, source_target_pairs={{0,128},{1,129},{2,130},{3,131},{4,132},{5,133},{6,134},{7,135},{8... | collective-permute-start | bytes 811016 | tf_op jit(solution)/shard_map/ppermute | solution.py:51
  33.3 2.4 %collective-permute-start.4 = (bf16[528,256]{1,0:T(8,128)(2,1)S(1)}, bf16[528,256]{1,0:T(8,128)(2,1)}, u32[]{:S(2)}, u32[]{:S(2)}) collective-permute-start(bf16[528,256]{1,0:T(8,128)(2,1)S(1)} %pad_maximum_fusion.3), channel_id=1, source_target_pairs={{0,192},{1,193},{2,194},{3,195},{4,196},{5,197},{6,198},{7,199},{8... | collective-permute-start | bytes 811016 | tf_op jit(solution)/shard_map/ppermute | solution.py:51
  36.4 0.8 slice.59
  37.2 2.7 %collective-permute-start.8 = (bf16[192,1024]{1,0:T(8,128)(2,1)}, bf16[192,1024]{1,0:T(8,128)(2,1)}, u32[]{:S(2)}, u32[]{:S(2)}) collective-permute-start(bf16[192,1024]{1,0:T(8,128)(2,1)} %slice.59), channel_id=1, source_target_pairs={{0,3},{1,0},{2,1},{3,2},{4,7},{5,4},{6,5},{7,6},{8,11},{9,8},{10,9... | collective-permute-start | bytes 1179656 | tf_op jit(solution)/shard_map/ppermute | solution.py:51
  40.5 5.5 %collective-permute-done.6 = bf16[528,256]{1,0:T(8,128)(2,1)} collective-permute-done((bf16[528,256]{1,0:T(8,128)(2,1)S(1)}, bf16[528,256]{1,0:T(8,128)(2,1)}, u32[]{:S(2)}, u32[]{:S(2)}) %collective-permute-start.6) | collective-permute-done | bytes 270368 | tf_op jit(solution)/shard_map/ppermute | solution.py:51
  46.0 1.3 %pad_maximum_fusion.mine_ref = bf16[4,528,256]{2,1,0:T(8,128)(2,1)S(1)} fusion(bf16[1,528,256]{2,1,0:T(8,128)(2,1)} %bitcast.11, bf16[1,528,256]{2,1,0:T(8,128)(2,1)} %bitcast.10, bf16[1,528,256]{2,1,0:T(8,128)(2,1)} %bitcast.9, bf16[1,528,256]{2,1,0:T(8,128)(2,1)S(1)} %bitcast.44), kind=kLoop, calls=%fused_computation | loop fusion | flops 1622016 | bytes 2162688 | tf_op jit(solution)/shard_map/stack | solution.py:417
  47.3 2.2 %collective-permute-start.9 = (bf16[4,528,256]{2,1,0:T(8,128)(2,1)S(1)}, bf16[4,528,256]{2,1,0:T(8,128)(2,1)}, u32[]{:S(2)}, u32[]{:S(2)}) collective-permute-start(bf16[4,528,256]{2,1,0:T(8,128)(2,1)S(1)} %pad_maximum_fusion.mine_ref), channel_id=1, source_target_pairs={{0,8},{1,9},{2,10},{3,11},{4,12},{5,13},{6,14},{7,15},{8,0},{9,1},... | collective-permute-start | bytes 3244040 | tf_op jit(solution)/shard_map/ppermute | solution.py:51
  50.6 1.4 %collective-permute-done.9.other_ref = bf16[4,528,256]{2,1,0:T(8,128)(2,1)} collective-permute-done((bf16[4,528,256]{2,1,0:T(8,128)(2,1)S(1)}, bf16[4,528,256]{2,1,0:T(8,128)(2,1)}, u32[]{:S(2)}, u32[]{:S(2)}) %collective-permute-start.9) | collective-permute-done | bytes 1081376 | tf_op jit(solution)/shard_map/ppermute | solution.py:51
  52.7 5.8 %project.1 = (f32[384,256]{1,0:T(8,128)}, bf16[400,256]{1,0:T(8,128)(2,1)}, f32[384,128]{1,0:T(8,128)}) custom-call(s32[629]{0:T(1024)} %copy-done.4, f32[8,1024]{1,0:T(8,128)} %reshape.150.gain_ref, bf16[8192,256]{1,0:T(8,128)(2,1)} %own_ref.1, bf16[4,528,256]{2,1,0:T(8,128)(2,1)} %copy-done.6, bf16[4,528,256]{2,1,0:T(8,128)(2,1)} %collective-permute-done.9.other_ref, ...), custom_call_target="tpu_custom_call" | custom-call | flops 1610612736 | bytes 12582912 | tf_op jit(solution)/shard_map/project/pallas_call | solution.py:241
  58.4 8.1 %all-to-all-done = bf16[4,4,12,16,256]{4,3,2,1,0:T(8,128)(2,1)S(1)} async-done(((bf16[4,4,12,16,256]{4,3,2,1,0:T(8,128)(2,1)}), bf16[4,4,12,16,256]{4,3,2,1,0:T(8,128)(2,1)S(1)}, u32[]{:S(2)}, u32[]{:S(2)}) %all-to-all-start) | async-done | bytes 1572896 | tf_op jit(solution)/shard_map/all_to_all | solution.py:422
  66.5 1.0 slice_bitcast_fusion
  67.5 2.5 %collective-permute-start.13 = (bf16[4,12,16,256]{3,2,1,0:T(8,128)(2,1)}, bf16[4,12,16,256]{3,2,1,0:T(8,128)(2,1)S(1)}, u32[]{:S(2)}, u32[]{:S(2)}) collective-permute-start(bf16[4,12,16,256]{3,2,1,0:T(8,128)(2,1)} %get-tuple-element.40), channel_id=1, source_target_pairs={{0,192},{1,193},{2,194},{3,195},{4,196},{5,197},{6,198},{7,199},{8... | collective-permute-start | bytes 1179656 | tf_op jit(solution)/shard_map/ppermute | solution.py:51
  71.4 4.1 %collective-permute-start.10 = (bf16[400,256]{1,0:T(8,128)(2,1)}, bf16[400,256]{1,0:T(8,128)(2,1)S(1)}, u32[]{:S(2)}, u32[]{:S(2)}) collective-permute-start(bf16[400,256]{1,0:T(8,128)(2,1)} %get-tuple-element.31), channel_id=1, source_target_pairs={{0,4},{1,5},{2,6},{3,7},{4,0},{5,1},{6,2},{7,3},{8,12},{9,13},{10,... | collective-permute-start | bytes 614408 | tf_op jit(solution)/shard_map/ppermute | solution.py:51
  75.6 8.4 %collective-permute-done.10.got_ref = bf16[400,256]{1,0:T(8,128)(2,1)S(1)} collective-permute-done((bf16[400,256]{1,0:T(8,128)(2,1)}, bf16[400,256]{1,0:T(8,128)(2,1)S(1)}, u32[]{:S(2)}, u32[]{:S(2)}) %collective-permute-start.10) | collective-permute-done | bytes 204832 | tf_op jit(solution)/shard_map/ppermute | solution.py:51
  84.0 1.6 %combine.1 = bf16[64,16,256]{2,1,0:T(8,128)(2,1)} custom-call(s32[629]{0:T(1024)S(1)} %copy-done.5, f32[384,256]{1,0:T(8,128)S(1)} %copy-done.2, f32[384,128]{1,0:T(8,128)S(1)} %copy-done.3, bf16[400,256]{1,0:T(8,128)(2,1)S(1)} %collective-permute-done.10.got_ref, f32[384,128]{1,0:T(8,128)S(1)} %pad_maximum_fusion.4.turn_ref), custom_call_target="tpu_custom_call" | custom-call | tf_op jit(solution)/shard_map/combine/pallas_call | solution.py:296
  85.7 7.7 %all-to-all-start.1 = ((bf16[32,32,256]{2,1,0:T(8,128)(2,1)}), bf16[32,32,256]{2,1,0:T(8,128)(2,1)S(1)}, u32[]{:S(2)}, u32[]{:S(2)}) async-start(bf16[32,32,256]{2,1,0:T(8,128)(2,1)} %bitcast.15), calls=%async_computation.1 | async-start | bytes 1048576 | tf_op jit(solution)/shard_map/all_to_all | solution.py:354
  93.4 1.0 pad_maximum_fusion.1
  94.7 1.1 reshape.146.q_ref
  95.9 2.2 %copy-done.1 = bf16[512,16,256]{2,1,0:T(8,128)(2,1)S(1)} copy-done((bf16[512,16,256]{2,1,0:T(8,128)(2,1)S(1)}, bf16[512,16,256]{2,1,0:T(8,128)(2,1)}, u32[]{:S(2)}) %copy-start.1) | copy-done | bytes 4194328
  98.1 5.1 %attend.1 = bf16[64,16,128]{2,1,0:T(8,128)(2,1)S(1)} custom-call(s32[629]{0:T(1024)S(1)} %copy-done.5, bf16[64,16,128]{2,1,0:T(8,128)(2,1)S(1)} %reshape.146.q_ref, bf16[64,16,256]{2,1,0:T(8,128)(2,1)S(1)} %pad.14.new_ref, bf16[512,16,256]{2,1,0:T(8,128)(2,1)S(1)} %copy-done.1), custom_call_target="tpu_custom_call" | custom-call | flops 75497472 | bytes 33554432 | tf_op jit(solution)/shard_map/attend/pallas_call | solution.py:155
  104.2 5.9 %all-to-all-done.1 = bf16[32,32,256]{2,1,0:T(8,128)(2,1)S(1)} async-done(((bf16[32,32,256]{2,1,0:T(8,128)(2,1)}), bf16[32,32,256]{2,1,0:T(8,128)(2,1)S(1)}, u32[]{:S(2)}, u32[]{:S(2)}) %all-to-all-start.1) | async-done | bytes 524320 | tf_op jit(solution)/shard_map/all_to_all | solution.py:354
  110.1 3.3 %assemble.1 = bf16[256,16,256]{2,1,0:T(8,128)(2,1)} custom-call(s32[629]{0:T(1024)S(1)} %copy-done.5, s32[64]{0:T(128)S(1)} %reshape.148.counts_ref, bf16[4,12,16,256]{3,2,1,0:T(8,128)(2,1)S(1)} %get-tuple-element.43.refs_0_, bf16[4,12,16,256]{3,2,1,0:T(8,128)(2,1)S(1)} %collective-permute-done.11.refs_1_, ...), custom_call_target="tpu_custom_call" | custom-call | tf_op jit(solution)/shard_map/assemble/pallas_call | solution.py:342
  (73 shorter events, 9.1 us)
Async XLA Ops:
  0.6 25.9 %collective-permute-start.2 = (bf16[384,1024]{1,0:T(8,128)(2,1)}, bf16[384,1024]{1,0:T(8,128)(2,1)S(1)}, u32[]{:S(2)}, u32[]{:S(2)}) collective-permute-start(bf16[384,1024]{1,0:T(8,128)(2,1)} %bitcast.45), channel_id=1, source_target_pairs={{0,1},{1,2},{2,3},{3,0},{4,5},{5,6},{6,7},{7,4},{8,9},{9,10},{10,1... | collective-permute-start | bytes 2359304 | tf_op jit(solution)/shard_map/ppermute | solution.py:51
  2.8 23.7 %collective-permute-start.3 = (bf16[384,1024]{1,0:T(8,128)(2,1)}, bf16[384,1024]{1,0:T(8,128)(2,1)S(1)}, u32[]{:S(2)}, u32[]{:S(2)}) collective-permute-start(bf16[384,1024]{1,0:T(8,128)(2,1)} %bitcast.46), channel_id=1, source_target_pairs={{0,3},{1,0},{2,1},{3,2},{4,7},{5,4},{6,5},{7,6},{8,11},{9,8},{10,9... | collective-permute-start | bytes 2359304 | tf_op jit(solution)/shard_map/ppermute | solution.py:51
  5.9 3.1 %collective-permute-start = (bf16[16,256]{1,0:T(8,128)(2,1)S(1)}, bf16[16,256]{1,0:T(8,128)(2,1)S(1)}, u32[]{:S(2)}, u32[]{:S(2)}) collective-permute-start(bf16[16,256]{1,0:T(8,128)(2,1)S(1)} %fusion.7), channel_id=1, source_target_pairs={{0,16},{1,17},{2,18},{3,19},{4,20},{5,21},{6,22},{7,23},{8,24},{9,... | collective-permute-start | bytes 24584 | tf_op jit(solution)/shard_map/ppermute | solution.py:51
  9.0 17.4 %collective-permute-start.1 = (bf16[528,256]{1,0:T(8,128)(2,1)S(1)}, bf16[528,256]{1,0:T(8,128)(2,1)S(1)}, u32[]{:S(2)}, u32[]{:S(2)}) collective-permute-start(bf16[528,256]{1,0:T(8,128)(2,1)S(1)} %pad_maximum_fusion.2), channel_id=1, source_target_pairs={{0,36},{1,37},{2,38},{3,39},{4,32},{5,33},{6,34},{7,35},{8,44},{9,... | collective-permute-start | bytes 811016 | tf_op jit(solution)/shard_map/ppermute | solution.py:51
  16.6 2.2 %copy-start = (bf16[512,16,256]{2,1,0:T(8,128)(2,1)S(1)}, bf16[512,16,256]{2,1,0:T(8,128)(2,1)}, u32[]{:S(2)}) copy-start(bf16[512,16,256]{2,1,0:T(8,128)(2,1)} %cache_ref.3) | copy-start | bytes 12582916
  18.8 2.4 %copy-start.4 = (s32[629]{0:T(1024)}, s32[629]{0:T(1024)S(1)}, u32[]{:S(2)}) copy-start(s32[629]{0:T(1024)S(1)} %concatenate.17.meta_ref) | copy-start | bytes 7552
  26.5 9.1 %copy-start.7 = (bf16[384,1024]{1,0:T(8,128)(2,1)}, bf16[384,1024]{1,0:T(8,128)(2,1)S(1)}, u32[]{:S(2)}) copy-start(bf16[384,1024]{1,0:T(8,128)(2,1)S(1)} %collective-permute-done.2.refs_1_) | copy-start | bytes 2359300
  26.5 9.9 %copy-start.8 = (bf16[384,1024]{1,0:T(8,128)(2,1)}, bf16[384,1024]{1,0:T(8,128)(2,1)S(1)}, u32[]{:S(2)}) copy-start(bf16[384,1024]{1,0:T(8,128)(2,1)S(1)} %collective-permute-done.3.refs_2_) | copy-start | bytes 2359300
  26.5 40.0 %all-to-all-start = ((bf16[4,4,12,16,256]{4,3,2,1,0:T(8,128)(2,1)}), bf16[4,4,12,16,256]{4,3,2,1,0:T(8,128)(2,1)S(1)}, u32[]{:S(2)}, u32[]{:S(2)}) async-start(bf16[4,4,12,16,256]{4,3,2,1,0:T(8,128)(2,1)} %pack.1), calls=%async_computation | async-start | bytes 3145728 | tf_op jit(solution)/shard_map/all_to_all | solution.py:422
  30.1 9.8 %copy-start.10 = (bf16[8192]{0:T(1024)(128)(2,1)S(1)}, bf16[8192]{0:T(1024)(128)(2,1)}, u32[]{:S(2)}) copy-start(bf16[8192]{0:T(1024)(128)(2,1)} %param.18) | copy-start | bytes 49156
  30.1 10.4 %collective-permute-start.5 = (bf16[528,256]{1,0:T(8,128)(2,1)S(1)}, bf16[528,256]{1,0:T(8,128)(2,1)}, u32[]{:S(2)}, u32[]{:S(2)}) collective-permute-start(bf16[528,256]{1,0:T(8,128)(2,1)S(1)} %pad_maximum_fusion.3), channel_id=1, source_target_pairs={{0,128},{1,129},{2,130},{3,131},{4,132},{5,133},{6,134},{7,135},{8... | collective-permute-start | bytes 811016 | tf_op jit(solution)/shard_map/ppermute | solution.py:51
  32.9 13.1 %collective-permute-start.6 = (bf16[528,256]{1,0:T(8,128)(2,1)S(1)}, bf16[528,256]{1,0:T(8,128)(2,1)}, u32[]{:S(2)}, u32[]{:S(2)}) collective-permute-start(bf16[528,256]{1,0:T(8,128)(2,1)S(1)} %pad_maximum_fusion.3), channel_id=1, source_target_pairs={{0,64},{1,65},{2,66},{3,67},{4,68},{5,69},{6,70},{7,71},{8,72},{9,... | collective-permute-start | bytes 811016 | tf_op jit(solution)/shard_map/ppermute | solution.py:51
  33.3 12.8 %collective-permute-start.4 = (bf16[528,256]{1,0:T(8,128)(2,1)S(1)}, bf16[528,256]{1,0:T(8,128)(2,1)}, u32[]{:S(2)}, u32[]{:S(2)}) collective-permute-start(bf16[528,256]{1,0:T(8,128)(2,1)S(1)} %pad_maximum_fusion.3), channel_id=1, source_target_pairs={{0,192},{1,193},{2,194},{3,195},{4,196},{5,197},{6,198},{7,199},{8... | collective-permute-start | bytes 811016 | tf_op jit(solution)/shard_map/ppermute | solution.py:51
  36.4 10.9 %collective-permute-start.7 = (bf16[192,1024]{1,0:T(8,128)(2,1)}, bf16[192,1024]{1,0:T(8,128)(2,1)}, u32[]{:S(2)}, u32[]{:S(2)}) collective-permute-start(bf16[192,1024]{1,0:T(8,128)(2,1)} %slice.58), channel_id=1, source_target_pairs={{0,1},{1,2},{2,3},{3,0},{4,5},{5,6},{6,7},{7,4},{8,9},{9,10},{10,1... | collective-permute-start | bytes 1179656 | tf_op jit(solution)/shard_map/ppermute | solution.py:51
  37.2 10.1 %collective-permute-start.8 = (bf16[192,1024]{1,0:T(8,128)(2,1)}, bf16[192,1024]{1,0:T(8,128)(2,1)}, u32[]{:S(2)}, u32[]{:S(2)}) collective-permute-start(bf16[192,1024]{1,0:T(8,128)(2,1)} %slice.59), channel_id=1, source_target_pairs={{0,3},{1,0},{2,1},{3,2},{4,7},{5,4},{6,5},{7,6},{8,11},{9,8},{10,9... | collective-permute-start | bytes 1179656 | tf_op jit(solution)/shard_map/ppermute | solution.py:51
  47.3 5.4 %copy-start.6 = (bf16[4,528,256]{2,1,0:T(8,128)(2,1)}, bf16[4,528,256]{2,1,0:T(8,128)(2,1)S(1)}, u32[]{:S(2)}) copy-start(bf16[4,528,256]{2,1,0:T(8,128)(2,1)S(1)} %pad_maximum_fusion.mine_ref) | copy-start | bytes 3244036
  47.3 4.7 %collective-permute-start.9 = (bf16[4,528,256]{2,1,0:T(8,128)(2,1)S(1)}, bf16[4,528,256]{2,1,0:T(8,128)(2,1)}, u32[]{:S(2)}, u32[]{:S(2)}) collective-permute-start(bf16[4,528,256]{2,1,0:T(8,128)(2,1)S(1)} %pad_maximum_fusion.mine_ref), channel_id=1, source_target_pairs={{0,8},{1,9},{2,10},{3,11},{4,12},{5,13},{6,14},{7,15},{8,0},{9,1},... | collective-permute-start | bytes 3244040 | tf_op jit(solution)/shard_map/ppermute | solution.py:51
  66.5 17.5 %copy-start.2 = (f32[384,256]{1,0:T(8,128)S(1)}, f32[384,256]{1,0:T(8,128)}, u32[]{:S(2)}) copy-start(f32[384,256]{1,0:T(8,128)} %get-tuple-element.27.own_ref) | copy-start | bytes 1179652
  66.5 17.5 %copy-start.3 = (f32[384,128]{1,0:T(8,128)S(1)}, f32[384,128]{1,0:T(8,128)}, u32[]{:S(2)}) copy-start(f32[384,128]{1,0:T(8,128)} %get-tuple-element.28.sq_ref) | copy-start | bytes 589828
  66.5 17.5 %copy-start.5 = (s32[629]{0:T(1024)S(1)}, s32[629]{0:T(1024)}, u32[]{:S(2)}) copy-start(s32[629]{0:T(1024)} %copy-done.4) | copy-start | bytes 7552
  67.5 25.8 %collective-permute-start.13 = (bf16[4,12,16,256]{3,2,1,0:T(8,128)(2,1)}, bf16[4,12,16,256]{3,2,1,0:T(8,128)(2,1)S(1)}, u32[]{:S(2)}, u32[]{:S(2)}) collective-permute-start(bf16[4,12,16,256]{3,2,1,0:T(8,128)(2,1)} %get-tuple-element.40), channel_id=1, source_target_pairs={{0,192},{1,193},{2,194},{3,195},{4,196},{5,197},{6,198},{7,199},{8... | collective-permute-start | bytes 1179656 | tf_op jit(solution)/shard_map/ppermute | solution.py:51
  70.2 23.2 %collective-permute-start.12 = (bf16[4,12,16,256]{3,2,1,0:T(8,128)(2,1)}, bf16[4,12,16,256]{3,2,1,0:T(8,128)(2,1)S(1)}, u32[]{:S(2)}, u32[]{:S(2)}) collective-permute-start(bf16[4,12,16,256]{3,2,1,0:T(8,128)(2,1)} %get-tuple-element.41), channel_id=1, source_target_pairs={{0,128},{1,129},{2,130},{3,131},{4,132},{5,133},{6,134},{7,135},{8... | collective-permute-start | bytes 1179656 | tf_op jit(solution)/shard_map/ppermute | solution.py:51
  70.8 22.6 %collective-permute-start.11 = (bf16[4,12,16,256]{3,2,1,0:T(8,128)(2,1)S(1)}, bf16[4,12,16,256]{3,2,1,0:T(8,128)(2,1)S(1)}, u32[]{:S(2)}, u32[]{:S(2)}) collective-permute-start(bf16[4,12,16,256]{3,2,1,0:T(8,128)(2,1)S(1)} %get-tuple-element.42), channel_id=1, source_target_pairs={{0,64},{1,65},{2,66},{3,67},{4,68},{5,69},{6,70},{7,71},{8,72},{9,... | collective-permute-start | bytes 1179656 | tf_op jit(solution)/shard_map/ppermute | solution.py:51
  71.4 12.6 %collective-permute-start.10 = (bf16[400,256]{1,0:T(8,128)(2,1)}, bf16[400,256]{1,0:T(8,128)(2,1)S(1)}, u32[]{:S(2)}, u32[]{:S(2)}) collective-permute-start(bf16[400,256]{1,0:T(8,128)(2,1)} %get-tuple-element.31), channel_id=1, source_target_pairs={{0,4},{1,5},{2,6},{3,7},{4,0},{5,1},{6,2},{7,3},{8,12},{9,13},{10,... | collective-permute-start | bytes 614408 | tf_op jit(solution)/shard_map/ppermute | solution.py:51
  85.7 24.5 %all-to-all-start.1 = ((bf16[32,32,256]{2,1,0:T(8,128)(2,1)}), bf16[32,32,256]{2,1,0:T(8,128)(2,1)S(1)}, u32[]{:S(2)}, u32[]{:S(2)}) async-start(bf16[32,32,256]{2,1,0:T(8,128)(2,1)} %bitcast.15), calls=%async_computation.1 | async-start | bytes 1048576 | tf_op jit(solution)/shard_map/all_to_all | solution.py:354
  93.3 2.5 %copy-start.9 = (bf16[64,2,256]{2,1,0:T(2,128)(2,1)S(1)}, bf16[64,2,256]{2,1,0:T(2,128)(2,1)}, u32[]{:S(2)}) copy-start(bf16[64,2,256]{2,1,0:T(2,128)(2,1)} %param.11) | copy-start | bytes 196612
  94.4 15.7 %collective-permute-start.14 = (bf16[4,4,6,16,256]{4,3,2,1,0:T(8,128)(2,1)}, bf16[4,4,6,16,256]{4,3,2,1,0:T(8,128)(2,1)S(1)}, u32[]{:S(2)}, u32[]{:S(2)}) collective-permute-start(bf16[4,4,6,16,256]{4,3,2,1,0:T(8,128)(2,1)} %pad_maximum_fusion.1), channel_id=1, source_target_pairs={{0,8},{1,9},{2,10},{3,11},{4,12},{5,13},{6,14},{7,15},{8,0},{9,1},... | collective-permute-start | bytes 2359304 | tf_op jit(solution)/shard_map/ppermute | solution.py:51
  95.9 2.2 %copy-start.1 = (bf16[512,16,256]{2,1,0:T(8,128)(2,1)S(1)}, bf16[512,16,256]{2,1,0:T(8,128)(2,1)}, u32[]{:S(2)}) copy-start(bf16[512,16,256]{2,1,0:T(8,128)(2,1)} %cache_ref.3) | copy-start | bytes 12582916

commit v3 on v2

--- a/solution.py
+++ b/solution.py
@@ -72,16 +72,12 @@
     return lengths, rows, target, target + MIG
 
 
-def pack_kernel(row_count, meta_ref, cache_ref, out_ref, sems):
+def pack_kernel(row_count, meta_ref, cache_ref, out_ref, held_ref, in_sems, out_sems):
     len_at, rows_at, target_at, place_at = meta_at(row_count)
     x_at, core_at = meta_ref[place_at], meta_ref[place_at + 2]
     for c in range(PAIRS):
         first = meta_ref[rows_at + 2 * c]
         second = meta_ref[rows_at + 2 * c + 1]
-        target = meta_ref[target_at + 2 * c]
-        x, z, core = target // (NZL * NCORE), target // NCORE % NZL, target % NCORE
-        far_x = (x - x_at + NX) % NX
-        base = (core ^ core_at) * STORED
         front = (meta_ref[len_at + first] + PAGE - 1) // PAGE - 1
         for m in range(STORED):
             in_front = m < front
@@ -89,10 +85,27 @@
             slot = jnp.where(in_front, m, jnp.minimum(m - front, MAXP - 1))
             page = meta_ref[row * MAXP + slot]
             pltpu.make_async_copy(
-                cache_ref.at[page], out_ref.at[z, far_x, base + m], sems.at[c * STORED + m]
+                cache_ref.at[page], held_ref.at[c, m], in_sems.at[c * STORED + m]
             ).start()
-    for i in range(PAIRS * STORED):
-        pltpu.make_async_copy(cache_ref.at[0], out_ref.at[0, 0, 0], sems.at[i]).wait()
+
+    def out_copy(c):
+        target = meta_ref[target_at + 2 * c]
+        x, z, core = target // (NZL * NCORE), target // NCORE % NZL, target % NCORE
+        far_x = (x - x_at + NX) % NX
+        return pltpu.make_async_copy(
+            held_ref.at[c],
+            out_ref.at[z, far_x, pl.ds((core ^ core_at) * STORED, STORED)],
+            out_sems.at[c],
+        )
+
+    for c in range(PAIRS):
+        for m in range(STORED):
+            pltpu.make_async_copy(
+                cache_ref.at[0], held_ref.at[c, m], in_sems.at[c * STORED + m]
+            ).wait()
+        out_copy(c).start()
+    for c in range(PAIRS):
+        out_copy(c).wait()
 
 
 def pack(meta, row_count, cache):
@@ -102,10 +115,14 @@
         out_shape=jax.ShapeDtypeStruct(
             (NZL, NX, NCORE * STORED, PAGE, lanes), cache.dtype
         ),
-        in_specs=[SMEM, VMEM],
+        in_specs=[SMEM, HBM],
         out_specs=HBM,
-        scratch_shapes=[pltpu.SemaphoreType.DMA((PAIRS * STORED,))],
-        compiler_params=params(10),
+        scratch_shapes=[
+            pltpu.VMEM((PAIRS, STORED, PAGE, lanes), cache.dtype),
+            pltpu.SemaphoreType.DMA((PAIRS * STORED,)),
+            pltpu.SemaphoreType.DMA((PAIRS,)),
+        ],
+        compiler_params=params(60),
         cost_estimate=pl.CostEstimate(flops=0, bytes_accessed=4 * 1024 * 1024, transcendentals=0),
         name="pack",
     )(meta, cache)
@@ -316,7 +333,7 @@
             def one(z, carry, d=d, x=x, near=near, far_core=far_core):
                 far_z = z ^ z_at
                 source = (x * NZL + z) * NCORE + (core_at ^ far_core)
-                entry = (far_core * NX + near) * NZL + far_z
+                entry = (far_z * NCORE + far_core) * NX + near
                 first = counts_ref[2 * entry]
                 second = counts_ref[2 * entry + 1]
                 for m in range(MAXP):
@@ -393,25 +410,17 @@
     slice_rows = half_features // (NX * NCORE)
     begin = (1 - zh) * half_features + (x_at * NCORE + core) * slice_rows
     width = kv_weight.shape[1]
+    slice_here = send(
+        lax.dynamic_slice_in_dim(kv_weight, begin, slice_rows, axis=0), dzh=1, zl_xor=2
+    )
     notes = jnp.pad(
         jnp.stack([mig_target, mig_pages]).astype(BF16), ((0, PAGE - 2), (0, width - MIG))
     )
-    notes = jnp.concatenate([notes[:2], send(notes, zl_xor=1)[:2]], axis=0)
-    outgoing_slice = jnp.concatenate(
-        [
-            lax.dynamic_slice_in_dim(kv_weight, begin, slice_rows, axis=0),
-            jnp.pad(notes, ((0, PAGE - 4), (0, 0))),
-        ],
-        axis=0,
-    )
-    slice_here = send(outgoing_slice, dzh=1, zl_xor=2)
-    noted = jnp.concatenate(
-        [slice_here[:slice_rows], notes, slice_here[slice_rows : slice_rows + PAGE - 4]], axis=0
-    )
     packed = pack(meta, row_count, kv_cache)
-    noted, from_below, from_above, packed = lax.optimization_barrier(
-        (noted, from_below, from_above, packed)
-    )
+    slice_here, from_below, from_above, _ = lax.optimization_barrier(
+        (slice_here, from_below, from_above, packed)
+    )
+    noted = jnp.concatenate([slice_here, notes], axis=0)
     across_top = send(from_below[: tokens // 2], dy=1)
     across_bottom = send(from_above[tokens // 2 :], dy=-1)
     slices = jnp.stack([noted] + [send(noted, dx=-d) for d in range(1, NX)])
@@ -452,28 +461,30 @@
 
     by_x = [by_z[:, d] for d in range(NX)]
     by_x = [by_x[0]] + [send(by_x[d], dx=d) for d in range(1, NX)]
-    lines = slice(slice_rows, slice_rows + 2 * NZL)
+    heads = queries.shape[-1] // HD
+    q = queries.reshape(row_count, 2 * heads, HD)
+    fresh = jnp.pad(new_kv, ((0, 0), (0, PAGE - 2), (0, 0)))
+    q, fresh, _ = lax.optimization_barrier((q, fresh, outgoing))
+    decoded = attend(0, row_count, q, fresh, kv_cache, meta)
+    decoded = decoded.reshape(row_count, 2, heads * HD)
+    got, turn, decoded = lax.optimization_barrier((got, turn, decoded))
+    made = combine(features, row_count, meta, own, squares, got, turn, members)
+
+    lines = slice(slice_rows, slice_rows + 2)
     heard = jnp.stack([slices[:, lines, :MIG], other_slices[:, lines, :MIG]])
-    heard = heard.reshape(NCORE, NX, NZL, 2, MIG)
+    heard, _ = lax.optimization_barrier((heard, made))
+    heard = jnp.stack([heard, send(heard, zl_xor=1)])
+    heard = jnp.concatenate([heard, send(heard, zl_xor=2)])
     aimed_here = heard[..., 0, :] == inst.astype(BF16)
     counts = jnp.sum(
         jnp.where(aimed_here, heard[..., 1, :], jnp.zeros((), BF16))
         .astype(F32)
-        .reshape(NCORE, NX, NZL, PAIRS, 2),
+        .reshape(NZL, NCORE, NX, PAIRS, 2),
         axis=3,
     ).astype(jnp.int32)
-    got, counts, turn = lax.optimization_barrier((got, counts, turn))
-    made = combine(features, row_count, meta, own, squares, got, turn, members)
     dirty = exchange(made, members, 2)
 
-    heads = queries.shape[-1] // HD
-    q = queries.reshape(row_count, 2 * heads, HD)
-    fresh = jnp.pad(new_kv, ((0, 0), (0, PAGE - 2), (0, 0)))
-    q, fresh, _ = lax.optimization_barrier((q, fresh, made))
-    decoded = attend(0, row_count, q, fresh, kv_cache, meta)
-    decoded = decoded.reshape(row_count, 2, heads * HD)
     other_kept = send(jnp.stack([part[:, STORED:] for part in by_x]), dcore=1)
-    dirty, decoded = lax.optimization_barrier((dirty, decoded))
     mig_kv = assemble(
         row_count, meta, counts.reshape(-1), by_x, other_kept, dirty, members
     )

time: 114 us -> 105 us (0.921)
  waiting for transfers between devices: 35 us -> 26.7 us
  other arithmetic: 4.88 us -> 2.49 us
    ppermute x15 -> x16, waiting for transfers between devices: 21 us -> 16.8 us  [send(): return lax.ppermute(value, AXES, moves(**by))]
    all_to_all x1, waiting for transfers between devices: 5.94 us -> 2.19 us  [exchange(): lax.all_to_all(pages.reshape(members, each * PAGE, lanes), 'inst', split_...]
    unnamed x24 -> x29, local copies, waits for them, and re-layouts: 5.19 us -> 3.02 us
    squeeze x1, local copies, waits for them, and re-layouts: 0.99 us -> 2.42 us  [per_device(): by_x = [by_z[:, d] for d in range(NX)]]
    ppermute x15 -> x16, starting transfers between devices: 29.8 us -> 30.5 us  [send(): return lax.ppermute(value, AXES, moves(**by))]
  transfers between devices with their start and end apart: 17 -> 18, of which waited for: 7 -> 10; matrix products, arithmetic and copies ran while one was open for 11% -> 11% of each run, Pallas kernels for 13% -> 15%
where the time goes in v3:
time: 105 us
  starting transfers between devices  42.1 us (40%)
  waiting for transfers between devices  26.7 us (25%)
  Pallas kernels  19.1 us (18%)
  local copies, waits for them, and re-layouts  13.2 us (13%)
  other arithmetic  2.49 us (2%)
    ppermute x16, starting transfers between devices, send(): return lax.ppermute(value, AXES, moves(**by))  30.5 us
    ppermute x16, waiting for transfers between devices, send(): return lax.ppermute(value, AXES, moves(**by))  16.8 us
    all_to_all x1, waiting for transfers between devices, per_device(): lax.all_to_all(packed, 'inst', split_axis=0, concat_axis=0, axis_index_gr...  7.68 us
    all_to_all x1, starting transfers between devices, exchange(): lax.all_to_all(pages.reshape(members, each * PAGE, lanes), 'inst', split_...  7.14 us
    pallas_call x1, Pallas kernels, project(): pl.pallas_call(functools.partial(project_kernel, row_total), out_shape=(j...  5.76 us
    pallas_call x1, Pallas kernels, attend(): pl.pallas_call(functools.partial(attend_kernel, start, row_total), out_sh...  5.12 us
    all_to_all x1, starting transfers between devices, per_device(): lax.all_to_all(packed, 'inst', split_axis=0, concat_axis=0, axis_index_gr...  4.5 us
    pallas_call x1, Pallas kernels, assemble(): pl.pallas_call(functools.partial(assemble_kernel, row_total), out_shape=j...  3.34 us
  transfers between devices with their start and end apart: 18, of which 10 were waited for; matrix products, arithmetic and copies ran while one was open for 11% of the time, Pallas kernels for 15%

profile of v3, /device:TPU:1, one launch (start us, length us, event | category | flops | bytes accessed | tf_op | source)
XLA Modules:
  0.0 104.5 jit_solution(5188982333656934282)
XLA Ops:
  0.6 2.2 %collective-permute-start.1 = (bf16[384,1024]{1,0:T(8,128)(2,1)}, bf16[384,1024]{1,0:T(8,128)(2,1)S(1)}, u32[]{:S(2)}, u32[]{:S(2)}) collective-permute-start(bf16[384,1024]{1,0:T(8,128)(2,1)} %bitcast.49), channel_id=1, source_target_pairs={{0,1},{1,2},{2,3},{3,0},{4,5},{5,6},{6,7},{7,4},{8,9},{9,10},{10,1... | collective-permute-start | bytes 2359304 | tf_op jit(solution)/shard_map/ppermute | solution.py:51
  2.8 1.5 %collective-permute-start.2 = (bf16[384,1024]{1,0:T(8,128)(2,1)}, bf16[384,1024]{1,0:T(8,128)(2,1)S(1)}, u32[]{:S(2)}, u32[]{:S(2)}) collective-permute-start(bf16[384,1024]{1,0:T(8,128)(2,1)} %bitcast.50), channel_id=1, source_target_pairs={{0,3},{1,0},{2,1},{3,2},{4,7},{5,4},{6,5},{7,6},{8,11},{9,8},{10,9... | collective-permute-start | bytes 2359304 | tf_op jit(solution)/shard_map/ppermute | solution.py:51
  4.4 1.0 constant_dynamic-slice_fusion
  5.3 6.1 %collective-permute-start = (bf16[512,256]{1,0:T(8,128)(2,1)S(1)}, bf16[512,256]{1,0:T(8,128)(2,1)S(1)}, u32[]{:S(2)}, u32[]{:S(2)}) collective-permute-start(bf16[512,256]{1,0:T(8,128)(2,1)S(1)} %constant_dynamic-slice_fusion), channel_id=1, source_target_pairs={{0,36},{1,37},{2,38},{3,39},{4,32},{5,33},{6,34},{7,35},{8,44},{9,... | collective-permute-start | bytes 786440 | tf_op jit(solution)/shard_map/ppermute | solution.py:51
  12.3 1.4 %concatenate.13.meta_ref = s32[629]{0:T(1024)} concatenate(s32[512]{0:T(512)S(1)} %reshape.135, s32[64]{0:T(128)} %param.14, s32[24]{0:T(128)} %param.15, s32[24]{0:T(128)} %param.16, s32[1]{0:T(128)} %bitcast, s32[1]{0:T(128)} %bitcast.1, s32[1]{0:T(128)} %bitcast.2, s32[1]{0:T(128)} %bitcast.3, s32[1]{0:T(128)} %bitcast.4), dimensions={0} | concatenate | bytes 5032 | tf_op jit(solution)/shard_map/concatenate | solution.py:65
  13.7 3.2 %pack.1 = bf16[4,4,12,16,256]{4,3,2,1,0:T(8,128)(2,1)} custom-call(s32[629]{0:T(1024)} %concatenate.13.meta_ref, bf16[512,16,256]{2,1,0:T(8,128)(2,1)} %cache_ref.3), custom_call_target="tpu_custom_call" | custom-call | bytes 4194304 | tf_op jit(solution)/shard_map/pack/pallas_call | solution.py:113
  16.9 4.5 %all-to-all-start = ((bf16[4,4,12,16,256]{4,3,2,1,0:T(8,128)(2,1)}), bf16[4,4,12,16,256]{4,3,2,1,0:T(8,128)(2,1)}, u32[]{:S(2)}, u32[]{:S(2)}) async-start(bf16[4,4,12,16,256]{4,3,2,1,0:T(8,128)(2,1)} %pack.1), calls=%async_computation | async-start | bytes 3145728 | tf_op jit(solution)/shard_map/all_to_all | solution.py:431
  21.7 0.9 collective-permute-done
  22.6 2.8 %collective-permute-start.4 = (bf16[528,256]{1,0:T(8,128)(2,1)S(1)}, bf16[528,256]{1,0:T(8,128)(2,1)S(1)}, u32[]{:S(2)}, u32[]{:S(2)}) collective-permute-start(bf16[528,256]{1,0:T(8,128)(2,1)S(1)} %get-tuple-element.41), channel_id=1, source_target_pairs={{0,128},{1,129},{2,130},{3,131},{4,132},{5,133},{6,134},{7,135},{8... | collective-permute-start | bytes 811016 | tf_op jit(solution)/shard_map/ppermute | solution.py:51
  25.8 2.4 %collective-permute-start.3 = (bf16[528,256]{1,0:T(8,128)(2,1)S(1)}, bf16[528,256]{1,0:T(8,128)(2,1)S(1)}, u32[]{:S(2)}, u32[]{:S(2)}) collective-permute-start(bf16[528,256]{1,0:T(8,128)(2,1)S(1)} %get-tuple-element.41), channel_id=1, source_target_pairs={{0,192},{1,193},{2,194},{3,195},{4,196},{5,197},{6,198},{7,199},{8... | collective-permute-start | bytes 811016 | tf_op jit(solution)/shard_map/ppermute | solution.py:51
  28.9 0.8 slice.43
  29.7 2.7 %collective-permute-start.7 = (bf16[192,1024]{1,0:T(8,128)(2,1)}, bf16[192,1024]{1,0:T(8,128)(2,1)}, u32[]{:S(2)}, u32[]{:S(2)}) collective-permute-start(bf16[192,1024]{1,0:T(8,128)(2,1)} %slice.43), channel_id=1, source_target_pairs={{0,3},{1,0},{2,1},{3,2},{4,7},{5,4},{6,5},{7,6},{8,11},{9,8},{10,9... | collective-permute-start | bytes 1179656 | tf_op jit(solution)/shard_map/ppermute | solution.py:51
  33.0 1.1 %reshape.139.q_ref = bf16[64,16,128]{2,1,0:T(8,128)(2,1)S(1)} reshape(bf16[64,2,1024]{2,1,0:T(2,128)(2,1)} %param.10) | data formatting | bytes 524288 | tf_op jit(solution)/shard_map/reshape | solution.py:465
  34.1 4.3 %collective-permute-done.5 = bf16[528,256]{1,0:T(8,128)(2,1)S(1)} collective-permute-done((bf16[528,256]{1,0:T(8,128)(2,1)S(1)}, bf16[528,256]{1,0:T(8,128)(2,1)S(1)}, u32[]{:S(2)}, u32[]{:S(2)}) %collective-permute-start.5) | collective-permute-done | bytes 270368 | tf_op jit(solution)/shard_map/ppermute | solution.py:51
  39.1 2.9 %collective-permute-start.8 = (bf16[4,528,256]{2,1,0:T(8,128)(2,1)S(1)}, bf16[4,528,256]{2,1,0:T(8,128)(2,1)}, u32[]{:S(2)}, u32[]{:S(2)}) collective-permute-start(bf16[4,528,256]{2,1,0:T(8,128)(2,1)S(1)} %pad_maximum_fusion.mine_ref), channel_id=1, source_target_pairs={{0,8},{1,9},{2,10},{3,11},{4,12},{5,13},{6,14},{7,15},{8,0},{9,1},... | collective-permute-start | bytes 3244040 | tf_op jit(solution)/shard_map/ppermute | solution.py:51
  43.2 1.3 %collective-permute-done.8.other_ref = bf16[4,528,256]{2,1,0:T(8,128)(2,1)} collective-permute-done((bf16[4,528,256]{2,1,0:T(8,128)(2,1)S(1)}, bf16[4,528,256]{2,1,0:T(8,128)(2,1)}, u32[]{:S(2)}, u32[]{:S(2)}) %collective-permute-start.8) | collective-permute-done | bytes 1081376 | tf_op jit(solution)/shard_map/ppermute | solution.py:51
  44.5 5.8 %project.1 = (f32[384,256]{1,0:T(8,128)}, bf16[400,256]{1,0:T(8,128)(2,1)}, f32[384,128]{1,0:T(8,128)}) custom-call(s32[629]{0:T(1024)} %concatenate.13.meta_ref, f32[8,1024]{1,0:T(8,128)} %reshape.144.gain_ref, bf16[8192,256]{1,0:T(8,128)(2,1)} %own_ref.1, bf16[4,528,256]{2,1,0:T(8,128)(2,1)} %copy-done.4, ...), custom_call_target="tpu_custom_call" | custom-call | flops 1610612736 | bytes 12582912 | tf_op jit(solution)/shard_map/project/pallas_call | solution.py:258
  50.3 7.7 %all-to-all-done = bf16[4,4,12,16,256]{4,3,2,1,0:T(8,128)(2,1)} async-done(((bf16[4,4,12,16,256]{4,3,2,1,0:T(8,128)(2,1)}), bf16[4,4,12,16,256]{4,3,2,1,0:T(8,128)(2,1)}, u32[]{:S(2)}, u32[]{:S(2)}) %all-to-all-start) | async-done | bytes 1572896 | tf_op jit(solution)/shard_map/all_to_all | solution.py:431
  58.0 2.4 %slice_bitcast_fusion = (bf16[4,12,16,256]{3,2,1,0:T(8,128)(2,1)}, bf16[4,12,16,256]{3,2,1,0:T(8,128)(2,1)}, bf16[4,12,16,256]{3,2,1,0:T(8,128)(2,1)}, bf16[4,12,16,256]{3,2,1,0:T(8,128)(2,1)S(1)}) fusion(bf16[4,4,12,16,256]{4,3,2,1,0:T(8,128)(2,1)} %all-to-all-done), kind=kLoop, calls=%fused_computation.2 | loop fusion | bytes 3145728 | tf_op jit(solution)/shard_map/squeeze | solution.py:462
  60.4 2.5 %collective-permute-start.14 = (bf16[4,12,16,256]{3,2,1,0:T(8,128)(2,1)}, bf16[4,12,16,256]{3,2,1,0:T(8,128)(2,1)S(1)}, u32[]{:S(2)}, u32[]{:S(2)}) collective-permute-start(bf16[4,12,16,256]{3,2,1,0:T(8,128)(2,1)} %get-tuple-element.36), channel_id=1, source_target_pairs={{0,192},{1,193},{2,194},{3,195},{4,196},{5,197},{6,198},{7,199},{8... | collective-permute-start | bytes 1179656 | tf_op jit(solution)/shard_map/ppermute | solution.py:51
  65.2 2.2 %copy-done = bf16[512,16,256]{2,1,0:T(8,128)(2,1)S(1)} copy-done((bf16[512,16,256]{2,1,0:T(8,128)(2,1)S(1)}, bf16[512,16,256]{2,1,0:T(8,128)(2,1)}, u32[]{:S(2)}) %copy-start) | copy-done | bytes 4194328
  67.3 5.1 %attend.1 = bf16[64,16,128]{2,1,0:T(8,128)(2,1)S(1)} custom-call(s32[629]{0:T(1024)S(1)} %copy-done.3, bf16[64,16,128]{2,1,0:T(8,128)(2,1)S(1)} %reshape.139.q_ref, bf16[64,16,256]{2,1,0:T(8,128)(2,1)S(1)} %pad.9.new_ref, bf16[512,16,256]{2,1,0:T(8,128)(2,1)S(1)} %copy-done), custom_call_target="tpu_custom_call" | custom-call | flops 75497472 | bytes 33554432 | tf_op jit(solution)/shard_map/attend/pallas_call | solution.py:172
  73.3 2.1 %collective-permute-done.9.got_ref = bf16[400,256]{1,0:T(8,128)(2,1)S(1)} collective-permute-done((bf16[400,256]{1,0:T(8,128)(2,1)S(1)}, bf16[400,256]{1,0:T(8,128)(2,1)S(1)}, u32[]{:S(2)}, u32[]{:S(2)}) %collective-permute-start.9) | collective-permute-done | bytes 204832 | tf_op jit(solution)/shard_map/ppermute | solution.py:51
  75.4 1.6 %combine.1 = bf16[64,16,256]{2,1,0:T(8,128)(2,1)} custom-call(s32[629]{0:T(1024)S(1)} %copy-done.3, f32[384,256]{1,0:T(8,128)S(1)} %copy-done.1, f32[384,128]{1,0:T(8,128)S(1)} %copy-done.2, bf16[400,256]{1,0:T(8,128)(2,1)S(1)} %collective-permute-done.9.got_ref, f32[384,128]{1,0:T(8,128)S(1)} %pad_maximum_fusion.3.turn_ref), custom_call_target="tpu_custom_call" | custom-call | tf_op jit(solution)/shard_map/combine/pallas_call | solution.py:313
  77.1 7.1 %all-to-all-start.1 = ((bf16[32,32,256]{2,1,0:T(8,128)(2,1)}), bf16[32,32,256]{2,1,0:T(8,128)(2,1)S(1)}, u32[]{:S(2)}, u32[]{:S(2)}) async-start(bf16[32,32,256]{2,1,0:T(8,128)(2,1)} %bitcast.25), calls=%async_computation.1 | async-start | bytes 1048576 | tf_op jit(solution)/shard_map/all_to_all | solution.py:371
  84.8 1.0 pad_maximum_fusion.1
  86.2 0.9 collective-permute-start.10
  87.1 5.9 %collective-permute-done.10 = bf16[2,4,2,24]{3,2,1,0:T(2,128)(2,1)S(1)} collective-permute-done((bf16[2,4,2,24]{3,2,1,0:T(2,128)(2,1)S(1)}, bf16[2,4,2,24]{3,2,1,0:T(2,128)(2,1)S(1)}, u32[]{:S(2)}, u32[]{:S(2)}) %collective-permute-start.10) | collective-permute-done | bytes 800 | tf_op jit(solution)/shard_map/ppermute | solution.py:51
  93.0 4.1 %collective-permute-start.11 = (bf16[2,2,4,2,24]{4,3,2,1,0:T(2,128)(2,1)S(1)}, bf16[2,2,4,2,24]{4,3,2,1,0:T(2,128)(2,1)S(1)}, u32[]{:S(2)}, u32[]{:S(2)}) collective-permute-start(bf16[2,2,4,2,24]{4,3,2,1,0:T(2,128)(2,1)S(1)} %pad_maximum_fusion.5), channel_id=1, source_target_pairs={{0,32},{1,33},{2,34},{3,35},{4,36},{5,37},{6,38},{7,39},{8,40},{9,... | collective-permute-start | bytes 4616 | tf_op jit(solution)/shard_map/ppermute | solution.py:51
  97.2 1.3 %collective-permute-done.11 = bf16[2,2,4,2,24]{4,3,2,1,0:T(2,128)(2,1)S(1)} collective-permute-done((bf16[2,2,4,2,24]{4,3,2,1,0:T(2,128)(2,1)S(1)}, bf16[2,2,4,2,24]{4,3,2,1,0:T(2,128)(2,1)S(1)}, u32[]{:S(2)}, u32[]{:S(2)}) %collective-permute-start.11) | collective-permute-done | bytes 1568 | tf_op jit(solution)/shard_map/ppermute | solution.py:51
  99.0 2.2 %all-to-all-done.1 = bf16[32,32,256]{2,1,0:T(8,128)(2,1)S(1)} async-done(((bf16[32,32,256]{2,1,0:T(8,128)(2,1)}), bf16[32,32,256]{2,1,0:T(8,128)(2,1)S(1)}, u32[]{:S(2)}, u32[]{:S(2)}) %all-to-all-start.1) | async-done | bytes 524320 | tf_op jit(solution)/shard_map/all_to_all | solution.py:371
  101.2 3.3 %assemble.1 = bf16[256,16,256]{2,1,0:T(8,128)(2,1)} custom-call(s32[629]{0:T(1024)S(1)} %copy-done.3, s32[64]{0:T(128)S(1)} %convert_element_type.43.counts_ref, bf16[4,12,16,256]{3,2,1,0:T(8,128)(2,1)S(1)} %get-tuple-element.39.refs_0_, bf16[4,12,16,256]{3,2,1,0:T(8,128)(2,1)S(1)} %collective-permute-done.12.refs_1_, ...), custom_call_target="tpu_custom_call" | custom-call | tf_op jit(solution)/shard_map/assemble/pallas_call | solution.py:359
  (76 shorter events, 9.3 us)
Async XLA Ops:
  0.6 21.9 %collective-permute-start.1 = (bf16[384,1024]{1,0:T(8,128)(2,1)}, bf16[384,1024]{1,0:T(8,128)(2,1)S(1)}, u32[]{:S(2)}, u32[]{:S(2)}) collective-permute-start(bf16[384,1024]{1,0:T(8,128)(2,1)} %bitcast.49), channel_id=1, source_target_pairs={{0,1},{1,2},{2,3},{3,0},{4,5},{5,6},{6,7},{7,4},{8,9},{9,10},{10,1... | collective-permute-start | bytes 2359304 | tf_op jit(solution)/shard_map/ppermute | solution.py:51
  2.8 19.7 %collective-permute-start.2 = (bf16[384,1024]{1,0:T(8,128)(2,1)}, bf16[384,1024]{1,0:T(8,128)(2,1)S(1)}, u32[]{:S(2)}, u32[]{:S(2)}) collective-permute-start(bf16[384,1024]{1,0:T(8,128)(2,1)} %bitcast.50), channel_id=1, source_target_pairs={{0,3},{1,0},{2,1},{3,2},{4,7},{5,4},{6,5},{7,6},{8,11},{9,8},{10,9... | collective-permute-start | bytes 2359304 | tf_op jit(solution)/shard_map/ppermute | solution.py:51
  5.3 17.2 %collective-permute-start = (bf16[512,256]{1,0:T(8,128)(2,1)S(1)}, bf16[512,256]{1,0:T(8,128)(2,1)S(1)}, u32[]{:S(2)}, u32[]{:S(2)}) collective-permute-start(bf16[512,256]{1,0:T(8,128)(2,1)S(1)} %constant_dynamic-slice_fusion), channel_id=1, source_target_pairs={{0,36},{1,37},{2,38},{3,39},{4,32},{5,33},{6,34},{7,35},{8,44},{9,... | collective-permute-start | bytes 786440 | tf_op jit(solution)/shard_map/ppermute | solution.py:51
  16.9 4.5 %copy-start.10 = (s32[64]{0:T(128)S(1)}, s32[64]{0:T(128)}, u32[]{:S(2)}) copy-start(s32[64]{0:T(128)} %param.14) | copy-start | bytes 772
  16.9 4.5 %copy-start.11 = (s32[24]{0:T(128)S(1)}, s32[24]{0:T(128)}, u32[]{:S(2)}) copy-start(s32[24]{0:T(128)} %param.15) | copy-start | bytes 292
  16.9 4.7 %copy-start.12 = (s32[24]{0:T(128)S(1)}, s32[24]{0:T(128)}, u32[]{:S(2)}) copy-start(s32[24]{0:T(128)} %param.16) | copy-start | bytes 292
  16.9 41.0 %all-to-all-start = ((bf16[4,4,12,16,256]{4,3,2,1,0:T(8,128)(2,1)}), bf16[4,4,12,16,256]{4,3,2,1,0:T(8,128)(2,1)}, u32[]{:S(2)}, u32[]{:S(2)}) async-start(bf16[4,4,12,16,256]{4,3,2,1,0:T(8,128)(2,1)} %pack.1), calls=%async_computation | async-start | bytes 3145728 | tf_op jit(solution)/shard_map/all_to_all | solution.py:431
  21.7 10.7 %copy-start.9 = (bf16[8192]{0:T(1024)(128)(2,1)S(1)}, bf16[8192]{0:T(1024)(128)(2,1)}, u32[]{:S(2)}) copy-start(bf16[8192]{0:T(1024)(128)(2,1)} %param.18) | copy-start | bytes 49156
  22.6 7.1 %copy-start.5 = (bf16[384,1024]{1,0:T(8,128)(2,1)}, bf16[384,1024]{1,0:T(8,128)(2,1)S(1)}, u32[]{:S(2)}) copy-start(bf16[384,1024]{1,0:T(8,128)(2,1)S(1)} %collective-permute-done.1.refs_1_) | copy-start | bytes 2359300
  22.6 7.1 %copy-start.6 = (bf16[384,1024]{1,0:T(8,128)(2,1)}, bf16[384,1024]{1,0:T(8,128)(2,1)S(1)}, u32[]{:S(2)}) copy-start(bf16[384,1024]{1,0:T(8,128)(2,1)S(1)} %collective-permute-done.2.refs_2_) | copy-start | bytes 2359300
  22.6 11.5 %collective-permute-start.4 = (bf16[528,256]{1,0:T(8,128)(2,1)S(1)}, bf16[528,256]{1,0:T(8,128)(2,1)S(1)}, u32[]{:S(2)}, u32[]{:S(2)}) collective-permute-start(bf16[528,256]{1,0:T(8,128)(2,1)S(1)} %get-tuple-element.41), channel_id=1, source_target_pairs={{0,128},{1,129},{2,130},{3,131},{4,132},{5,133},{6,134},{7,135},{8... | collective-permute-start | bytes 811016 | tf_op jit(solution)/shard_map/ppermute | solution.py:51
  25.5 13.0 %collective-permute-start.5 = (bf16[528,256]{1,0:T(8,128)(2,1)S(1)}, bf16[528,256]{1,0:T(8,128)(2,1)S(1)}, u32[]{:S(2)}, u32[]{:S(2)}) collective-permute-start(bf16[528,256]{1,0:T(8,128)(2,1)S(1)} %get-tuple-element.41), channel_id=1, source_target_pairs={{0,64},{1,65},{2,66},{3,67},{4,68},{5,69},{6,70},{7,71},{8,72},{9,... | collective-permute-start | bytes 811016 | tf_op jit(solution)/shard_map/ppermute | solution.py:51
  25.8 12.6 %collective-permute-start.3 = (bf16[528,256]{1,0:T(8,128)(2,1)S(1)}, bf16[528,256]{1,0:T(8,128)(2,1)S(1)}, u32[]{:S(2)}, u32[]{:S(2)}) collective-permute-start(bf16[528,256]{1,0:T(8,128)(2,1)S(1)} %get-tuple-element.41), channel_id=1, source_target_pairs={{0,192},{1,193},{2,194},{3,195},{4,196},{5,197},{6,198},{7,199},{8... | collective-permute-start | bytes 811016 | tf_op jit(solution)/shard_map/ppermute | solution.py:51
  28.9 10.2 %collective-permute-start.6 = (bf16[192,1024]{1,0:T(8,128)(2,1)}, bf16[192,1024]{1,0:T(8,128)(2,1)S(1)}, u32[]{:S(2)}, u32[]{:S(2)}) collective-permute-start(bf16[192,1024]{1,0:T(8,128)(2,1)} %slice.42), channel_id=1, source_target_pairs={{0,1},{1,2},{2,3},{3,0},{4,5},{5,6},{6,7},{7,4},{8,9},{9,10},{10,1... | collective-permute-start | bytes 1179656 | tf_op jit(solution)/shard_map/ppermute | solution.py:51
  29.7 9.4 %collective-permute-start.7 = (bf16[192,1024]{1,0:T(8,128)(2,1)}, bf16[192,1024]{1,0:T(8,128)(2,1)}, u32[]{:S(2)}, u32[]{:S(2)}) collective-permute-start(bf16[192,1024]{1,0:T(8,128)(2,1)} %slice.43), channel_id=1, source_target_pairs={{0,3},{1,0},{2,1},{3,2},{4,7},{5,4},{6,5},{7,6},{8,11},{9,8},{10,9... | collective-permute-start | bytes 1179656 | tf_op jit(solution)/shard_map/ppermute | solution.py:51
  38.4 3.8 %copy-start.8 = (bf16[64,2,256]{2,1,0:T(2,128)(2,1)S(1)}, bf16[64,2,256]{2,1,0:T(2,128)(2,1)}, u32[]{:S(2)}) copy-start(bf16[64,2,256]{2,1,0:T(2,128)(2,1)} %param.11) | copy-start | bytes 196612
  38.6 5.9 %copy-start.4 = (bf16[4,528,256]{2,1,0:T(8,128)(2,1)}, bf16[4,528,256]{2,1,0:T(8,128)(2,1)S(1)}, u32[]{:S(2)}) copy-start(bf16[4,528,256]{2,1,0:T(8,128)(2,1)S(1)} %pad_maximum_fusion.mine_ref) | copy-start | bytes 3244036
  39.1 3.0 %copy-start.7 = (bf16[192,1024]{1,0:T(8,128)(2,1)}, bf16[192,1024]{1,0:T(8,128)(2,1)S(1)}, u32[]{:S(2)}) copy-start(bf16[192,1024]{1,0:T(8,128)(2,1)S(1)} %collective-permute-done.6.refs_3_) | copy-start | bytes 1179652
  39.1 5.4 %collective-permute-start.8 = (bf16[4,528,256]{2,1,0:T(8,128)(2,1)S(1)}, bf16[4,528,256]{2,1,0:T(8,128)(2,1)}, u32[]{:S(2)}, u32[]{:S(2)}) collective-permute-start(bf16[4,528,256]{2,1,0:T(8,128)(2,1)S(1)} %pad_maximum_fusion.mine_ref), channel_id=1, source_target_pairs={{0,8},{1,9},{2,10},{3,11},{4,12},{5,13},{6,14},{7,15},{8,0},{9,1},... | collective-permute-start | bytes 3244040 | tf_op jit(solution)/shard_map/ppermute | solution.py:51
  58.0 6.7 %copy-start.13 = (bf16[400,256]{1,0:T(8,128)(2,1)S(1)}, bf16[400,256]{1,0:T(8,128)(2,1)}, u32[]{:S(2)}) copy-start(bf16[400,256]{1,0:T(8,128)(2,1)} %get-tuple-element.26) | copy-start | bytes 614404
  58.0 7.2 %copy-start.3 = (s32[629]{0:T(1024)S(1)}, s32[629]{0:T(1024)}, u32[]{:S(2)}) copy-start(s32[629]{0:T(1024)} %concatenate.13.meta_ref) | copy-start | bytes 7552
  60.4 23.8 %collective-permute-start.14 = (bf16[4,12,16,256]{3,2,1,0:T(8,128)(2,1)}, bf16[4,12,16,256]{3,2,1,0:T(8,128)(2,1)S(1)}, u32[]{:S(2)}, u32[]{:S(2)}) collective-permute-start(bf16[4,12,16,256]{3,2,1,0:T(8,128)(2,1)} %get-tuple-element.36), channel_id=1, source_target_pairs={{0,192},{1,193},{2,194},{3,195},{4,196},{5,197},{6,198},{7,199},{8... | collective-permute-start | bytes 1179656 | tf_op jit(solution)/shard_map/ppermute | solution.py:51
  63.6 20.7 %collective-permute-start.13 = (bf16[4,12,16,256]{3,2,1,0:T(8,128)(2,1)}, bf16[4,12,16,256]{3,2,1,0:T(8,128)(2,1)S(1)}, u32[]{:S(2)}, u32[]{:S(2)}) collective-permute-start(bf16[4,12,16,256]{3,2,1,0:T(8,128)(2,1)} %get-tuple-element.37), channel_id=1, source_target_pairs={{0,128},{1,129},{2,130},{3,131},{4,132},{5,133},{6,134},{7,135},{8... | collective-permute-start | bytes 1179656 | tf_op jit(solution)/shard_map/ppermute | solution.py:51
  64.1 20.7 %collective-permute-start.12 = (bf16[4,12,16,256]{3,2,1,0:T(8,128)(2,1)}, bf16[4,12,16,256]{3,2,1,0:T(8,128)(2,1)S(1)}, u32[]{:S(2)}, u32[]{:S(2)}) collective-permute-start(bf16[4,12,16,256]{3,2,1,0:T(8,128)(2,1)} %get-tuple-element.38), channel_id=1, source_target_pairs={{0,64},{1,65},{2,66},{3,67},{4,68},{5,69},{6,70},{7,71},{8,72},{9,... | collective-permute-start | bytes 1179656 | tf_op jit(solution)/shard_map/ppermute | solution.py:51
  64.7 10.7 %collective-permute-start.9 = (bf16[400,256]{1,0:T(8,128)(2,1)S(1)}, bf16[400,256]{1,0:T(8,128)(2,1)S(1)}, u32[]{:S(2)}, u32[]{:S(2)}) collective-permute-start(bf16[400,256]{1,0:T(8,128)(2,1)S(1)} %copy-done.13), channel_id=1, source_target_pairs={{0,4},{1,5},{2,6},{3,7},{4,0},{5,1},{6,2},{7,3},{8,12},{9,13},{10,... | collective-permute-start | bytes 614408 | tf_op jit(solution)/shard_map/ppermute | solution.py:51
  65.1 2.2 %copy-start = (bf16[512,16,256]{2,1,0:T(8,128)(2,1)S(1)}, bf16[512,16,256]{2,1,0:T(8,128)(2,1)}, u32[]{:S(2)}) copy-start(bf16[512,16,256]{2,1,0:T(8,128)(2,1)} %cache_ref.3) | copy-start | bytes 12582916
  67.3 8.1 %copy-start.2 = (f32[384,128]{1,0:T(8,128)S(1)}, f32[384,128]{1,0:T(8,128)}, u32[]{:S(2)}) copy-start(f32[384,128]{1,0:T(8,128)} %get-tuple-element.31.sq_ref) | copy-start | bytes 589828
  72.5 3.0 %copy-start.1 = (f32[384,256]{1,0:T(8,128)S(1)}, f32[384,256]{1,0:T(8,128)}, u32[]{:S(2)}) copy-start(f32[384,256]{1,0:T(8,128)} %get-tuple-element.30.own_ref) | copy-start | bytes 1179652
  77.1 24.1 %all-to-all-start.1 = ((bf16[32,32,256]{2,1,0:T(8,128)(2,1)}), bf16[32,32,256]{2,1,0:T(8,128)(2,1)S(1)}, u32[]{:S(2)}, u32[]{:S(2)}) async-start(bf16[32,32,256]{2,1,0:T(8,128)(2,1)} %bitcast.25), calls=%async_computation.1 | async-start | bytes 1048576 | tf_op jit(solution)/shard_map/all_to_all | solution.py:371
  85.7 13.3 %collective-permute-start.15 = (bf16[4,4,6,16,256]{4,3,2,1,0:T(8,128)(2,1)}, bf16[4,4,6,16,256]{4,3,2,1,0:T(8,128)(2,1)S(1)}, u32[]{:S(2)}, u32[]{:S(2)}) collective-permute-start(bf16[4,4,6,16,256]{4,3,2,1,0:T(8,128)(2,1)} %pad_maximum_fusion.1), channel_id=1, source_target_pairs={{0,8},{1,9},{2,10},{3,11},{4,12},{5,13},{6,14},{7,15},{8,0},{9,1},... | collective-permute-start | bytes 2359304 | tf_op jit(solution)/shard_map/ppermute | solution.py:51
  86.2 6.8 %collective-permute-start.10 = (bf16[2,4,2,24]{3,2,1,0:T(2,128)(2,1)S(1)}, bf16[2,4,2,24]{3,2,1,0:T(2,128)(2,1)S(1)}, u32[]{:S(2)}, u32[]{:S(2)}) collective-permute-start(bf16[2,4,2,24]{3,2,1,0:T(2,128)(2,1)S(1)} %pad_maximum_fusion.6), channel_id=1, source_target_pairs={{0,16},{1,17},{2,18},{3,19},{4,20},{5,21},{6,22},{7,23},{8,24},{9,... | collective-permute-start | bytes 2312 | tf_op jit(solution)/shard_map/ppermute | solution.py:51
  93.0 5.4 %collective-permute-start.11 = (bf16[2,2,4,2,24]{4,3,2,1,0:T(2,128)(2,1)S(1)}, bf16[2,2,4,2,24]{4,3,2,1,0:T(2,128)(2,1)S(1)}, u32[]{:S(2)}, u32[]{:S(2)}) collective-permute-start(bf16[2,2,4,2,24]{4,3,2,1,0:T(2,128)(2,1)S(1)} %pad_maximum_fusion.5), channel_id=1, source_target_pairs={{0,32},{1,33},{2,34},{3,35},{4,36},{5,37},{6,38},{7,39},{8,40},{9,... | collective-permute-start | bytes 4616 | tf_op jit(solution)/shard_map/ppermute | solution.py:51

commit v4 on v3

--- a/solution.py
+++ b/solution.py
@@ -321,9 +321,16 @@
 
 
 def assemble_kernel(row_total, meta_ref, counts_ref, *refs):
-    kept_refs, other_ref, dirty_ref, out_ref = refs[:NX], refs[NX], refs[NX + 1], refs[NX + 2]
+    kept_refs, other_ref, dirty_ref, target_ref, out_ref, sems = refs[:NX], *refs[NX:]
     place_at = meta_at(row_total)[3]
     x_at, z_at, core_at = (meta_ref[place_at + i] for i in range(3))
+
+    chunk = NZL * NCORE * MAXP
+
+    def leave(d):
+        x = (x_at - d + NX) % NX
+        pages = pl.ds(x * chunk, chunk)
+        return pltpu.make_async_copy(out_ref.at[pages], target_ref.at[pages], sems.at[d])
 
     for d in range(NX):
         x = (x_at - d + NX) % NX
@@ -352,6 +359,9 @@
                 return carry
 
             lax.fori_loop(0, NZL, one, 0, unroll=2)
+        leave(d).start()
+    for d in range(NX):
+        leave(d).wait()
 
 
 def assemble(row_total, meta, counts, kept, other, dirty, members):
@@ -360,7 +370,11 @@
         functools.partial(assemble_kernel, row_total),
         out_shape=jax.ShapeDtypeStruct((members * MAXP, PAGE, lanes), dirty.dtype),
         in_specs=[SMEM, SMEM] + [VMEM] * (NX + 2),
-        out_specs=VMEM,
+        out_specs=HBM,
+        scratch_shapes=[
+            pltpu.VMEM((members * MAXP, PAGE, lanes), dirty.dtype),
+            pltpu.SemaphoreType.DMA((NX,)),
+        ],
         compiler_params=params(14),
         name="assemble",
     )(meta, counts, *kept, other, dirty)
@@ -456,24 +470,26 @@
         other_slices,
         (hidden, from_below, from_above, across_top, across_bottom),
     )
-    outgoing, by_z = lax.optimization_barrier((outgoing, by_z))
     got = send(outgoing, dzh=1)
 
-    by_x = [by_z[:, d] for d in range(NX)]
-    by_x = [by_x[0]] + [send(by_x[d], dx=d) for d in range(1, NX)]
     heads = queries.shape[-1] // HD
     q = queries.reshape(row_count, 2 * heads, HD)
     fresh = jnp.pad(new_kv, ((0, 0), (0, PAGE - 2), (0, 0)))
     q, fresh, _ = lax.optimization_barrier((q, fresh, outgoing))
     decoded = attend(0, row_count, q, fresh, kv_cache, meta)
     decoded = decoded.reshape(row_count, 2, heads * HD)
-    got, turn, decoded = lax.optimization_barrier((got, turn, decoded))
-    made = combine(features, row_count, meta, own, squares, got, turn, members)
-
+    by_z, decoded = lax.optimization_barrier((by_z, decoded))
     lines = slice(slice_rows, slice_rows + 2)
     heard = jnp.stack([slices[:, lines, :MIG], other_slices[:, lines, :MIG]])
-    heard, _ = lax.optimization_barrier((heard, made))
-    heard = jnp.stack([heard, send(heard, zl_xor=1)])
+    heard, _ = lax.optimization_barrier((heard, outgoing))
+    heard_next = send(heard, zl_xor=1)
+    by_x = [by_z[:, d] for d in range(NX)]
+    got, *by_x = lax.optimization_barrier((got, *by_x))
+    by_x = [by_x[0]] + [send(by_x[d], dx=d) for d in range(1, NX)]
+    got, turn, heard_next = lax.optimization_barrier((got, turn, heard_next))
+    made = combine(features, row_count, meta, own, squares, got, turn, members)
+
+    heard = jnp.stack([heard, heard_next])
     heard = jnp.concatenate([heard, send(heard, zl_xor=2)])
     aimed_here = heard[..., 0, :] == inst.astype(BF16)
     counts = jnp.sum(
@@ -484,6 +500,7 @@
     ).astype(jnp.int32)
     dirty = exchange(made, members, 2)
 
+    counts, *by_x = lax.optimization_barrier((counts, *by_x))
     other_kept = send(jnp.stack([part[:, STORED:] for part in by_x]), dcore=1)
     mig_kv = assemble(
         row_count, meta, counts.reshape(-1), by_x, other_kept, dirty, members

time: 105 us -> 101 us (0.962)
  waiting for transfers between devices: 26.7 us -> 18.9 us
  starting transfers between devices: 42.1 us -> 48.1 us
  local copies, waits for them, and re-layouts: 13.2 us -> 10.9 us
    all_to_all x1, waiting for transfers between devices: 7.68 us -> 0.01 us  [per_device(): lax.all_to_all(packed, 'inst', split_axis=0, concat_axis=0, axis_index_gr...]
    ppermute x16, starting transfers between devices: 30.5 us -> 38.1 us  [send(): return lax.ppermute(value, AXES, moves(**by))]
    unnamed x29 -> x27, local copies, waits for them, and re-layouts: 3.02 us -> 0.83 us
    all_to_all x1, starting transfers between devices: 7.14 us -> 5.47 us  [exchange(): lax.all_to_all(pages.reshape(members, each * PAGE, lanes), 'inst', split_...]
  transfers between devices with their start and end apart: 18 -> 18, of which waited for: 10 -> 6; matrix products, arithmetic and copies ran while one was open for 11% -> 13% of each run, Pallas kernels for 15% -> 16%
where the time goes in v4:
time: 101 us; the launch traced here: 100 us
  starting transfers between devices  48.1 us (48%)
  Pallas kernels  19 us (19%)
  waiting for transfers between devices  18.9 us (19%)
  local copies, waits for them, and re-layouts  10.9 us (11%)
  other arithmetic  2.49 us (2%)
  between operations  1.07 us (1%)
    ppermute x16, starting transfers between devices, send(): return lax.ppermute(value, AXES, moves(**by))  38.1 us
    ppermute x16, waiting for transfers between devices, send(): return lax.ppermute(value, AXES, moves(**by))  16.5 us
    pallas_call x1, Pallas kernels, project(): pl.pallas_call(functools.partial(project_kernel, row_total), out_shape=(j...  6.14 us
    all_to_all x1, starting transfers between devices, exchange(): lax.all_to_all(pages.reshape(members, each * PAGE, lanes), 'inst', split_...  5.47 us
    pallas_call x1, Pallas kernels, attend(): pl.pallas_call(functools.partial(attend_kernel, start, row_total), out_sh...  5.12 us
    all_to_all x1, starting transfers between devices, per_device(): lax.all_to_all(packed, 'inst', split_axis=0, concat_axis=0, axis_index_gr...  4.48 us
    pallas_call x1, Pallas kernels, pack(): pl.pallas_call(functools.partial(pack_kernel, row_count), out_shape=jax.S...  3.21 us
    pallas_call x1, Pallas kernels, assemble(): pl.pallas_call(functools.partial(assemble_kernel, row_total), out_shape=j...  2.86 us
  transfers between devices with their start and end apart: 18, of which 6 were waited for; matrix products, arithmetic and copies ran while one was open for 13% of the time, Pallas kernels for 16%

profile of v4, /device:TPU:1, one launch (start us, length us, event | category | flops | bytes accessed | tf_op | source)
XLA Modules:
  0.0 100.4 jit_solution(2785476344585341099)
XLA Ops:
  0.6 2.2 %collective-permute-start.1 = (bf16[384,1024]{1,0:T(8,128)(2,1)}, bf16[384,1024]{1,0:T(8,128)(2,1)S(1)}, u32[]{:S(2)}, u32[]{:S(2)}) collective-permute-start(bf16[384,1024]{1,0:T(8,128)(2,1)} %bitcast.49), channel_id=1, source_target_pairs={{0,1},{1,2},{2,3},{3,0},{4,5},{5,6},{6,7},{7,4},{8,9},{9,10},{10,1... | collective-permute-start | bytes 2359304 | tf_op jit(solution)/shard_map/ppermute | solution.py:51
  2.8 1.5 %collective-permute-start.2 = (bf16[384,1024]{1,0:T(8,128)(2,1)}, bf16[384,1024]{1,0:T(8,128)(2,1)S(1)}, u32[]{:S(2)}, u32[]{:S(2)}) collective-permute-start(bf16[384,1024]{1,0:T(8,128)(2,1)} %bitcast.50), channel_id=1, source_target_pairs={{0,3},{1,0},{2,1},{3,2},{4,7},{5,4},{6,5},{7,6},{8,11},{9,8},{10,9... | collective-permute-start | bytes 2359304 | tf_op jit(solution)/shard_map/ppermute | solution.py:51
  4.4 1.0 constant_dynamic-slice_fusion
  5.3 6.1 %collective-permute-start = (bf16[512,256]{1,0:T(8,128)(2,1)S(1)}, bf16[512,256]{1,0:T(8,128)(2,1)S(1)}, u32[]{:S(2)}, u32[]{:S(2)}) collective-permute-start(bf16[512,256]{1,0:T(8,128)(2,1)S(1)} %constant_dynamic-slice_fusion), channel_id=1, source_target_pairs={{0,36},{1,37},{2,38},{3,39},{4,32},{5,33},{6,34},{7,35},{8,44},{9,... | collective-permute-start | bytes 786440 | tf_op jit(solution)/shard_map/ppermute | solution.py:51
  12.3 1.4 %concatenate.13.meta_ref = s32[629]{0:T(1024)} concatenate(s32[512]{0:T(512)S(1)} %reshape.135, s32[64]{0:T(128)} %param.14, s32[24]{0:T(128)} %param.15, s32[24]{0:T(128)} %param.16, s32[1]{0:T(128)} %bitcast, s32[1]{0:T(128)} %bitcast.1, s32[1]{0:T(128)} %bitcast.2, s32[1]{0:T(128)} %bitcast.3, s32[1]{0:T(128)} %bitcast.4), dimensions={0} | concatenate | bytes 5032 | tf_op jit(solution)/shard_map/concatenate | solution.py:65
  13.7 3.2 %pack.1 = bf16[4,4,12,16,256]{4,3,2,1,0:T(8,128)(2,1)} custom-call(s32[629]{0:T(1024)} %concatenate.13.meta_ref, bf16[512,16,256]{2,1,0:T(8,128)(2,1)} %cache_ref.3), custom_call_target="tpu_custom_call" | custom-call | bytes 4194304 | tf_op jit(solution)/shard_map/pack/pallas_call | solution.py:113
  16.9 4.5 %all-to-all-start = ((bf16[4,4,12,16,256]{4,3,2,1,0:T(8,128)(2,1)}), bf16[4,4,12,16,256]{4,3,2,1,0:T(8,128)(2,1)}, u32[]{:S(2)}, u32[]{:S(2)}) async-start(bf16[4,4,12,16,256]{4,3,2,1,0:T(8,128)(2,1)} %pack.1), calls=%async_computation | async-start | bytes 3145728 | tf_op jit(solution)/shard_map/all_to_all | solution.py:445
  21.7 0.9 collective-permute-done
  22.6 2.8 %collective-permute-start.4 = (bf16[528,256]{1,0:T(8,128)(2,1)S(1)}, bf16[528,256]{1,0:T(8,128)(2,1)S(1)}, u32[]{:S(2)}, u32[]{:S(2)}) collective-permute-start(bf16[528,256]{1,0:T(8,128)(2,1)S(1)} %get-tuple-element.61), channel_id=1, source_target_pairs={{0,128},{1,129},{2,130},{3,131},{4,132},{5,133},{6,134},{7,135},{8... | collective-permute-start | bytes 811016 | tf_op jit(solution)/shard_map/ppermute | solution.py:51
  25.8 2.4 %collective-permute-start.3 = (bf16[528,256]{1,0:T(8,128)(2,1)S(1)}, bf16[528,256]{1,0:T(8,128)(2,1)S(1)}, u32[]{:S(2)}, u32[]{:S(2)}) collective-permute-start(bf16[528,256]{1,0:T(8,128)(2,1)S(1)} %get-tuple-element.61), channel_id=1, source_target_pairs={{0,192},{1,193},{2,194},{3,195},{4,196},{5,197},{6,198},{7,199},{8... | collective-permute-start | bytes 811016 | tf_op jit(solution)/shard_map/ppermute | solution.py:51
  28.9 0.8 slice.43
  29.7 2.7 %collective-permute-start.7 = (bf16[192,1024]{1,0:T(8,128)(2,1)}, bf16[192,1024]{1,0:T(8,128)(2,1)}, u32[]{:S(2)}, u32[]{:S(2)}) collective-permute-start(bf16[192,1024]{1,0:T(8,128)(2,1)} %slice.43), channel_id=1, source_target_pairs={{0,3},{1,0},{2,1},{3,2},{4,7},{5,4},{6,5},{7,6},{8,11},{9,8},{10,9... | collective-permute-start | bytes 1179656 | tf_op jit(solution)/shard_map/ppermute | solution.py:51
  33.0 1.1 %reshape.136.q_ref = bf16[64,16,128]{2,1,0:T(8,128)(2,1)S(1)} reshape(bf16[64,2,1024]{2,1,0:T(2,128)(2,1)} %param.10) | data formatting | bytes 524288 | tf_op jit(solution)/shard_map/reshape | solution.py:476
  34.1 4.3 %collective-permute-done.5 = bf16[528,256]{1,0:T(8,128)(2,1)S(1)} collective-permute-done((bf16[528,256]{1,0:T(8,128)(2,1)S(1)}, bf16[528,256]{1,0:T(8,128)(2,1)S(1)}, u32[]{:S(2)}, u32[]{:S(2)}) %collective-permute-start.5) | collective-permute-done | bytes 270368 | tf_op jit(solution)/shard_map/ppermute | solution.py:51
  39.1 2.9 %collective-permute-start.8 = (bf16[4,528,256]{2,1,0:T(8,128)(2,1)S(1)}, bf16[4,528,256]{2,1,0:T(8,128)(2,1)}, u32[]{:S(2)}, u32[]{:S(2)}) collective-permute-start(bf16[4,528,256]{2,1,0:T(8,128)(2,1)S(1)} %pad_maximum_fusion.mine_ref), channel_id=1, source_target_pairs={{0,8},{1,9},{2,10},{3,11},{4,12},{5,13},{6,14},{7,15},{8,0},{9,1},... | collective-permute-start | bytes 3244040 | tf_op jit(solution)/shard_map/ppermute | solution.py:51
  43.2 1.3 %collective-permute-done.8.other_ref = bf16[4,528,256]{2,1,0:T(8,128)(2,1)} collective-permute-done((bf16[4,528,256]{2,1,0:T(8,128)(2,1)S(1)}, bf16[4,528,256]{2,1,0:T(8,128)(2,1)}, u32[]{:S(2)}, u32[]{:S(2)}) %collective-permute-start.8) | collective-permute-done | bytes 1081376 | tf_op jit(solution)/shard_map/ppermute | solution.py:51
  44.5 6.1 %project.1 = (f32[384,256]{1,0:T(8,128)}, bf16[400,256]{1,0:T(8,128)(2,1)}, f32[384,128]{1,0:T(8,128)}) custom-call(s32[629]{0:T(1024)} %concatenate.13.meta_ref, f32[8,1024]{1,0:T(8,128)} %reshape.145.gain_ref, bf16[8192,256]{1,0:T(8,128)(2,1)} %own_ref.1, bf16[4,528,256]{2,1,0:T(8,128)(2,1)} %copy-done.4, ...), custom_call_target="tpu_custom_call" | custom-call | flops 1610612736 | bytes 12582912 | tf_op jit(solution)/shard_map/project/pallas_call | solution.py:258
  50.7 6.5 %collective-permute-start.9 = (bf16[400,256]{1,0:T(8,128)(2,1)}, bf16[400,256]{1,0:T(8,128)(2,1)S(1)}, u32[]{:S(2)}, u32[]{:S(2)}) collective-permute-start(bf16[400,256]{1,0:T(8,128)(2,1)} %get-tuple-element.35), channel_id=1, source_target_pairs={{0,4},{1,5},{2,6},{3,7},{4,0},{5,1},{6,2},{7,3},{8,12},{9,13},{10,... | collective-permute-start | bytes 614408 | tf_op jit(solution)/shard_map/ppermute | solution.py:51
  57.9 1.0 %collective-permute-start.10 = (bf16[2,4,2,24]{3,2,1,0:T(2,128)(2,1)S(1)}, bf16[2,4,2,24]{3,2,1,0:T(2,128)(2,1)S(1)}, u32[]{:S(2)}, u32[]{:S(2)}) collective-permute-start(bf16[2,4,2,24]{3,2,1,0:T(2,128)(2,1)S(1)} %pad_maximum_fusion.6), channel_id=1, source_target_pairs={{0,16},{1,17},{2,18},{3,19},{4,20},{5,21},{6,22},{7,23},{8,24},{9,... | collective-permute-start | bytes 2312 | tf_op jit(solution)/shard_map/ppermute | solution.py:51
  58.9 5.1 %attend.1 = bf16[64,16,128]{2,1,0:T(8,128)(2,1)S(1)} custom-call(s32[629]{0:T(1024)S(1)} %copy-done.3, bf16[64,16,128]{2,1,0:T(8,128)(2,1)S(1)} %reshape.136.q_ref, bf16[64,16,256]{2,1,0:T(8,128)(2,1)S(1)} %pad.8.new_ref, bf16[512,16,256]{2,1,0:T(8,128)(2,1)S(1)} %copy-done), custom_call_target="tpu_custom_call" | custom-call | flops 75497472 | bytes 33554432 | tf_op jit(solution)/shard_map/attend/pallas_call | solution.py:172
  64.8 2.3 %slice_bitcast_fusion = (bf16[4,12,16,256]{3,2,1,0:T(8,128)(2,1)S(1)}, bf16[4,12,16,256]{3,2,1,0:T(8,128)(2,1)S(1)}, bf16[4,12,16,256]{3,2,1,0:T(8,128)(2,1)}, bf16[4,12,16,256]{3,2,1,0:T(8,128)(2,1)S(1)}) fusion(bf16[4,4,12,16,256]{4,3,2,1,0:T(8,128)(2,1)} %all-to-all-done), kind=kLoop, calls=%fused_computation.2 | loop fusion | bytes 3145728 | tf_op jit(solution)/shard_map/squeeze | solution.py:486
  67.0 1.6 %collective-permute-start.12 = (bf16[4,12,16,256]{3,2,1,0:T(8,128)(2,1)}, bf16[4,12,16,256]{3,2,1,0:T(8,128)(2,1)S(1)}, u32[]{:S(2)}, u32[]{:S(2)}) collective-permute-start(bf16[4,12,16,256]{3,2,1,0:T(8,128)(2,1)} %get-tuple-element.44), channel_id=1, source_target_pairs={{0,64},{1,65},{2,66},{3,67},{4,68},{5,69},{6,70},{7,71},{8,72},{9,... | collective-permute-start | bytes 1179656 | tf_op jit(solution)/shard_map/ppermute | solution.py:51
  68.6 2.4 %collective-permute-start.13 = (bf16[4,12,16,256]{3,2,1,0:T(8,128)(2,1)S(1)}, bf16[4,12,16,256]{3,2,1,0:T(8,128)(2,1)S(1)}, u32[]{:S(2)}, u32[]{:S(2)}) collective-permute-start(bf16[4,12,16,256]{3,2,1,0:T(8,128)(2,1)S(1)} %get-tuple-element.45), channel_id=1, source_target_pairs={{0,128},{1,129},{2,130},{3,131},{4,132},{5,133},{6,134},{7,135},{8... | collective-permute-start | bytes 1179656 | tf_op jit(solution)/shard_map/ppermute | solution.py:51
  71.0 1.2 %collective-permute-start.14 = (bf16[4,12,16,256]{3,2,1,0:T(8,128)(2,1)S(1)}, bf16[4,12,16,256]{3,2,1,0:T(8,128)(2,1)S(1)}, u32[]{:S(2)}, u32[]{:S(2)}) collective-permute-start(bf16[4,12,16,256]{3,2,1,0:T(8,128)(2,1)S(1)} %get-tuple-element.46), channel_id=1, source_target_pairs={{0,192},{1,193},{2,194},{3,195},{4,196},{5,197},{6,198},{7,199},{8... | collective-permute-start | bytes 1179656 | tf_op jit(solution)/shard_map/ppermute | solution.py:51
  72.2 1.2 %collective-permute-start.11 = (bf16[2,2,4,2,24]{4,3,2,1,0:T(2,128)(2,1)S(1)}, bf16[2,2,4,2,24]{4,3,2,1,0:T(2,128)(2,1)S(1)}, u32[]{:S(2)}, u32[]{:S(2)}) collective-permute-start(bf16[2,2,4,2,24]{4,3,2,1,0:T(2,128)(2,1)S(1)} %pad_maximum_fusion.5), channel_id=1, source_target_pairs={{0,32},{1,33},{2,34},{3,35},{4,36},{5,37},{6,38},{7,39},{8,40},{9,... | collective-permute-start | bytes 4616 | tf_op jit(solution)/shard_map/ppermute | solution.py:51
  73.5 1.6 %combine.1 = bf16[64,16,256]{2,1,0:T(8,128)(2,1)} custom-call(s32[629]{0:T(1024)S(1)} %copy-done.3, f32[384,256]{1,0:T(8,128)S(1)} %copy-done.1, f32[384,128]{1,0:T(8,128)S(1)} %copy-done.2, bf16[400,256]{1,0:T(8,128)(2,1)S(1)} %collective-permute-done.9.got_ref, f32[384,128]{1,0:T(8,128)S(1)} %pad_maximum_fusion.3.turn_ref), custom_call_target="tpu_custom_call" | custom-call | tf_op jit(solution)/shard_map/combine/pallas_call | solution.py:313
  75.1 5.5 %all-to-all-start.1 = ((bf16[32,32,256]{2,1,0:T(8,128)(2,1)}), bf16[32,32,256]{2,1,0:T(8,128)(2,1)S(1)}, u32[]{:S(2)}, u32[]{:S(2)}) async-start(bf16[32,32,256]{2,1,0:T(8,128)(2,1)} %bitcast.25), calls=%async_computation.1 | async-start | bytes 1048576 | tf_op jit(solution)/shard_map/all_to_all | solution.py:385
  80.9 9.5 %collective-permute-done.13.refs_2_ = bf16[4,12,16,256]{3,2,1,0:T(8,128)(2,1)S(1)} collective-permute-done((bf16[4,12,16,256]{3,2,1,0:T(8,128)(2,1)S(1)}, bf16[4,12,16,256]{3,2,1,0:T(8,128)(2,1)S(1)}, u32[]{:S(2)}, u32[]{:S(2)}) %collective-permute-start.13) | collective-permute-done | bytes 393248 | tf_op jit(solution)/shard_map/ppermute | solution.py:51
  90.5 1.0 pad_maximum_fusion.1
  91.4 3.3 %collective-permute-start.15 = (bf16[4,4,6,16,256]{4,3,2,1,0:T(8,128)(2,1)}, bf16[4,4,6,16,256]{4,3,2,1,0:T(8,128)(2,1)S(1)}, u32[]{:S(2)}, u32[]{:S(2)}) collective-permute-start(bf16[4,4,6,16,256]{4,3,2,1,0:T(8,128)(2,1)} %pad_maximum_fusion.1), channel_id=1, source_target_pairs={{0,8},{1,9},{2,10},{3,11},{4,12},{5,13},{6,14},{7,15},{8,0},{9,1},... | collective-permute-start | bytes 2359304 | tf_op jit(solution)/shard_map/ppermute | solution.py:51
  95.0 2.4 %all-to-all-done.1 = bf16[32,32,256]{2,1,0:T(8,128)(2,1)S(1)} async-done(((bf16[32,32,256]{2,1,0:T(8,128)(2,1)}), bf16[32,32,256]{2,1,0:T(8,128)(2,1)S(1)}, u32[]{:S(2)}, u32[]{:S(2)}) %all-to-all-start.1) | async-done | bytes 524320 | tf_op jit(solution)/shard_map/all_to_all | solution.py:385
  97.4 2.9 %assemble.1 = bf16[256,16,256]{2,1,0:T(8,128)(2,1)} custom-call(s32[629]{0:T(1024)S(1)} %copy-done.3, s32[64]{0:T(128)S(1)} %reshape.141.counts_ref, bf16[4,12,16,256]{3,2,1,0:T(8,128)(2,1)S(1)} %get-tuple-element.48.refs_0_, bf16[4,12,16,256]{3,2,1,0:T(8,128)(2,1)S(1)} %collective-permute-done.12.refs_1_, ...), custom_call_target="tpu_custom_call" | custom-call | tf_op jit(solution)/shard_map/assemble/pallas_call | solution.py:369
  (72 shorter events, 6.8 us)
Async XLA Ops:
  0.6 21.9 %collective-permute-start.1 = (bf16[384,1024]{1,0:T(8,128)(2,1)}, bf16[384,1024]{1,0:T(8,128)(2,1)S(1)}, u32[]{:S(2)}, u32[]{:S(2)}) collective-permute-start(bf16[384,1024]{1,0:T(8,128)(2,1)} %bitcast.49), channel_id=1, source_target_pairs={{0,1},{1,2},{2,3},{3,0},{4,5},{5,6},{6,7},{7,4},{8,9},{9,10},{10,1... | collective-permute-start | bytes 2359304 | tf_op jit(solution)/shard_map/ppermute | solution.py:51
  2.8 19.7 %collective-permute-start.2 = (bf16[384,1024]{1,0:T(8,128)(2,1)}, bf16[384,1024]{1,0:T(8,128)(2,1)S(1)}, u32[]{:S(2)}, u32[]{:S(2)}) collective-permute-start(bf16[384,1024]{1,0:T(8,128)(2,1)} %bitcast.50), channel_id=1, source_target_pairs={{0,3},{1,0},{2,1},{3,2},{4,7},{5,4},{6,5},{7,6},{8,11},{9,8},{10,9... | collective-permute-start | bytes 2359304 | tf_op jit(solution)/shard_map/ppermute | solution.py:51
  5.3 17.2 %collective-permute-start = (bf16[512,256]{1,0:T(8,128)(2,1)S(1)}, bf16[512,256]{1,0:T(8,128)(2,1)S(1)}, u32[]{:S(2)}, u32[]{:S(2)}) collective-permute-start(bf16[512,256]{1,0:T(8,128)(2,1)S(1)} %constant_dynamic-slice_fusion), channel_id=1, source_target_pairs={{0,36},{1,37},{2,38},{3,39},{4,32},{5,33},{6,34},{7,35},{8,44},{9,... | collective-permute-start | bytes 786440 | tf_op jit(solution)/shard_map/ppermute | solution.py:51
  16.9 4.5 %copy-start.10 = (s32[64]{0:T(128)S(1)}, s32[64]{0:T(128)}, u32[]{:S(2)}) copy-start(s32[64]{0:T(128)} %param.14) | copy-start | bytes 772
  16.9 4.5 %copy-start.11 = (s32[24]{0:T(128)S(1)}, s32[24]{0:T(128)}, u32[]{:S(2)}) copy-start(s32[24]{0:T(128)} %param.15) | copy-start | bytes 292
  16.9 4.7 %copy-start.12 = (s32[24]{0:T(128)S(1)}, s32[24]{0:T(128)}, u32[]{:S(2)}) copy-start(s32[24]{0:T(128)} %param.16) | copy-start | bytes 292
  16.9 47.8 %all-to-all-start = ((bf16[4,4,12,16,256]{4,3,2,1,0:T(8,128)(2,1)}), bf16[4,4,12,16,256]{4,3,2,1,0:T(8,128)(2,1)}, u32[]{:S(2)}, u32[]{:S(2)}) async-start(bf16[4,4,12,16,256]{4,3,2,1,0:T(8,128)(2,1)} %pack.1), calls=%async_computation | async-start | bytes 3145728 | tf_op jit(solution)/shard_map/all_to_all | solution.py:445
  21.7 10.7 %copy-start.9 = (bf16[8192]{0:T(1024)(128)(2,1)S(1)}, bf16[8192]{0:T(1024)(128)(2,1)}, u32[]{:S(2)}) copy-start(bf16[8192]{0:T(1024)(128)(2,1)} %param.18) | copy-start | bytes 49156
  22.6 7.1 %copy-start.5 = (bf16[384,1024]{1,0:T(8,128)(2,1)}, bf16[384,1024]{1,0:T(8,128)(2,1)S(1)}, u32[]{:S(2)}) copy-start(bf16[384,1024]{1,0:T(8,128)(2,1)S(1)} %collective-permute-done.1.refs_1_) | copy-start | bytes 2359300
  22.6 7.1 %copy-start.6 = (bf16[384,1024]{1,0:T(8,128)(2,1)}, bf16[384,1024]{1,0:T(8,128)(2,1)S(1)}, u32[]{:S(2)}) copy-start(bf16[384,1024]{1,0:T(8,128)(2,1)S(1)} %collective-permute-done.2.refs_2_) | copy-start | bytes 2359300
  22.6 11.5 %collective-permute-start.4 = (bf16[528,256]{1,0:T(8,128)(2,1)S(1)}, bf16[528,256]{1,0:T(8,128)(2,1)S(1)}, u32[]{:S(2)}, u32[]{:S(2)}) collective-permute-start(bf16[528,256]{1,0:T(8,128)(2,1)S(1)} %get-tuple-element.61), channel_id=1, source_target_pairs={{0,128},{1,129},{2,130},{3,131},{4,132},{5,133},{6,134},{7,135},{8... | collective-permute-start | bytes 811016 | tf_op jit(solution)/shard_map/ppermute | solution.py:51
  25.5 13.0 %collective-permute-start.5 = (bf16[528,256]{1,0:T(8,128)(2,1)S(1)}, bf16[528,256]{1,0:T(8,128)(2,1)S(1)}, u32[]{:S(2)}, u32[]{:S(2)}) collective-permute-start(bf16[528,256]{1,0:T(8,128)(2,1)S(1)} %get-tuple-element.61), channel_id=1, source_target_pairs={{0,64},{1,65},{2,66},{3,67},{4,68},{5,69},{6,70},{7,71},{8,72},{9,... | collective-permute-start | bytes 811016 | tf_op jit(solution)/shard_map/ppermute | solution.py:51
  25.8 12.6 %collective-permute-start.3 = (bf16[528,256]{1,0:T(8,128)(2,1)S(1)}, bf16[528,256]{1,0:T(8,128)(2,1)S(1)}, u32[]{:S(2)}, u32[]{:S(2)}) collective-permute-start(bf16[528,256]{1,0:T(8,128)(2,1)S(1)} %get-tuple-element.61), channel_id=1, source_target_pairs={{0,192},{1,193},{2,194},{3,195},{4,196},{5,197},{6,198},{7,199},{8... | collective-permute-start | bytes 811016 | tf_op jit(solution)/shard_map/ppermute | solution.py:51
  28.9 10.2 %collective-permute-start.6 = (bf16[192,1024]{1,0:T(8,128)(2,1)}, bf16[192,1024]{1,0:T(8,128)(2,1)S(1)}, u32[]{:S(2)}, u32[]{:S(2)}) collective-permute-start(bf16[192,1024]{1,0:T(8,128)(2,1)} %slice.42), channel_id=1, source_target_pairs={{0,1},{1,2},{2,3},{3,0},{4,5},{5,6},{6,7},{7,4},{8,9},{9,10},{10,1... | collective-permute-start | bytes 1179656 | tf_op jit(solution)/shard_map/ppermute | solution.py:51
  29.7 9.4 %collective-permute-start.7 = (bf16[192,1024]{1,0:T(8,128)(2,1)}, bf16[192,1024]{1,0:T(8,128)(2,1)}, u32[]{:S(2)}, u32[]{:S(2)}) collective-permute-start(bf16[192,1024]{1,0:T(8,128)(2,1)} %slice.43), channel_id=1, source_target_pairs={{0,3},{1,0},{2,1},{3,2},{4,7},{5,4},{6,5},{7,6},{8,11},{9,8},{10,9... | collective-permute-start | bytes 1179656 | tf_op jit(solution)/shard_map/ppermute | solution.py:51
  38.4 3.8 %copy-start.8 = (bf16[64,2,256]{2,1,0:T(2,128)(2,1)S(1)}, bf16[64,2,256]{2,1,0:T(2,128)(2,1)}, u32[]{:S(2)}) copy-start(bf16[64,2,256]{2,1,0:T(2,128)(2,1)} %param.11) | copy-start | bytes 196612
  38.6 5.9 %copy-start.4 = (bf16[4,528,256]{2,1,0:T(8,128)(2,1)}, bf16[4,528,256]{2,1,0:T(8,128)(2,1)S(1)}, u32[]{:S(2)}) copy-start(bf16[4,528,256]{2,1,0:T(8,128)(2,1)S(1)} %pad_maximum_fusion.mine_ref) | copy-start | bytes 3244036
  39.1 5.4 %copy-start.7 = (bf16[192,1024]{1,0:T(8,128)(2,1)}, bf16[192,1024]{1,0:T(8,128)(2,1)S(1)}, u32[]{:S(2)}) copy-start(bf16[192,1024]{1,0:T(8,128)(2,1)S(1)} %collective-permute-done.6.refs_3_) | copy-start | bytes 1179652
  39.1 5.4 %collective-permute-start.8 = (bf16[4,528,256]{2,1,0:T(8,128)(2,1)S(1)}, bf16[4,528,256]{2,1,0:T(8,128)(2,1)}, u32[]{:S(2)}, u32[]{:S(2)}) collective-permute-start(bf16[4,528,256]{2,1,0:T(8,128)(2,1)S(1)} %pad_maximum_fusion.mine_ref), channel_id=1, source_target_pairs={{0,8},{1,9},{2,10},{3,11},{4,12},{5,13},{6,14},{7,15},{8,0},{9,1},... | collective-permute-start | bytes 3244040 | tf_op jit(solution)/shard_map/ppermute | solution.py:51
  43.2 15.7 %copy-start.3 = (s32[629]{0:T(1024)S(1)}, s32[629]{0:T(1024)}, u32[]{:S(2)}) copy-start(s32[629]{0:T(1024)} %concatenate.13.meta_ref) | copy-start | bytes 7552
  44.5 14.4 %copy-start = (bf16[512,16,256]{2,1,0:T(8,128)(2,1)S(1)}, bf16[512,16,256]{2,1,0:T(8,128)(2,1)}, u32[]{:S(2)}) copy-start(bf16[512,16,256]{2,1,0:T(8,128)(2,1)} %cache_ref.3) | copy-start | bytes 12582916
  50.7 16.4 %collective-permute-start.9 = (bf16[400,256]{1,0:T(8,128)(2,1)}, bf16[400,256]{1,0:T(8,128)(2,1)S(1)}, u32[]{:S(2)}, u32[]{:S(2)}) collective-permute-start(bf16[400,256]{1,0:T(8,128)(2,1)} %get-tuple-element.35), channel_id=1, source_target_pairs={{0,4},{1,5},{2,6},{3,7},{4,0},{5,1},{6,2},{7,3},{8,12},{9,13},{10,... | collective-permute-start | bytes 614408 | tf_op jit(solution)/shard_map/ppermute | solution.py:51
  57.9 9.2 %collective-permute-start.10 = (bf16[2,4,2,24]{3,2,1,0:T(2,128)(2,1)S(1)}, bf16[2,4,2,24]{3,2,1,0:T(2,128)(2,1)S(1)}, u32[]{:S(2)}, u32[]{:S(2)}) collective-permute-start(bf16[2,4,2,24]{3,2,1,0:T(2,128)(2,1)S(1)} %pad_maximum_fusion.6), channel_id=1, source_target_pairs={{0,16},{1,17},{2,18},{3,19},{4,20},{5,21},{6,22},{7,23},{8,24},{9,... | collective-permute-start | bytes 2312 | tf_op jit(solution)/shard_map/ppermute | solution.py:51
  64.8 8.7 %copy-start.1 = (f32[384,256]{1,0:T(8,128)S(1)}, f32[384,256]{1,0:T(8,128)}, u32[]{:S(2)}) copy-start(f32[384,256]{1,0:T(8,128)} %get-tuple-element.52.own_ref) | copy-start | bytes 1179652
  64.8 8.7 %copy-start.2 = (f32[384,128]{1,0:T(8,128)S(1)}, f32[384,128]{1,0:T(8,128)}, u32[]{:S(2)}) copy-start(f32[384,128]{1,0:T(8,128)} %get-tuple-element.53.sq_ref) | copy-start | bytes 589828
  67.0 13.8 %collective-permute-start.12 = (bf16[4,12,16,256]{3,2,1,0:T(8,128)(2,1)}, bf16[4,12,16,256]{3,2,1,0:T(8,128)(2,1)S(1)}, u32[]{:S(2)}, u32[]{:S(2)}) collective-permute-start(bf16[4,12,16,256]{3,2,1,0:T(8,128)(2,1)} %get-tuple-element.44), channel_id=1, source_target_pairs={{0,64},{1,65},{2,66},{3,67},{4,68},{5,69},{6,70},{7,71},{8,72},{9,... | collective-permute-start | bytes 1179656 | tf_op jit(solution)/shard_map/ppermute | solution.py:51
  68.6 21.8 %collective-permute-start.13 = (bf16[4,12,16,256]{3,2,1,0:T(8,128)(2,1)S(1)}, bf16[4,12,16,256]{3,2,1,0:T(8,128)(2,1)S(1)}, u32[]{:S(2)}, u32[]{:S(2)}) collective-permute-start(bf16[4,12,16,256]{3,2,1,0:T(8,128)(2,1)S(1)} %get-tuple-element.45), channel_id=1, source_target_pairs={{0,128},{1,129},{2,130},{3,131},{4,132},{5,133},{6,134},{7,135},{8... | collective-permute-start | bytes 1179656 | tf_op jit(solution)/shard_map/ppermute | solution.py:51
  71.0 19.3 %collective-permute-start.14 = (bf16[4,12,16,256]{3,2,1,0:T(8,128)(2,1)S(1)}, bf16[4,12,16,256]{3,2,1,0:T(8,128)(2,1)S(1)}, u32[]{:S(2)}, u32[]{:S(2)}) collective-permute-start(bf16[4,12,16,256]{3,2,1,0:T(8,128)(2,1)S(1)} %get-tuple-element.46), channel_id=1, source_target_pairs={{0,192},{1,193},{2,194},{3,195},{4,196},{5,197},{6,198},{7,199},{8... | collective-permute-start | bytes 1179656 | tf_op jit(solution)/shard_map/ppermute | solution.py:51
  72.2 8.4 %collective-permute-start.11 = (bf16[2,2,4,2,24]{4,3,2,1,0:T(2,128)(2,1)S(1)}, bf16[2,2,4,2,24]{4,3,2,1,0:T(2,128)(2,1)S(1)}, u32[]{:S(2)}, u32[]{:S(2)}) collective-permute-start(bf16[2,2,4,2,24]{4,3,2,1,0:T(2,128)(2,1)S(1)} %pad_maximum_fusion.5), channel_id=1, source_target_pairs={{0,32},{1,33},{2,34},{3,35},{4,36},{5,37},{6,38},{7,39},{8,40},{9,... | collective-permute-start | bytes 4616 | tf_op jit(solution)/shard_map/ppermute | solution.py:51
  75.1 22.3 %all-to-all-start.1 = ((bf16[32,32,256]{2,1,0:T(8,128)(2,1)}), bf16[32,32,256]{2,1,0:T(8,128)(2,1)S(1)}, u32[]{:S(2)}, u32[]{:S(2)}) async-start(bf16[32,32,256]{2,1,0:T(8,128)(2,1)} %bitcast.25), calls=%async_computation.1 | async-start | bytes 1048576 | tf_op jit(solution)/shard_map/all_to_all | solution.py:385
  91.4 5.9 %collective-permute-start.15 = (bf16[4,4,6,16,256]{4,3,2,1,0:T(8,128)(2,1)}, bf16[4,4,6,16,256]{4,3,2,1,0:T(8,128)(2,1)S(1)}, u32[]{:S(2)}, u32[]{:S(2)}) collective-permute-start(bf16[4,4,6,16,256]{4,3,2,1,0:T(8,128)(2,1)} %pad_maximum_fusion.1), channel_id=1, source_target_pairs={{0,8},{1,9},{2,10},{3,11},{4,12},{5,13},{6,14},{7,15},{8,0},{9,1},... | collective-permute-start | bytes 2359304 | tf_op jit(solution)/shard_map/ppermute | solution.py:51

commit v5 on v4

--- a/solution.py
+++ b/solution.py
@@ -484,7 +484,7 @@
     heard, _ = lax.optimization_barrier((heard, outgoing))
     heard_next = send(heard, zl_xor=1)
     by_x = [by_z[:, d] for d in range(NX)]
-    got, *by_x = lax.optimization_barrier((got, *by_x))
+    got, *by_x[1:] = lax.optimization_barrier((got, *by_x[1:]))
     by_x = [by_x[0]] + [send(by_x[d], dx=d) for d in range(1, NX)]
     got, turn, heard_next = lax.optimization_barrier((got, turn, heard_next))
     made = combine(features, row_count, meta, own, squares, got, turn, members)

time: 101 us -> 101 us (level)
  no operation moved by 1% of the time
where the time goes in v5:
time: 101 us; the launch traced here: 100 us
  starting transfers between devices  48.1 us (48%)
  Pallas kernels  19 us (19%)
  waiting for transfers between devices  18.9 us (19%)
  local copies, waits for them, and re-layouts  10.9 us (11%)
  other arithmetic  2.49 us (2%)
  between operations  1.07 us (1%)
    ppermute x16, starting transfers between devices, send(): return lax.ppermute(value, AXES, moves(**by))  38.1 us
    ppermute x16, waiting for transfers between devices, send(): return lax.ppermute(value, AXES, moves(**by))  16.5 us
    pallas_call x1, Pallas kernels, project(): pl.pallas_call(functools.partial(project_kernel, row_total), out_shape=(j...  6.14 us
    all_to_all x1, starting transfers between devices, exchange(): lax.all_to_all(pages.reshape(members, each * PAGE, lanes), 'inst', split_...  5.47 us
    pallas_call x1, Pallas kernels, attend(): pl.pallas_call(functools.partial(attend_kernel, start, row_total), out_sh...  5.12 us
    all_to_all x1, starting transfers between devices, per_device(): lax.all_to_all(packed, 'inst', split_axis=0, concat_axis=0, axis_index_gr...  4.48 us
    pallas_call x1, Pallas kernels, pack(): pl.pallas_call(functools.partial(pack_kernel, row_count), out_shape=jax.S...  3.21 us
    pallas_call x1, Pallas kernels, assemble(): pl.pallas_call(functools.partial(assemble_kernel, row_total), out_shape=j...  2.86 us
  transfers between devices with their start and end apart: 18, of which 6 were waited for; matrix products, arithmetic and copies ran while one was open for 13% of the time, Pallas kernels for 16%

profile of v5, /device:TPU:1, one launch (start us, length us, event | category | flops | bytes accessed | tf_op | source)
XLA Modules:
  0.0 100.4 jit_solution(12815150559779708440)
XLA Ops:
  0.6 2.2 %collective-permute-start.1 = (bf16[384,1024]{1,0:T(8,128)(2,1)}, bf16[384,1024]{1,0:T(8,128)(2,1)S(1)}, u32[]{:S(2)}, u32[]{:S(2)}) collective-permute-start(bf16[384,1024]{1,0:T(8,128)(2,1)} %bitcast.49), channel_id=1, source_target_pairs={{0,1},{1,2},{2,3},{3,0},{4,5},{5,6},{6,7},{7,4},{8,9},{9,10},{10,1... | collective-permute-start | bytes 2359304 | tf_op jit(solution)/shard_map/ppermute | solution.py:51
  2.8 1.5 %collective-permute-start.2 = (bf16[384,1024]{1,0:T(8,128)(2,1)}, bf16[384,1024]{1,0:T(8,128)(2,1)S(1)}, u32[]{:S(2)}, u32[]{:S(2)}) collective-permute-start(bf16[384,1024]{1,0:T(8,128)(2,1)} %bitcast.50), channel_id=1, source_target_pairs={{0,3},{1,0},{2,1},{3,2},{4,7},{5,4},{6,5},{7,6},{8,11},{9,8},{10,9... | collective-permute-start | bytes 2359304 | tf_op jit(solution)/shard_map/ppermute | solution.py:51
  4.4 1.0 constant_dynamic-slice_fusion
  5.3 6.1 %collective-permute-start = (bf16[512,256]{1,0:T(8,128)(2,1)S(1)}, bf16[512,256]{1,0:T(8,128)(2,1)S(1)}, u32[]{:S(2)}, u32[]{:S(2)}) collective-permute-start(bf16[512,256]{1,0:T(8,128)(2,1)S(1)} %constant_dynamic-slice_fusion), channel_id=1, source_target_pairs={{0,36},{1,37},{2,38},{3,39},{4,32},{5,33},{6,34},{7,35},{8,44},{9,... | collective-permute-start | bytes 786440 | tf_op jit(solution)/shard_map/ppermute | solution.py:51
  12.3 1.4 %concatenate.13.meta_ref = s32[629]{0:T(1024)} concatenate(s32[512]{0:T(512)S(1)} %reshape.135, s32[64]{0:T(128)} %param.14, s32[24]{0:T(128)} %param.15, s32[24]{0:T(128)} %param.16, s32[1]{0:T(128)} %bitcast, s32[1]{0:T(128)} %bitcast.1, s32[1]{0:T(128)} %bitcast.2, s32[1]{0:T(128)} %bitcast.3, s32[1]{0:T(128)} %bitcast.4), dimensions={0} | concatenate | bytes 5032 | tf_op jit(solution)/shard_map/concatenate | solution.py:65
  13.7 3.2 %pack.1 = bf16[4,4,12,16,256]{4,3,2,1,0:T(8,128)(2,1)} custom-call(s32[629]{0:T(1024)} %concatenate.13.meta_ref, bf16[512,16,256]{2,1,0:T(8,128)(2,1)} %cache_ref.3), custom_call_target="tpu_custom_call" | custom-call | bytes 4194304 | tf_op jit(solution)/shard_map/pack/pallas_call | solution.py:113
  16.9 4.5 %all-to-all-start = ((bf16[4,4,12,16,256]{4,3,2,1,0:T(8,128)(2,1)}), bf16[4,4,12,16,256]{4,3,2,1,0:T(8,128)(2,1)}, u32[]{:S(2)}, u32[]{:S(2)}) async-start(bf16[4,4,12,16,256]{4,3,2,1,0:T(8,128)(2,1)} %pack.1), calls=%async_computation | async-start | bytes 3145728 | tf_op jit(solution)/shard_map/all_to_all | solution.py:445
  21.7 0.9 collective-permute-done
  22.6 2.8 %collective-permute-start.4 = (bf16[528,256]{1,0:T(8,128)(2,1)S(1)}, bf16[528,256]{1,0:T(8,128)(2,1)S(1)}, u32[]{:S(2)}, u32[]{:S(2)}) collective-permute-start(bf16[528,256]{1,0:T(8,128)(2,1)S(1)} %get-tuple-element.59), channel_id=1, source_target_pairs={{0,128},{1,129},{2,130},{3,131},{4,132},{5,133},{6,134},{7,135},{8... | collective-permute-start | bytes 811016 | tf_op jit(solution)/shard_map/ppermute | solution.py:51
  25.8 2.4 %collective-permute-start.3 = (bf16[528,256]{1,0:T(8,128)(2,1)S(1)}, bf16[528,256]{1,0:T(8,128)(2,1)S(1)}, u32[]{:S(2)}, u32[]{:S(2)}) collective-permute-start(bf16[528,256]{1,0:T(8,128)(2,1)S(1)} %get-tuple-element.59), channel_id=1, source_target_pairs={{0,192},{1,193},{2,194},{3,195},{4,196},{5,197},{6,198},{7,199},{8... | collective-permute-start | bytes 811016 | tf_op jit(solution)/shard_map/ppermute | solution.py:51
  28.9 0.8 slice.43
  29.7 2.7 %collective-permute-start.7 = (bf16[192,1024]{1,0:T(8,128)(2,1)}, bf16[192,1024]{1,0:T(8,128)(2,1)}, u32[]{:S(2)}, u32[]{:S(2)}) collective-permute-start(bf16[192,1024]{1,0:T(8,128)(2,1)} %slice.43), channel_id=1, source_target_pairs={{0,3},{1,0},{2,1},{3,2},{4,7},{5,4},{6,5},{7,6},{8,11},{9,8},{10,9... | collective-permute-start | bytes 1179656 | tf_op jit(solution)/shard_map/ppermute | solution.py:51
  33.0 1.1 %reshape.136.q_ref = bf16[64,16,128]{2,1,0:T(8,128)(2,1)S(1)} reshape(bf16[64,2,1024]{2,1,0:T(2,128)(2,1)} %param.10) | data formatting | bytes 524288 | tf_op jit(solution)/shard_map/reshape | solution.py:476
  34.1 4.3 %collective-permute-done.5 = bf16[528,256]{1,0:T(8,128)(2,1)S(1)} collective-permute-done((bf16[528,256]{1,0:T(8,128)(2,1)S(1)}, bf16[528,256]{1,0:T(8,128)(2,1)S(1)}, u32[]{:S(2)}, u32[]{:S(2)}) %collective-permute-start.5) | collective-permute-done | bytes 270368 | tf_op jit(solution)/shard_map/ppermute | solution.py:51
  39.1 2.9 %collective-permute-start.8 = (bf16[4,528,256]{2,1,0:T(8,128)(2,1)S(1)}, bf16[4,528,256]{2,1,0:T(8,128)(2,1)}, u32[]{:S(2)}, u32[]{:S(2)}) collective-permute-start(bf16[4,528,256]{2,1,0:T(8,128)(2,1)S(1)} %pad_maximum_fusion.mine_ref), channel_id=1, source_target_pairs={{0,8},{1,9},{2,10},{3,11},{4,12},{5,13},{6,14},{7,15},{8,0},{9,1},... | collective-permute-start | bytes 3244040 | tf_op jit(solution)/shard_map/ppermute | solution.py:51
  43.2 1.3 %collective-permute-done.8.other_ref = bf16[4,528,256]{2,1,0:T(8,128)(2,1)} collective-permute-done((bf16[4,528,256]{2,1,0:T(8,128)(2,1)S(1)}, bf16[4,528,256]{2,1,0:T(8,128)(2,1)}, u32[]{:S(2)}, u32[]{:S(2)}) %collective-permute-start.8) | collective-permute-done | bytes 1081376 | tf_op jit(solution)/shard_map/ppermute | solution.py:51
  44.5 6.1 %project.1 = (f32[384,256]{1,0:T(8,128)}, bf16[400,256]{1,0:T(8,128)(2,1)}, f32[384,128]{1,0:T(8,128)}) custom-call(s32[629]{0:T(1024)} %concatenate.13.meta_ref, f32[8,1024]{1,0:T(8,128)} %reshape.145.gain_ref, bf16[8192,256]{1,0:T(8,128)(2,1)} %own_ref.1, bf16[4,528,256]{2,1,0:T(8,128)(2,1)} %copy-done.4, ...), custom_call_target="tpu_custom_call" | custom-call | flops 1610612736 | bytes 12582912 | tf_op jit(solution)/shard_map/project/pallas_call | solution.py:258
  50.7 6.5 %collective-permute-start.9 = (bf16[400,256]{1,0:T(8,128)(2,1)}, bf16[400,256]{1,0:T(8,128)(2,1)S(1)}, u32[]{:S(2)}, u32[]{:S(2)}) collective-permute-start(bf16[400,256]{1,0:T(8,128)(2,1)} %get-tuple-element.34), channel_id=1, source_target_pairs={{0,4},{1,5},{2,6},{3,7},{4,0},{5,1},{6,2},{7,3},{8,12},{9,13},{10,... | collective-permute-start | bytes 614408 | tf_op jit(solution)/shard_map/ppermute | solution.py:51
  57.9 1.0 %collective-permute-start.10 = (bf16[2,4,2,24]{3,2,1,0:T(2,128)(2,1)S(1)}, bf16[2,4,2,24]{3,2,1,0:T(2,128)(2,1)S(1)}, u32[]{:S(2)}, u32[]{:S(2)}) collective-permute-start(bf16[2,4,2,24]{3,2,1,0:T(2,128)(2,1)S(1)} %pad_maximum_fusion.6), channel_id=1, source_target_pairs={{0,16},{1,17},{2,18},{3,19},{4,20},{5,21},{6,22},{7,23},{8,24},{9,... | collective-permute-start | bytes 2312 | tf_op jit(solution)/shard_map/ppermute | solution.py:51
  58.9 5.1 %attend.1 = bf16[64,16,128]{2,1,0:T(8,128)(2,1)S(1)} custom-call(s32[629]{0:T(1024)S(1)} %copy-done.3, bf16[64,16,128]{2,1,0:T(8,128)(2,1)S(1)} %reshape.136.q_ref, bf16[64,16,256]{2,1,0:T(8,128)(2,1)S(1)} %pad.8.new_ref, bf16[512,16,256]{2,1,0:T(8,128)(2,1)S(1)} %copy-done), custom_call_target="tpu_custom_call" | custom-call | flops 75497472 | bytes 33554432 | tf_op jit(solution)/shard_map/attend/pallas_call | solution.py:172
  64.8 2.3 %slice_bitcast_fusion = (bf16[4,12,16,256]{3,2,1,0:T(8,128)(2,1)S(1)}, bf16[4,12,16,256]{3,2,1,0:T(8,128)(2,1)S(1)}, bf16[4,12,16,256]{3,2,1,0:T(8,128)(2,1)S(1)}, bf16[4,12,16,256]{3,2,1,0:T(8,128)(2,1)}) fusion(bf16[4,4,12,16,256]{4,3,2,1,0:T(8,128)(2,1)} %all-to-all-done), kind=kLoop, calls=%fused_computation.2 | loop fusion | bytes 3145728 | tf_op jit(solution)/shard_map/squeeze | solution.py:486
  67.0 1.6 %collective-permute-start.12 = (bf16[4,12,16,256]{3,2,1,0:T(8,128)(2,1)}, bf16[4,12,16,256]{3,2,1,0:T(8,128)(2,1)S(1)}, u32[]{:S(2)}, u32[]{:S(2)}) collective-permute-start(bf16[4,12,16,256]{3,2,1,0:T(8,128)(2,1)} %get-tuple-element.42), channel_id=1, source_target_pairs={{0,64},{1,65},{2,66},{3,67},{4,68},{5,69},{6,70},{7,71},{8,72},{9,... | collective-permute-start | bytes 1179656 | tf_op jit(solution)/shard_map/ppermute | solution.py:51
  68.6 2.4 %collective-permute-start.13 = (bf16[4,12,16,256]{3,2,1,0:T(8,128)(2,1)S(1)}, bf16[4,12,16,256]{3,2,1,0:T(8,128)(2,1)S(1)}, u32[]{:S(2)}, u32[]{:S(2)}) collective-permute-start(bf16[4,12,16,256]{3,2,1,0:T(8,128)(2,1)S(1)} %get-tuple-element.43), channel_id=1, source_target_pairs={{0,128},{1,129},{2,130},{3,131},{4,132},{5,133},{6,134},{7,135},{8... | collective-permute-start | bytes 1179656 | tf_op jit(solution)/shard_map/ppermute | solution.py:51
  71.0 1.2 %collective-permute-start.14 = (bf16[4,12,16,256]{3,2,1,0:T(8,128)(2,1)S(1)}, bf16[4,12,16,256]{3,2,1,0:T(8,128)(2,1)S(1)}, u32[]{:S(2)}, u32[]{:S(2)}) collective-permute-start(bf16[4,12,16,256]{3,2,1,0:T(8,128)(2,1)S(1)} %get-tuple-element.44), channel_id=1, source_target_pairs={{0,192},{1,193},{2,194},{3,195},{4,196},{5,197},{6,198},{7,199},{8... | collective-permute-start | bytes 1179656 | tf_op jit(solution)/shard_map/ppermute | solution.py:51
  72.2 1.2 %collective-permute-start.11 = (bf16[2,2,4,2,24]{4,3,2,1,0:T(2,128)(2,1)S(1)}, bf16[2,2,4,2,24]{4,3,2,1,0:T(2,128)(2,1)S(1)}, u32[]{:S(2)}, u32[]{:S(2)}) collective-permute-start(bf16[2,2,4,2,24]{4,3,2,1,0:T(2,128)(2,1)S(1)} %pad_maximum_fusion.5), channel_id=1, source_target_pairs={{0,32},{1,33},{2,34},{3,35},{4,36},{5,37},{6,38},{7,39},{8,40},{9,... | collective-permute-start | bytes 4616 | tf_op jit(solution)/shard_map/ppermute | solution.py:51
  73.5 1.6 %combine.1 = bf16[64,16,256]{2,1,0:T(8,128)(2,1)} custom-call(s32[629]{0:T(1024)S(1)} %copy-done.3, f32[384,256]{1,0:T(8,128)S(1)} %copy-done.1, f32[384,128]{1,0:T(8,128)S(1)} %copy-done.2, bf16[400,256]{1,0:T(8,128)(2,1)S(1)} %collective-permute-done.9.got_ref, f32[384,128]{1,0:T(8,128)S(1)} %pad_maximum_fusion.3.turn_ref), custom_call_target="tpu_custom_call" | custom-call | tf_op jit(solution)/shard_map/combine/pallas_call | solution.py:313
  75.1 5.5 %all-to-all-start.1 = ((bf16[32,32,256]{2,1,0:T(8,128)(2,1)}), bf16[32,32,256]{2,1,0:T(8,128)(2,1)S(1)}, u32[]{:S(2)}, u32[]{:S(2)}) async-start(bf16[32,32,256]{2,1,0:T(8,128)(2,1)} %bitcast.25), calls=%async_computation.1 | async-start | bytes 1048576 | tf_op jit(solution)/shard_map/all_to_all | solution.py:385
  80.9 9.5 %collective-permute-done.13.refs_2_ = bf16[4,12,16,256]{3,2,1,0:T(8,128)(2,1)S(1)} collective-permute-done((bf16[4,12,16,256]{3,2,1,0:T(8,128)(2,1)S(1)}, bf16[4,12,16,256]{3,2,1,0:T(8,128)(2,1)S(1)}, u32[]{:S(2)}, u32[]{:S(2)}) %collective-permute-start.13) | collective-permute-done | bytes 393248 | tf_op jit(solution)/shard_map/ppermute | solution.py:51
  90.5 1.0 pad_maximum_fusion.1
  91.4 3.3 %collective-permute-start.15 = (bf16[4,4,6,16,256]{4,3,2,1,0:T(8,128)(2,1)}, bf16[4,4,6,16,256]{4,3,2,1,0:T(8,128)(2,1)S(1)}, u32[]{:S(2)}, u32[]{:S(2)}) collective-permute-start(bf16[4,4,6,16,256]{4,3,2,1,0:T(8,128)(2,1)} %pad_maximum_fusion.1), channel_id=1, source_target_pairs={{0,8},{1,9},{2,10},{3,11},{4,12},{5,13},{6,14},{7,15},{8,0},{9,1},... | collective-permute-start | bytes 2359304 | tf_op jit(solution)/shard_map/ppermute | solution.py:51
  95.0 2.4 %all-to-all-done.1 = bf16[32,32,256]{2,1,0:T(8,128)(2,1)S(1)} async-done(((bf16[32,32,256]{2,1,0:T(8,128)(2,1)}), bf16[32,32,256]{2,1,0:T(8,128)(2,1)S(1)}, u32[]{:S(2)}, u32[]{:S(2)}) %all-to-all-start.1) | async-done | bytes 524320 | tf_op jit(solution)/shard_map/all_to_all | solution.py:385
  97.4 2.9 %assemble.1 = bf16[256,16,256]{2,1,0:T(8,128)(2,1)} custom-call(s32[629]{0:T(1024)S(1)} %copy-done.3, s32[64]{0:T(128)S(1)} %reshape.141.counts_ref, bf16[4,12,16,256]{3,2,1,0:T(8,128)(2,1)S(1)} %get-tuple-element.46.refs_0_, bf16[4,12,16,256]{3,2,1,0:T(8,128)(2,1)S(1)} %collective-permute-done.12.refs_1_, ...), custom_call_target="tpu_custom_call" | custom-call | tf_op jit(solution)/shard_map/assemble/pallas_call | solution.py:369
  (72 shorter events, 6.8 us)
Async XLA Ops:
  0.6 21.9 %collective-permute-start.1 = (bf16[384,1024]{1,0:T(8,128)(2,1)}, bf16[384,1024]{1,0:T(8,128)(2,1)S(1)}, u32[]{:S(2)}, u32[]{:S(2)}) collective-permute-start(bf16[384,1024]{1,0:T(8,128)(2,1)} %bitcast.49), channel_id=1, source_target_pairs={{0,1},{1,2},{2,3},{3,0},{4,5},{5,6},{6,7},{7,4},{8,9},{9,10},{10,1... | collective-permute-start | bytes 2359304 | tf_op jit(solution)/shard_map/ppermute | solution.py:51
  2.8 19.7 %collective-permute-start.2 = (bf16[384,1024]{1,0:T(8,128)(2,1)}, bf16[384,1024]{1,0:T(8,128)(2,1)S(1)}, u32[]{:S(2)}, u32[]{:S(2)}) collective-permute-start(bf16[384,1024]{1,0:T(8,128)(2,1)} %bitcast.50), channel_id=1, source_target_pairs={{0,3},{1,0},{2,1},{3,2},{4,7},{5,4},{6,5},{7,6},{8,11},{9,8},{10,9... | collective-permute-start | bytes 2359304 | tf_op jit(solution)/shard_map/ppermute | solution.py:51
  5.3 17.2 %collective-permute-start = (bf16[512,256]{1,0:T(8,128)(2,1)S(1)}, bf16[512,256]{1,0:T(8,128)(2,1)S(1)}, u32[]{:S(2)}, u32[]{:S(2)}) collective-permute-start(bf16[512,256]{1,0:T(8,128)(2,1)S(1)} %constant_dynamic-slice_fusion), channel_id=1, source_target_pairs={{0,36},{1,37},{2,38},{3,39},{4,32},{5,33},{6,34},{7,35},{8,44},{9,... | collective-permute-start | bytes 786440 | tf_op jit(solution)/shard_map/ppermute | solution.py:51
  16.9 4.5 %copy-start.10 = (s32[64]{0:T(128)S(1)}, s32[64]{0:T(128)}, u32[]{:S(2)}) copy-start(s32[64]{0:T(128)} %param.14) | copy-start | bytes 772
  16.9 4.5 %copy-start.11 = (s32[24]{0:T(128)S(1)}, s32[24]{0:T(128)}, u32[]{:S(2)}) copy-start(s32[24]{0:T(128)} %param.15) | copy-start | bytes 292
  16.9 4.7 %copy-start.12 = (s32[24]{0:T(128)S(1)}, s32[24]{0:T(128)}, u32[]{:S(2)}) copy-start(s32[24]{0:T(128)} %param.16) | copy-start | bytes 292
  16.9 47.8 %all-to-all-start = ((bf16[4,4,12,16,256]{4,3,2,1,0:T(8,128)(2,1)}), bf16[4,4,12,16,256]{4,3,2,1,0:T(8,128)(2,1)}, u32[]{:S(2)}, u32[]{:S(2)}) async-start(bf16[4,4,12,16,256]{4,3,2,1,0:T(8,128)(2,1)} %pack.1), calls=%async_computation | async-start | bytes 3145728 | tf_op jit(solution)/shard_map/all_to_all | solution.py:445
  21.7 10.7 %copy-start.9 = (bf16[8192]{0:T(1024)(128)(2,1)S(1)}, bf16[8192]{0:T(1024)(128)(2,1)}, u32[]{:S(2)}) copy-start(bf16[8192]{0:T(1024)(128)(2,1)} %param.18) | copy-start | bytes 49156
  22.6 7.1 %copy-start.5 = (bf16[384,1024]{1,0:T(8,128)(2,1)}, bf16[384,1024]{1,0:T(8,128)(2,1)S(1)}, u32[]{:S(2)}) copy-start(bf16[384,1024]{1,0:T(8,128)(2,1)S(1)} %collective-permute-done.1.refs_1_) | copy-start | bytes 2359300
  22.6 7.1 %copy-start.6 = (bf16[384,1024]{1,0:T(8,128)(2,1)}, bf16[384,1024]{1,0:T(8,128)(2,1)S(1)}, u32[]{:S(2)}) copy-start(bf16[384,1024]{1,0:T(8,128)(2,1)S(1)} %collective-permute-done.2.refs_2_) | copy-start | bytes 2359300
  22.6 11.5 %collective-permute-start.4 = (bf16[528,256]{1,0:T(8,128)(2,1)S(1)}, bf16[528,256]{1,0:T(8,128)(2,1)S(1)}, u32[]{:S(2)}, u32[]{:S(2)}) collective-permute-start(bf16[528,256]{1,0:T(8,128)(2,1)S(1)} %get-tuple-element.59), channel_id=1, source_target_pairs={{0,128},{1,129},{2,130},{3,131},{4,132},{5,133},{6,134},{7,135},{8... | collective-permute-start | bytes 811016 | tf_op jit(solution)/shard_map/ppermute | solution.py:51
  25.5 13.0 %collective-permute-start.5 = (bf16[528,256]{1,0:T(8,128)(2,1)S(1)}, bf16[528,256]{1,0:T(8,128)(2,1)S(1)}, u32[]{:S(2)}, u32[]{:S(2)}) collective-permute-start(bf16[528,256]{1,0:T(8,128)(2,1)S(1)} %get-tuple-element.59), channel_id=1, source_target_pairs={{0,64},{1,65},{2,66},{3,67},{4,68},{5,69},{6,70},{7,71},{8,72},{9,... | collective-permute-start | bytes 811016 | tf_op jit(solution)/shard_map/ppermute | solution.py:51
  25.8 12.6 %collective-permute-start.3 = (bf16[528,256]{1,0:T(8,128)(2,1)S(1)}, bf16[528,256]{1,0:T(8,128)(2,1)S(1)}, u32[]{:S(2)}, u32[]{:S(2)}) collective-permute-start(bf16[528,256]{1,0:T(8,128)(2,1)S(1)} %get-tuple-element.59), channel_id=1, source_target_pairs={{0,192},{1,193},{2,194},{3,195},{4,196},{5,197},{6,198},{7,199},{8... | collective-permute-start | bytes 811016 | tf_op jit(solution)/shard_map/ppermute | solution.py:51
  28.9 10.2 %collective-permute-start.6 = (bf16[192,1024]{1,0:T(8,128)(2,1)}, bf16[192,1024]{1,0:T(8,128)(2,1)S(1)}, u32[]{:S(2)}, u32[]{:S(2)}) collective-permute-start(bf16[192,1024]{1,0:T(8,128)(2,1)} %slice.42), channel_id=1, source_target_pairs={{0,1},{1,2},{2,3},{3,0},{4,5},{5,6},{6,7},{7,4},{8,9},{9,10},{10,1... | collective-permute-start | bytes 1179656 | tf_op jit(solution)/shard_map/ppermute | solution.py:51
  29.7 9.4 %collective-permute-start.7 = (bf16[192,1024]{1,0:T(8,128)(2,1)}, bf16[192,1024]{1,0:T(8,128)(2,1)}, u32[]{:S(2)}, u32[]{:S(2)}) collective-permute-start(bf16[192,1024]{1,0:T(8,128)(2,1)} %slice.43), channel_id=1, source_target_pairs={{0,3},{1,0},{2,1},{3,2},{4,7},{5,4},{6,5},{7,6},{8,11},{9,8},{10,9... | collective-permute-start | bytes 1179656 | tf_op jit(solution)/shard_map/ppermute | solution.py:51
  38.4 3.8 %copy-start.8 = (bf16[64,2,256]{2,1,0:T(2,128)(2,1)S(1)}, bf16[64,2,256]{2,1,0:T(2,128)(2,1)}, u32[]{:S(2)}) copy-start(bf16[64,2,256]{2,1,0:T(2,128)(2,1)} %param.11) | copy-start | bytes 196612
  38.6 5.9 %copy-start.4 = (bf16[4,528,256]{2,1,0:T(8,128)(2,1)}, bf16[4,528,256]{2,1,0:T(8,128)(2,1)S(1)}, u32[]{:S(2)}) copy-start(bf16[4,528,256]{2,1,0:T(8,128)(2,1)S(1)} %pad_maximum_fusion.mine_ref) | copy-start | bytes 3244036
  39.1 5.4 %copy-start.7 = (bf16[192,1024]{1,0:T(8,128)(2,1)}, bf16[192,1024]{1,0:T(8,128)(2,1)S(1)}, u32[]{:S(2)}) copy-start(bf16[192,1024]{1,0:T(8,128)(2,1)S(1)} %collective-permute-done.6.refs_3_) | copy-start | bytes 1179652
  39.1 5.4 %collective-permute-start.8 = (bf16[4,528,256]{2,1,0:T(8,128)(2,1)S(1)}, bf16[4,528,256]{2,1,0:T(8,128)(2,1)}, u32[]{:S(2)}, u32[]{:S(2)}) collective-permute-start(bf16[4,528,256]{2,1,0:T(8,128)(2,1)S(1)} %pad_maximum_fusion.mine_ref), channel_id=1, source_target_pairs={{0,8},{1,9},{2,10},{3,11},{4,12},{5,13},{6,14},{7,15},{8,0},{9,1},... | collective-permute-start | bytes 3244040 | tf_op jit(solution)/shard_map/ppermute | solution.py:51
  43.2 15.7 %copy-start.3 = (s32[629]{0:T(1024)S(1)}, s32[629]{0:T(1024)}, u32[]{:S(2)}) copy-start(s32[629]{0:T(1024)} %concatenate.13.meta_ref) | copy-start | bytes 7552
  44.5 14.4 %copy-start = (bf16[512,16,256]{2,1,0:T(8,128)(2,1)S(1)}, bf16[512,16,256]{2,1,0:T(8,128)(2,1)}, u32[]{:S(2)}) copy-start(bf16[512,16,256]{2,1,0:T(8,128)(2,1)} %cache_ref.3) | copy-start | bytes 12582916
  50.7 16.4 %collective-permute-start.9 = (bf16[400,256]{1,0:T(8,128)(2,1)}, bf16[400,256]{1,0:T(8,128)(2,1)S(1)}, u32[]{:S(2)}, u32[]{:S(2)}) collective-permute-start(bf16[400,256]{1,0:T(8,128)(2,1)} %get-tuple-element.34), channel_id=1, source_target_pairs={{0,4},{1,5},{2,6},{3,7},{4,0},{5,1},{6,2},{7,3},{8,12},{9,13},{10,... | collective-permute-start | bytes 614408 | tf_op jit(solution)/shard_map/ppermute | solution.py:51
  57.9 9.2 %collective-permute-start.10 = (bf16[2,4,2,24]{3,2,1,0:T(2,128)(2,1)S(1)}, bf16[2,4,2,24]{3,2,1,0:T(2,128)(2,1)S(1)}, u32[]{:S(2)}, u32[]{:S(2)}) collective-permute-start(bf16[2,4,2,24]{3,2,1,0:T(2,128)(2,1)S(1)} %pad_maximum_fusion.6), channel_id=1, source_target_pairs={{0,16},{1,17},{2,18},{3,19},{4,20},{5,21},{6,22},{7,23},{8,24},{9,... | collective-permute-start | bytes 2312 | tf_op jit(solution)/shard_map/ppermute | solution.py:51
  64.8 8.7 %copy-start.1 = (f32[384,256]{1,0:T(8,128)S(1)}, f32[384,256]{1,0:T(8,128)}, u32[]{:S(2)}) copy-start(f32[384,256]{1,0:T(8,128)} %get-tuple-element.50.own_ref) | copy-start | bytes 1179652
  64.8 8.7 %copy-start.2 = (f32[384,128]{1,0:T(8,128)S(1)}, f32[384,128]{1,0:T(8,128)}, u32[]{:S(2)}) copy-start(f32[384,128]{1,0:T(8,128)} %get-tuple-element.51.sq_ref) | copy-start | bytes 589828
  67.0 13.8 %collective-permute-start.12 = (bf16[4,12,16,256]{3,2,1,0:T(8,128)(2,1)}, bf16[4,12,16,256]{3,2,1,0:T(8,128)(2,1)S(1)}, u32[]{:S(2)}, u32[]{:S(2)}) collective-permute-start(bf16[4,12,16,256]{3,2,1,0:T(8,128)(2,1)} %get-tuple-element.42), channel_id=1, source_target_pairs={{0,64},{1,65},{2,66},{3,67},{4,68},{5,69},{6,70},{7,71},{8,72},{9,... | collective-permute-start | bytes 1179656 | tf_op jit(solution)/shard_map/ppermute | solution.py:51
  68.6 21.8 %collective-permute-start.13 = (bf16[4,12,16,256]{3,2,1,0:T(8,128)(2,1)S(1)}, bf16[4,12,16,256]{3,2,1,0:T(8,128)(2,1)S(1)}, u32[]{:S(2)}, u32[]{:S(2)}) collective-permute-start(bf16[4,12,16,256]{3,2,1,0:T(8,128)(2,1)S(1)} %get-tuple-element.43), channel_id=1, source_target_pairs={{0,128},{1,129},{2,130},{3,131},{4,132},{5,133},{6,134},{7,135},{8... | collective-permute-start | bytes 1179656 | tf_op jit(solution)/shard_map/ppermute | solution.py:51
  71.0 19.3 %collective-permute-start.14 = (bf16[4,12,16,256]{3,2,1,0:T(8,128)(2,1)S(1)}, bf16[4,12,16,256]{3,2,1,0:T(8,128)(2,1)S(1)}, u32[]{:S(2)}, u32[]{:S(2)}) collective-permute-start(bf16[4,12,16,256]{3,2,1,0:T(8,128)(2,1)S(1)} %get-tuple-element.44), channel_id=1, source_target_pairs={{0,192},{1,193},{2,194},{3,195},{4,196},{5,197},{6,198},{7,199},{8... | collective-permute-start | bytes 1179656 | tf_op jit(solution)/shard_map/ppermute | solution.py:51
  72.2 8.4 %collective-permute-start.11 = (bf16[2,2,4,2,24]{4,3,2,1,0:T(2,128)(2,1)S(1)}, bf16[2,2,4,2,24]{4,3,2,1,0:T(2,128)(2,1)S(1)}, u32[]{:S(2)}, u32[]{:S(2)}) collective-permute-start(bf16[2,2,4,2,24]{4,3,2,1,0:T(2,128)(2,1)S(1)} %pad_maximum_fusion.5), channel_id=1, source_target_pairs={{0,32},{1,33},{2,34},{3,35},{4,36},{5,37},{6,38},{7,39},{8,40},{9,... | collective-permute-start | bytes 4616 | tf_op jit(solution)/shard_map/ppermute | solution.py:51
  75.1 22.3 %all-to-all-start.1 = ((bf16[32,32,256]{2,1,0:T(8,128)(2,1)}), bf16[32,32,256]{2,1,0:T(8,128)(2,1)S(1)}, u32[]{:S(2)}, u32[]{:S(2)}) async-start(bf16[32,32,256]{2,1,0:T(8,128)(2,1)} %bitcast.25), calls=%async_computation.1 | async-start | bytes 1048576 | tf_op jit(solution)/shard_map/all_to_all | solution.py:385
  91.4 5.9 %collective-permute-start.15 = (bf16[4,4,6,16,256]{4,3,2,1,0:T(8,128)(2,1)}, bf16[4,4,6,16,256]{4,3,2,1,0:T(8,128)(2,1)S(1)}, u32[]{:S(2)}, u32[]{:S(2)}) collective-permute-start(bf16[4,4,6,16,256]{4,3,2,1,0:T(8,128)(2,1)} %pad_maximum_fusion.1), channel_id=1, source_target_pairs={{0,8},{1,9},{2,10},{3,11},{4,12},{5,13},{6,14},{7,15},{8,0},{9,1},... | collective-permute-start | bytes 2359304 | tf_op jit(solution)/shard_map/ppermute | solution.py:51
